TPU v7x, 32 devices: a whole 2x2x4 slice. The times are simulated.
32 devices in a mesh: dp: 4 (over y, x), seq: 8 (over z, core).
Axes of the slice: x: 2, y: 2, z: 4, core: 2. Of those that a mesh axis runs over, the one named last changes fastest.
Arguments:
- tokens: bfloat16 [8, 512, 2048], P('dp', 'seq'), may hold values from -6 to 6
- cotangent: bfloat16 [8, 512, 2048], P('dp', 'seq'), may hold values from -6 to 6
- prefix_len: int32 [8], P('dp'), may hold values from 0 to 511, as said below
- attn_gain: bfloat16 [2048], P(('dp', 'seq')), may hold values from 0.5 to 1.5
- w_query: bfloat16 [2048, 2048], P(('dp', 'seq')), may hold values from -0.125 to 0.125
- w_key: bfloat16 [2048, 512], P(('dp', 'seq')), may hold values from -0.125 to 0.125
- w_value: bfloat16 [2048, 512], P(('dp', 'seq')), may hold values from -0.125 to 0.125
- w_out: bfloat16 [2048, 2048], P(('dp', 'seq')), may hold values from -2 to 2
- mlp_gain: bfloat16 [2048], P(('dp', 'seq')), may hold values from 0.5 to 1.5
- w_gate: bfloat16 [2048, 8192], P(('dp', 'seq')), may hold values from -0.125 to 0.125
- w_up: bfloat16 [2048, 8192], P(('dp', 'seq')), may hold values from -0.125 to 0.125
- w_down: bfloat16 [8192, 2048], P(('dp', 'seq')), may hold values from -0.0625 to 0.0625
Outputs:
- block_out: bfloat16 [8, 512, 2048], P('dp', 'seq')
- input_grad: float32 [8, 512, 2048], P('dp', 'seq')
- attn_gain_grad: float32 [2048], P(('dp', 'seq'))
- w_query_grad: float32 [2048, 2048], P(('dp', 'seq'))
- w_key_grad: float32 [2048, 512], P(('dp', 'seq'))
- w_value_grad: float32 [2048, 512], P(('dp', 'seq'))
- w_out_grad: float32 [2048, 2048], P(('dp', 'seq'))
- mlp_gain_grad: float32 [2048], P(('dp', 'seq'))
- w_gate_grad: float32 [2048, 8192], P(('dp', 'seq'))
- w_up_grad: float32 [2048, 8192], P(('dp', 'seq'))
- w_down_grad: float32 [8192, 2048], P(('dp', 'seq'))
Inputs may be any that keep to these rules, and one draw needn't show every extreme that they name: A sequence's first prefix_len positions see one another both ways; some sequence has 0 and some has 511.
All inputs are finite; a program needn't handle non-finite values.
Results may differ from a plain program's by a relative error of at most 0.018.
Values may be sent and summed in bfloat16 or wider, within the bound.
A program may use at most 1.25 GiB of HBM per device.

v0:
```python
import math

import jax
import jax.numpy as jnp
from jax import lax
from jax.sharding import PartitionSpec as P

HEADS = 32
KV_HEADS = 8
HEAD_DIM = 64
KEY_BLOCK = 512


EPSILON = 1e-05
THETA = 500000.0
NEGATIVE = -1e30


def rope_table(positions, head_size):
    half_size = head_size // 2
    index_half = jnp.arange(half_size, dtype=jnp.float32)
    inverse = jnp.power(THETA, -2.0 * index_half / head_size)
    wavelength = 2.0 * math.pi / inverse
    smooth = (8192.0 / wavelength - 1.0) / 3.0
    blended = (1.0 - smooth) * inverse / 32.0 + smooth * inverse
    inverse = jnp.where(
        wavelength < 2048.0, inverse, jnp.where(wavelength > 8192.0, inverse / 32.0, blended)
    )
    angles = positions.astype(jnp.float32)[:, None] * inverse[None, :]
    cos_table = jnp.concatenate([jnp.cos(angles), jnp.cos(angles)], axis=1)
    sin_table = jnp.concatenate([jnp.sin(angles), jnp.sin(angles)], axis=1)
    return (cos_table, sin_table)


def rotate(values, cos_table, sin_table):
    rows_here = values.shape[0]
    head_size = cos_table.shape[1]
    half_size = head_size // 2
    split_heads = values.reshape(rows_here, -1, head_size)
    turned = jnp.concatenate(
        [-split_heads[:, :, half_size:], split_heads[:, :, :half_size]], axis=2
    )
    return (split_heads * cos_table[:, None, :] + turned * sin_table[:, None, :]).reshape(
        rows_here, -1
    )


def rotate_back(gradient, cos_table, sin_table):
    rows_here = gradient.shape[0]
    head_size = cos_table.shape[1]
    half_size = head_size // 2
    split_heads = gradient.reshape(rows_here, -1, head_size)
    sined = split_heads * sin_table[:, None, :]
    turned = jnp.concatenate([sined[:, :, half_size:], -sined[:, :, :half_size]], axis=2)
    return (split_heads * cos_table[:, None, :] + turned).reshape(rows_here, -1)


def rms_norm(values, gain_vec):
    scale_rows = lax.rsqrt(jnp.mean(values * values, axis=-1, keepdims=True) + EPSILON)
    return values * scale_rows * gain_vec


def swiglu(gate_in, up_in):
    return jax.nn.silu(gate_in) * up_in


def matmul(activation, weight):
    return jnp.dot(activation, weight, preferred_element_type=jnp.float32)


def inner_rows(activation, gradient):
    return lax.dot_general(
        activation, gradient, (((0,), (0,)), ((), ())), preferred_element_type=jnp.float32
    )


def times_transposed(gradient, weight):
    return lax.dot_general(
        gradient, weight, (((1,), (1,)), ((), ())), preferred_element_type=jnp.float32
    )


def split_query(values):
    rows_here = values.shape[0]
    groups = HEADS // KV_HEADS
    return (
        values.reshape(rows_here, KV_HEADS, groups, HEAD_DIM)
        .transpose(1, 2, 0, 3)
        .reshape(KV_HEADS, groups * rows_here, HEAD_DIM)
    )


def join_query(heads_in):
    groups = HEADS // KV_HEADS
    rows_here = heads_in.shape[1] // groups
    return (
        heads_in.reshape(KV_HEADS, groups, rows_here, HEAD_DIM)
        .transpose(2, 0, 1, 3)
        .reshape(rows_here, HEADS * HEAD_DIM)
    )


def split_keys(values):
    return values.reshape(values.shape[0], KV_HEADS, HEAD_DIM).transpose(1, 0, 2)


def join_keys(heads_in):
    return heads_in.transpose(1, 0, 2).reshape(heads_in.shape[1], KV_HEADS * HEAD_DIM)


def head_scores(query_group, key_group, query_pos, prefix_one, last_query):
    rows_here = query_group.shape[0]
    key_count = key_group.shape[0]
    block_count = key_count // KEY_BLOCK
    score_scale = 1.0 / math.sqrt(HEAD_DIM)

    def one_block(block_index):
        block_start = block_index * KEY_BLOCK
        key_block = lax.dynamic_slice_in_dim(key_group, block_start, KEY_BLOCK, 0)
        is_live = (block_start <= last_query) | (block_start < prefix_one)

        def compute():
            raw_scores = times_transposed(query_group, key_block) * score_scale
            key_pos = block_start + jnp.arange(KEY_BLOCK, dtype=jnp.int32)
            allowed = (key_pos[None, :] <= query_pos[:, None]) | (key_pos[None, :] < prefix_one)
            return jnp.where(allowed, raw_scores, NEGATIVE)

        def skipped():
            return jnp.full((rows_here, KEY_BLOCK), NEGATIVE, jnp.float32)

        return lax.cond(is_live, compute, skipped)

    blocks = lax.map(one_block, jnp.arange(block_count, dtype=jnp.int32))
    return blocks.transpose(1, 0, 2).reshape(rows_here, key_count)


def head_forward(operands, query_pos, prefix_one, last_query):
    query_group, key_group, value_group = operands
    scores = head_scores(query_group, key_group, query_pos, prefix_one, last_query)
    row_max = jnp.max(scores, axis=1, keepdims=True)
    expd_scores = jnp.exp(scores - row_max)
    row_total = jnp.sum(expd_scores, axis=1, keepdims=True)
    weights = (expd_scores / row_total).astype(jnp.bfloat16)
    return (matmul(weights, value_group), row_max, row_total)


def head_backward(operands, query_pos, prefix_one, last_query):
    query_group, key_group, value_group, grad_group, row_max, row_total = operands
    score_scale = 1.0 / math.sqrt(HEAD_DIM)
    scores = head_scores(query_group, key_group, query_pos, prefix_one, last_query)
    probs = jnp.exp(scores - row_max) / row_total
    probs_low = probs.astype(jnp.bfloat16)
    grad_probs = times_transposed(grad_group, value_group)
    delta_rows = jnp.sum(probs * grad_probs, axis=1, keepdims=True)
    grad_scores = (probs * (grad_probs - delta_rows)).astype(jnp.bfloat16)
    grad_query = matmul(grad_scores, key_group) * score_scale
    grad_key = inner_rows(grad_scores, query_group) * score_scale
    grad_value = inner_rows(probs_low, grad_group)
    return (grad_query, grad_key, grad_value)


def body(
    tokens,
    cotangent,
    prefix_len,
    attn_gain,
    w_query,
    w_key,
    w_value,
    w_out,
    mlp_gain,
    w_gate,
    w_up,
    w_down,
):
    micro_count = tokens.shape[0]
    span_rows = tokens.shape[1]
    width = tokens.shape[2]
    kv_width = w_key.shape[1]
    ff_width = w_gate.shape[1]
    shard_rows = attn_gain.shape[0]
    groups = HEADS // KV_HEADS
    seq_rank = lax.axis_index("seq")
    positions = seq_rank * span_rows + jnp.arange(span_rows, dtype=jnp.int32)
    cos_table, sin_table = rope_table(positions, HEAD_DIM)
    query_pos = jnp.tile(positions, groups)
    last_query = seq_rank * span_rows + span_rows - 1
    kept_sets = []
    outputs = []
    input_grads = []
    attn_gain_total = jnp.zeros((width,), jnp.float32)
    mlp_gain_total = jnp.zeros((width,), jnp.float32)
    attn_once = (
        lax.all_gather(attn_gain, ("dp", "seq"), axis=0, tiled=True),
        lax.all_gather(w_query, ("dp", "seq"), axis=0, tiled=True),
        lax.all_gather(w_key, ("dp", "seq"), axis=0, tiled=True),
        lax.all_gather(w_value, ("dp", "seq"), axis=0, tiled=True),
        lax.all_gather(w_out, ("dp", "seq"), axis=0, tiled=True),
    )
    mlp_once = (
        lax.all_gather(mlp_gain, ("dp", "seq"), axis=0, tiled=True),
        lax.all_gather(w_gate, ("dp", "seq"), axis=0, tiled=True),
        lax.all_gather(w_up, ("dp", "seq"), axis=0, tiled=True),
        lax.all_gather(w_down, ("dp", "seq"), axis=0, tiled=True),
    )
    for micro_index in range(micro_count):
        token_rows = tokens[micro_index].astype(jnp.float32)
        prefix_one = prefix_len[micro_index]
        gain_attn = attn_once[0].astype(jnp.float32)
        normed = rms_norm(token_rows, gain_attn).astype(jnp.bfloat16)
        query_rot = rotate(matmul(normed, attn_once[1]), cos_table, sin_table).astype(jnp.bfloat16)
        key_rot = rotate(matmul(normed, attn_once[2]), cos_table, sin_table).astype(jnp.bfloat16)
        value_low = matmul(normed, attn_once[3]).astype(jnp.bfloat16)
        key_all, value_all = (
            lax.all_gather(key_rot, "seq", axis=0, tiled=True),
            lax.all_gather(value_low, "seq", axis=0, tiled=True),
        )
        query_heads = split_query(query_rot)
        key_heads = split_keys(key_all)
        value_heads = split_keys(value_all)

        def forward_head(operands):
            return head_forward(operands, query_pos, prefix_one, last_query)

        head_out, row_max, row_total = lax.map(forward_head, (query_heads, key_heads, value_heads))
        attn_mixed = join_query(head_out).astype(jnp.bfloat16)
        hidden_state = token_rows + matmul(attn_mixed, attn_once[4])
        gain_mlp = mlp_once[0].astype(jnp.float32)
        normed_mlp = rms_norm(hidden_state, gain_mlp).astype(jnp.bfloat16)
        gate_proj = matmul(normed_mlp, mlp_once[1])
        up_proj = matmul(normed_mlp, mlp_once[2])
        activated = swiglu(gate_proj, up_proj).astype(jnp.bfloat16)
        block_value = hidden_state + matmul(activated, mlp_once[3])
        outputs.append(block_value.astype(jnp.bfloat16))
        grad_out = cotangent[micro_index]
        grad_activated = times_transposed(grad_out, mlp_once[3])
        mlp_pull = jax.vjp(swiglu, gate_proj, up_proj)[1]
        grad_gate, grad_up = mlp_pull(grad_activated)
        grad_gate_low = grad_gate.astype(jnp.bfloat16)
        grad_up_low = grad_up.astype(jnp.bfloat16)
        grad_normed_mlp = times_transposed(grad_gate_low, mlp_once[1]) + times_transposed(
            grad_up_low, mlp_once[2]
        )
        mlp_norm_pull = jax.vjp(rms_norm, hidden_state, gain_mlp)[1]
        grad_hidden_part, grad_mlp_gain = mlp_norm_pull(grad_normed_mlp)
        grad_hidden = grad_out.astype(jnp.float32) + grad_hidden_part
        grad_branch = grad_hidden.astype(jnp.bfloat16)
        grad_mixed = times_transposed(grad_branch, attn_once[4]).astype(jnp.bfloat16)
        grad_heads = split_query(grad_mixed)

        def backward_head(operands):
            return head_backward(operands, query_pos, prefix_one, last_query)

        grad_query_heads, grad_key_heads, grad_value_heads = lax.map(
            backward_head, (query_heads, key_heads, value_heads, grad_heads, row_max, row_total)
        )
        grad_query_rot = join_query(grad_query_heads)
        grad_key_mine, grad_value_mine = (
            lax.psum_scatter(
                join_keys(grad_key_heads).astype(jnp.bfloat16),
                "seq",
                scatter_dimension=0,
                tiled=True,
            ).astype(jnp.float32),
            lax.psum_scatter(
                join_keys(grad_value_heads).astype(jnp.bfloat16),
                "seq",
                scatter_dimension=0,
                tiled=True,
            ).astype(jnp.float32),
        )
        grad_query_low = rotate_back(grad_query_rot, cos_table, sin_table).astype(jnp.bfloat16)
        grad_key_low = rotate_back(grad_key_mine, cos_table, sin_table).astype(jnp.bfloat16)
        grad_value_low = grad_value_mine.astype(jnp.bfloat16)
        grad_normed = (
            times_transposed(grad_query_low, attn_once[1])
            + times_transposed(grad_key_low, attn_once[2])
            + times_transposed(grad_value_low, attn_once[3])
        )
        attn_norm_pull = jax.vjp(rms_norm, token_rows, attn_once[0].astype(jnp.float32))[1]
        grad_tokens_part, grad_attn_gain = attn_norm_pull(grad_normed)
        input_grads.append(grad_hidden + grad_tokens_part)
        attn_gain_total = attn_gain_total + grad_attn_gain
        mlp_gain_total = mlp_gain_total + grad_mlp_gain
        kept_sets.append(
            (
                normed,
                grad_query_low,
                grad_key_low,
                grad_value_low,
                attn_mixed,
                grad_branch,
                normed_mlp,
                grad_gate_low,
                grad_up_low,
                activated,
                grad_out,
            )
        )
    ratio = ff_width // width

    def one_term(entry, row_count):
        (
            normed_all,
            grad_query_all,
            grad_key_all,
            grad_value_all,
            mixed_all,
            branch_all,
            mlp_in_all,
            gate_all,
            up_all,
            act_all,
            out_all,
        ) = entry
        down_part = inner_rows(act_all, out_all).reshape(row_count, ratio * width)
        return jnp.concatenate(
            [
                inner_rows(normed_all, grad_query_all),
                inner_rows(normed_all, grad_key_all),
                inner_rows(normed_all, grad_value_all),
                inner_rows(mixed_all, branch_all),
                inner_rows(mlp_in_all, gate_all),
                inner_rows(mlp_in_all, up_all),
                down_part,
            ],
            axis=1,
        )

    summed = one_term(kept_sets[0], shard_rows * lax.axis_size(("dp", "seq")))
    for entry in kept_sets[1:]:
        summed = summed + one_term(entry, shard_rows * lax.axis_size(("dp", "seq")))
    grad_block = lax.psum_scatter(summed, ("dp", "seq"), scatter_dimension=0, tiled=True)
    attn_gain_grad, mlp_gain_grad = (
        lax.psum_scatter(attn_gain_total, ("dp", "seq"), scatter_dimension=0, tiled=True),
        lax.psum_scatter(mlp_gain_total, ("dp", "seq"), scatter_dimension=0, tiled=True),
    )
    offset_value = width + kv_width
    offset_out = offset_value + kv_width
    offset_gate = offset_out + width
    offset_up = offset_gate + ff_width
    offset_down = offset_up + ff_width
    w_query_grad = grad_block[:, :width]
    w_key_grad = grad_block[:, width:offset_value]
    w_value_grad = grad_block[:, offset_value:offset_out]
    w_out_grad = grad_block[:, offset_out:offset_gate]
    w_gate_grad = grad_block[:, offset_gate:offset_up]
    w_up_grad = grad_block[:, offset_up:offset_down]
    w_down_grad = grad_block[:, offset_down:].reshape(-1, width)
    return (
        jnp.stack(outputs),
        jnp.stack(input_grads),
        attn_gain_grad,
        w_query_grad,
        w_key_grad,
        w_value_grad,
        w_out_grad,
        mlp_gain_grad,
        w_gate_grad,
        w_up_grad,
        w_down_grad,
    )


def solution(mesh):
    in_specs = (
        P("dp", "seq", None),
        P("dp", "seq", None),
        P("dp"),
        P(("dp", "seq")),
        P(("dp", "seq"), None),
        P(("dp", "seq"), None),
        P(("dp", "seq"), None),
        P(("dp", "seq"), None),
        P(("dp", "seq")),
        P(("dp", "seq"), None),
        P(("dp", "seq"), None),
        P(("dp", "seq"), None),
    )
    out_specs = (
        P("dp", "seq", None),
        P("dp", "seq", None),
        P(("dp", "seq")),
        P(("dp", "seq"), None),
        P(("dp", "seq"), None),
        P(("dp", "seq"), None),
        P(("dp", "seq"), None),
        P(("dp", "seq")),
        P(("dp", "seq"), None),
        P(("dp", "seq"), None),
        P(("dp", "seq"), None),
    )
    return jax.shard_map(body, mesh=mesh, in_specs=in_specs, out_specs=out_specs, check_vma=False)
```

profile of v0, /device:TPU:0, one launch (start us, length us, event | category | flops | bytes accessed | tf_op | source)
XLA Modules:
  0.0 4422.2 jit_solution(16325040435642457158)
XLA Ops:
  16.5 42.2 all-reduce.5
  61.4 8.9 all-gather.10.cloned.1.call-done
  75.1 14.9 all_gather.50
  91.5 37.3 all-gather.12.cloned.1.call-done
  131.1 16.6 all_gather.51
  152.1 17.6 all_gather.42
  174.7 16.8 all_gather.44
  193.1 15.9 all-gather.8.cloned.1.call-done
  209.0 12.5 copy.73
  221.5 6.0 fusion.142
  231.8 44.0 while.85
  231.8 3.4 conditional.13
  237.4 3.3 conditional.13
  242.9 3.3 conditional.13
  248.3 3.3 conditional.13
  253.8 3.3 conditional.13
  259.4 3.3 conditional.13
  264.9 3.3 conditional.13
  270.4 3.3 conditional.13
  277.5 43.5 while.84
  277.6 3.3 conditional.12
  283.0 3.3 conditional.12
  299.3 3.3 conditional.12
  322.4 5.2 multiply_reduce_fusion.7
  330.1 155.0 %all-gather.16.cloned.1.call-done = bf16[2048,8192]{1,0:T(8,128)(2,1)} async-done(((bf16[64,8192]{1,0:T(8,128)(2,1)}), bf16[2048,8192]{1,0:T(8,128)(2,1)}) %all-gather.16.cloned.1.call-update) | async-done | bytes 33554448 | tf_op jit(solution)/shard_map/all_gather | solution.py:202
  485.1 16.1 fusion.186
  501.2 179.8 %all-gather.18.cloned.1.call-done = bf16[2048,8192]{1,0:T(8,128)(2,1)} async-done(((bf16[64,8192]{1,0:T(8,128)(2,1)}), bf16[2048,8192]{1,0:T(8,128)(2,1)}) %all-gather.18.cloned.1.call-update) | async-done | bytes 33554448 | tf_op jit(solution)/shard_map/all_gather | solution.py:203
  681.0 15.6 fusion.187
  696.6 180.4 %all-gather.20.cloned.1.call-done = bf16[8192,2048]{1,0:T(8,128)(2,1)} async-done(((bf16[256,2048]{1,0:T(8,128)(2,1)}), bf16[8192,2048]{1,0:T(8,128)(2,1)}) %all-gather.20.cloned.1.call-update) | async-done | bytes 33554448 | tf_op jit(solution)/shard_map/all_gather | solution.py:204
  877.0 17.3 multiply_convert_fusion.3
  894.3 15.6 fusion.190
  909.9 17.0 multiply_reduce_fusion.3
  927.0 15.1 fusion.188
  942.0 14.9 fusion.189
  956.9 17.7 multiply_convert_fusion.2
  974.6 15.3 fusion.192
  989.9 16.5 multiply_reduce_fusion.2
  1006.8 6.4 convolution_convert_fusion.1
  1017.3 75.8 %while.86 = (s32[]{:T(128)}, f32[8,256,64]{1,2,0:T(8,128)}, bf16[8,512,64]{1,2,0:T(8,128)(2,1)}, bf16[8,512,64]{1,2,0:T(8,128)(2,1)}, pred[]{:T(512)}, /*index=5...) while((s32[]{:T(128)}, f32[8,256,64]{1,2,0:T(8,128)}, ...), condition=%wide.region_21.22_spmd.clone, body=%wide.region_17.21_spmd.clone.sunk | while | flops 86032640 | bytes 5035466 | solution.py:254
  1093.1 6.0 convolution_convert_fusion
  1102.4 76.4 %while.87 = (s32[]{:T(128)}, f32[8,256,64]{1,2,0:T(8,128)S(1)}, bf16[8,512,64]{1,2,0:T(8,128)(2,1)}, bf16[8,512,64]{1,2,0:T(8,128)(2,1)}, pred[]{:T(512)}, /*ind...) while((s32[]{:T(128)}, f32[8,256,64]{1,2,0:T(8,128)S(1)}, ...), condition=%wide.region_30.31_spmd.clone, body=%wide.region_26.30_spmd.clone.sunk | while | flops 86032640 | bytes 5035466 | solution.py:254
  1181.0 23.3 fusion.136
  1206.5 23.7 fusion.132
  1238.1 79.4 %reshape.444 = f32[2048,8192]{1,0:T(8,128)} reshape(f32[8192,2048]{1,0:T(8,128)} %fusion.136) | data formatting | bytes 134217728 | tf_op jit(solution)/shard_map/reshape | solution.py:316
  1317.5 79.4 %reshape.445 = f32[2048,8192]{1,0:T(8,128)} reshape(f32[8192,2048]{1,0:T(8,128)} %fusion.132) | data formatting | bytes 134217728 | tf_op jit(solution)/shard_map/reshape | solution.py:316
  1402.5 8.3 convolution_dynamic-update-slice_fusion.7
  1410.7 8.4 convolution_dynamic-update-slice_fusion.5
  1424.5 4.0 reduce-scatter.18.cloned.1.call-done
  1428.5 3.7 convolution_dynamic-update-slice_fusion.10
  1432.3 8.2 convolution_dynamic-update-slice_fusion.6
  1440.4 23.5 convolution_dynamic-update-slice_fusion.3
  1463.9 23.2 convolution_dynamic-update-slice_fusion.2
  1490.1 3.7 convolution_dynamic-update-slice_fusion.8
  1493.9 8.3 convolution_dynamic-update-slice_fusion.4
  1502.2 23.4 convolution_dynamic-update-slice_fusion.1
  1525.6 23.2 convolution_dynamic-update-slice_fusion
  1548.8 44.3 %constant_dynamic-update-slice_fusion.4 = f32[2048,29696]{1,0:T(8,128)} fusion(f32[2048,29696]{1,0:T(8,128)} %convolution_dynamic-update-slice_fusion.2, f32[2048,8192]{1,0:T(8,128)} %reshape.444), kind=kLoop, calls=%fused_computation.276 | loop fusion | bytes 134217728 | tf_op jit(solution)/shard_map/concatenate | solution.py:317
  1593.1 44.5 %constant_dynamic-update-slice_fusion.5 = f32[2048,29696]{1,0:T(8,128)} fusion(f32[2048,29696]{1,0:T(8,128)} %convolution_dynamic-update-slice_fusion, f32[2048,8192]{1,0:T(8,128)} %reshape.445), kind=kLoop, calls=%fused_computation.277 | loop fusion | bytes 134217728 | tf_op jit(solution)/shard_map/concatenate | solution.py:317
  1637.6 228.6 %add.335 = f32[2048,29696]{1,0:T(8,128)} add(f32[2048,29696]{1,0:T(8,128)} %constant_dynamic-update-slice_fusion.4, f32[2048,29696]{1,0:T(8,128)} %constant_dynamic-update-slice_fusion.5) | non-fusion elementwise | flops 60817408 | bytes 729808896 | tf_op jit(solution)/shard_map/add | solution.py:332
  1870.5 17.5 fusion.72
  1888.1 15.1 fusion.73
  1913.9 40.4 all-reduce.4
  1956.9 2447.1 %reduce-scatter.14.cloned.1.call-done = f32[64,29696]{1,0:T(8,128)} async-done(((f32[2048,29696]{1,0:T(8,128)}), f32[64,29696]{1,0:T(8,128)}) %reduce-scatter.14.cloned.1.call-update) | async-done | bytes 7602192 | tf_op jit(solution)/shard_map/reduce_scatter | solution.py:333
  4404.0 5.4 fusion.177
  (631 shorter events, 366.5 us)
Async XLA Ops:
  7.2 66.1 %copy-start.2 = (bf16[2,64,2048]{2,1,0:T(8,128)(2,1)S(1)}, bf16[2,64,2048]{2,1,0:T(8,128)(2,1)}, u32[]{:S(2)}) copy-start(bf16[2,64,2048]{2,1,0:T(8,128)(2,1)} %param.28) | copy-start | bytes 1572868
  7.2 63.1 %all-gather.10.cloned.1.call-start = ((), (), s32[]{:S(2)}) async-start(), calls=%async_computation.6 | async-start | bytes 2162688 | tf_op jit(solution)/shard_map/all_gather | solution.py:196
  7.9 120.9 %all-gather.12.cloned.1.call-start = ((), (), s32[]{:S(2)}) async-start(), calls=%async_computation.7 | async-start | bytes 2162688 | tf_op jit(solution)/shard_map/all_gather | solution.py:197
  8.7 200.3 %all-gather.8.cloned.1.call-start = ((), (), s32[]{:S(2)}) async-start(), calls=%async_computation.5 | async-start | bytes 8650752 | tf_op jit(solution)/shard_map/all_gather | solution.py:195
  9.4 313.0 %all-gather.14.cloned.1.call-start = ((), (), s32[]{:S(2)}) async-start(), calls=%async_computation.8 | async-start | bytes 8650752 | tf_op jit(solution)/shard_map/all_gather | solution.py:198
  10.0 475.1 %all-gather.16.cloned.1.call-start = ((), (), s32[]{:S(2)}) async-start(), calls=%async_computation.9 | async-start | bytes 34603008 | tf_op jit(solution)/shard_map/all_gather | solution.py:202
  10.6 670.4 %all-gather.18.cloned.1.call-start = ((), (), s32[]{:S(2)}) async-start(), calls=%async_computation.10 | async-start | bytes 34603008 | tf_op jit(solution)/shard_map/all_gather | solution.py:203
  11.1 865.8 %all-gather.20.cloned.1.call-start = ((), (), s32[]{:S(2)}) async-start(), calls=%async_computation.11 | async-start | bytes 34603008 | tf_op jit(solution)/shard_map/all_gather | solution.py:204
  11.9 1407.4 %reduce-scatter.16.cloned.1.call-start = ((), (), s32[]{:S(2)}) async-start(), calls=%async_computation.13 | async-start | bytes 589824
  58.7 168.8 %copy-start.43 = (f32[2048]{0:T(1024)}, f32[2048]{0:T(1024)S(1)}, u32[]{:S(2)}) copy-start(f32[2048]{0:T(1024)S(1)} %convert_element_type.312) | copy-start | bytes 24580
  59.6 170.7 %copy-start.57 = (f32[64,64]{0,1:T(8,128)}, f32[64,64]{0,1:T(8,128)S(1)}, u32[]{:S(2)}) copy-start(f32[64,64]{0,1:T(8,128)S(1)} %pad_maximum_fusion.7) | copy-start | bytes 49156
  59.6 170.7 %copy-start.53 = (f32[64,64]{0,1:T(8,128)}, f32[64,64]{0,1:T(8,128)S(1)}, u32[]{:S(2)}) copy-start(f32[64,64]{0,1:T(8,128)S(1)} %pad_maximum_fusion.6) | copy-start | bytes 49156
  60.9 70.2 %copy-start.73 = (f32[64]{0:T(128)}, f32[64]{0:T(128)S(1)}, u32[]{:S(2)}) copy-start(f32[64]{0:T(128)S(1)} %get-tuple-element.1141) | copy-start | bytes 772
  61.4 160.1 %copy-start.61 = (f32[64]{0:T(128)}, f32[64]{0:T(128)S(1)}, u32[]{:S(2)}) copy-start(f32[64]{0:T(128)S(1)} %fusion.160) | copy-start | bytes 772
  61.4 166.1 %copy-start.64 = (f32[64]{0:T(128)}, f32[64]{0:T(128)S(1)}, u32[]{:S(2)}) copy-start(f32[64]{0:T(128)S(1)} %fusion.158) | copy-start | bytes 772
  128.8 45.4 %copy-start.5 = (bf16[2048,512]{1,0:T(8,128)(2,1)S(1)}, bf16[2048,512]{1,0:T(8,128)(2,1)}, u32[]{:S(2)}) copy-start(bf16[2048,512]{1,0:T(8,128)(2,1)} %all-gather.12.cloned.1.call-done) | copy-start | bytes 6291460
  221.5 6.0 copy-start.1
  231.8 45.7 %copy-start.56 = (bf16[8,256,64]{1,2,0:T(8,128)(2,1)S(1)}, bf16[8,256,64]{1,2,0:T(8,128)(2,1)}, u32[]{:S(2)}) copy-start(bf16[8,256,64]{1,2,0:T(8,128)(2,1)} %copy.164) | copy-start | bytes 786436
  277.2 50.4 %copy-start.38 = (bf16[64,2048]{1,0:T(8,128)(2,1)}, bf16[64,2048]{1,0:T(8,128)(2,1)S(1)}, u32[]{:S(2)}) copy-start(bf16[64,2048]{1,0:T(8,128)(2,1)S(1)} %convert_element_type.344) | copy-start | bytes 786436
  322.4 5.8 copy-start
  327.6 678.8 %copy-start.14 = (f32[64,2048]{1,0:T(8,128)}, f32[64,2048]{1,0:T(8,128)S(1)}, u32[]{:S(2)}) copy-start(f32[64,2048]{1,0:T(8,128)S(1)} %get-tuple-element.1314) | copy-start | bytes 1572868
  329.9 676.5 %copy-start.12 = (f32[64,2048]{1,0:T(8,128)}, f32[64,2048]{1,0:T(8,128)S(1)}, u32[]{:S(2)}) copy-start(f32[64,2048]{1,0:T(8,128)S(1)} %get-tuple-element.1316) | copy-start | bytes 1572868
  330.1 350.9 %copy-start.33 = (bf16[64,2048]{1,0:T(8,128)(2,1)}, bf16[64,2048]{1,0:T(8,128)(2,1)S(1)}, u32[]{:S(2)}) copy-start(bf16[64,2048]{1,0:T(8,128)(2,1)S(1)} %multiply_convert_fusion.7) | copy-start | bytes 786436
  501.2 375.8 %copy-start.35 = (bf16[2,64,2048]{2,1,0:T(8,128)(2,1)S(1)}, bf16[2,64,2048]{2,1,0:T(8,128)(2,1)}, u32[]{:S(2)}) copy-start(bf16[2,64,2048]{2,1,0:T(8,128)(2,1)} %param.29) | copy-start | bytes 1572868
  894.3 286.7 %copy-start.16 = (bf16[64,8192]{1,0:T(8,128)(2,1)}, bf16[64,8192]{1,0:T(8,128)(2,1)S(1)}, u32[]{:S(2)}) copy-start(bf16[64,8192]{1,0:T(8,128)(2,1)S(1)} %get-tuple-element.1264) | copy-start | bytes 3145732
  894.3 15.6 copy-start.21
  926.9 15.1 copy-start.31
  974.6 15.3 copy-start.19
  989.9 16.6 copy-start.36
  989.9 16.6 copy-start.46
  1006.8 10.5 copy-start.25
  1006.8 86.3 %copy-start.28 = (f32[64,2048]{1,0:T(8,128)}, f32[64,2048]{1,0:T(8,128)S(1)}, u32[]{:S(2)}) copy-start(f32[64,2048]{1,0:T(8,128)S(1)} %get-tuple-element.1283) | copy-start | bytes 1572868
  1102.4 78.6 %copy-start.37 = (bf16[2,64,2048]{2,1,0:T(8,128)(2,1)S(1)}, bf16[2,64,2048]{2,1,0:T(8,128)(2,1)}, u32[]{:S(2)}) copy-start(bf16[2,64,2048]{2,1,0:T(8,128)(2,1)} %param.29) | copy-start | bytes 1572868
  1180.9 239.4 %reduce-scatter.20.cloned.1.call-start = ((), (), s32[]{:S(2)}) async-start(), calls=%async_computation.15 | async-start | bytes 589824
  1181.0 25.5 copy-start.18
  1206.4 222.1 %reduce-scatter.18.cloned.1.call-start = ((), (), s32[]{:S(2)}) async-start(), calls=%async_computation.14 | async-start | bytes 589824
  1230.2 6.9 copy-start.48
  1231.9 167.3 %copy-start.8 = (f32[8,4,64,64]{2,3,1,0:T(8,128)}, f32[8,4,64,64]{2,3,1,0:T(8,128)S(1)}, u32[]{:S(2)}) copy-start(f32[8,4,64,64]{2,3,1,0:T(8,128)S(1)} %copy.92) | copy-start | bytes 1572868
  1234.7 164.5 %copy-start.10 = (f32[8,4,64,64]{2,3,1,0:T(8,128)}, f32[8,4,64,64]{2,3,1,0:T(8,128)S(1)}, u32[]{:S(2)}) copy-start(f32[8,4,64,64]{2,3,1,0:T(8,128)S(1)} %copy.96) | copy-start | bytes 1572868
  1317.5 79.4 %copy-start.58 = (f32[64,64]{0,1:T(8,128)S(1)}, f32[64,64]{0,1:T(8,128)}, u32[]{:S(2)}) copy-start(f32[64,64]{0,1:T(8,128)} %copy-done.57) | copy-start | bytes 49156
  1399.1 91.0 %reduce-scatter.22.cloned.1.call-start = ((), (), s32[]{:S(2)}) async-start(), calls=%async_computation.16 | async-start | bytes 589824
  1402.5 8.3 copy-start.62
  1419.2 13.1 copy-start.26
  1419.2 13.1 copy-start.41
  1419.2 2984.8 %reduce-scatter.14.cloned.1.call-start = ((), (), s32[]{:S(2)}) async-start(), calls=%async_computation.12 | async-start | bytes 250871808 | tf_op jit(solution)/shard_map/reduce_scatter | solution.py:333
  1421.5 18.9 copy-start.49
  1421.5 65.6 %copy-start.51 = (bf16[64,512]{0,1:T(8,128)(2,1)}, bf16[64,512]{0,1:T(8,128)(2,1)S(1)}, u32[]{:S(2)}) copy-start(bf16[64,512]{0,1:T(8,128)(2,1)S(1)} %get-tuple-element.1301) | copy-start | bytes 196612
  1432.2 8.2 copy-start.23
  1432.2 8.2 copy-start.34
  1440.4 23.5 copy-start.22
  1487.2 6.7 copy-start.29
  1487.2 6.7 copy-start.39
  1493.9 8.3 copy-start.24
  1493.9 8.3 copy-start.32
  1502.2 23.4 copy-start.20
  1870.5 17.6 copy-start.15
  1870.5 17.6 copy-start.17
  1870.5 34.5 slice-start
  1888.1 16.9 slice-start.1
  1888.1 16.9 copy-start.47
  1910.5 44.9 %copy-start.74 = (f32[64]{0:T(128)S(1)}, f32[64]{0:T(128)}, u32[]{:S(2)}) copy-start(f32[64]{0:T(128)} %copy-done.73) | copy-start | bytes 772
  1910.5 44.9 %copy-start.72 = (f32[64]{0:T(128)S(1)}, f32[64]{0:T(128)}, u32[]{:S(2)}) copy-start(f32[64]{0:T(128)} %copy-done.71) | copy-start | bytes 772
  1910.5 44.9 %copy-start.27 = (f32[64,2048]{1,0:T(8,128)S(1)}, f32[64,2048]{1,0:T(8,128)}, u32[]{:S(2)}) copy-start(f32[64,2048]{1,0:T(8,128)} %copy-done.25) | copy-start | bytes 1572868
  1910.5 44.9 %copy-start.30 = (f32[64,2048]{1,0:T(8,128)S(1)}, f32[64,2048]{1,0:T(8,128)}, u32[]{:S(2)}) copy-start(f32[64,2048]{1,0:T(8,128)} %copy-done.28) | copy-start | bytes 1572868
  (25 other events, 94.6 us)
Sparse Core Ops, SparseCore 0:
  11.0 59.2 all-gather.9
  73.3 55.4 all-gather.11
  131.8 77.1 all-gather.7
  211.8 76.8 all-gather.13
  291.5 193.5 all-gather.15
  488.0 192.9 all-gather.17
  684.0 192.9 all-gather.19
  1181.0 29.1 reduce-scatter.15
  1212.6 29.1 reduce-scatter.19
  1399.3 29.1 reduce-scatter.17
  1430.9 29.0 reduce-scatter.21
  1866.4 2537.5 reduce-scatter.13
where the time goes:
time: 4440 us; the launch traced here: 4420 us
  waiting for transfers between devices  3030 us (68%)
  matrix products  573 us (13%)
  local copies, waits for them, and re-layouts  366 us (8%)
  other arithmetic  282 us (6%)
  blocking collectives  148 us (3%)
    reduce_scatter x1, waiting for transfers between devices, body(): lax.psum_scatter(summed, ('dp', 'seq'), scatter_dimension=0, tiled=True)  2450 us
    dot_general x46, matrix products, inner_rows(): lax.dot_general(activation, gradient, (((0,), (0,)), ((), ())), preferred...  242 us
    add x1, other arithmetic, body(): summed = summed + one_term(entry, shard_rows * lax.axis_size(('dp', 'seq')))  229 us
    all_gather x1, waiting for transfers between devices, body(): lax.all_gather(w_down, ('dp', 'seq'), axis=0, tiled=True)  180 us
    all_gather x1, waiting for transfers between devices, body(): lax.all_gather(w_up, ('dp', 'seq'), axis=0, tiled=True)  180 us
    dot_general x62, matrix products, times_transposed(): lax.dot_general(gradient, weight, (((1,), (1,)), ((), ())), preferred_ele...  174 us
    reshape x2, local copies, waits for them, and re-layouts, one_term(): down_part = inner_rows(act_all, out_all).reshape(row_count, ratio * width)  159 us
    dot_general x46, matrix products, matmul(): return jnp.dot(activation, weight, preferred_element_type=jnp.float32)  157 us
  transfers between devices with their start and end apart: 12, of which 8 were waited for; matrix products, arithmetic and copies ran while one was open for 12% of the time, Pallas kernels for 0%

commit v1 on v0

v1 whole, which is shorter than its diff:
```python
import math

import jax
import jax.numpy as jnp
from jax import lax
from jax.sharding import PartitionSpec as P

HEADS = 32
KV_HEADS = 8
HEAD_DIM = 64
EPSILON = 1e-05
THETA = 500000.0
NEGATIVE = -1e30
BF16 = jnp.bfloat16
F32 = jnp.float32


def rope_table(positions, head_size):
    half_size = head_size // 2
    index_half = jnp.arange(half_size, dtype=jnp.float32)
    inverse = jnp.power(THETA, -2.0 * index_half / head_size)
    wavelength = 2.0 * math.pi / inverse
    smooth = (8192.0 / wavelength - 1.0) / 3.0
    blended = (1.0 - smooth) * inverse / 32.0 + smooth * inverse
    inverse = jnp.where(
        wavelength < 2048.0, inverse, jnp.where(wavelength > 8192.0, inverse / 32.0, blended)
    )
    angles = positions.astype(jnp.float32)[:, None] * inverse[None, :]
    cos_table = jnp.concatenate([jnp.cos(angles), jnp.cos(angles)], axis=1)
    sin_table = jnp.concatenate([jnp.sin(angles), jnp.sin(angles)], axis=1)
    return (cos_table, sin_table)


def rotate(values, cos_table, sin_table):
    half = HEAD_DIM // 2
    turned = jnp.concatenate([-values[..., half:], values[..., :half]], axis=-1)
    return values * cos_table + turned * sin_table


def rotate_back(gradient, cos_table, sin_table):
    half = HEAD_DIM // 2
    sined = gradient * sin_table
    turned = jnp.concatenate([sined[..., half:], -sined[..., :half]], axis=-1)
    return gradient * cos_table + turned


def rms_norm(values, gain_vec):
    scale_rows = lax.rsqrt(jnp.mean(values * values, axis=-1, keepdims=True) + EPSILON)
    return values * scale_rows * gain_vec


def swiglu(gate_in, up_in):
    return jax.nn.silu(gate_in) * up_in


def nn(a, b):
    return jnp.dot(a, b, preferred_element_type=F32)


def tn(a, b):
    return lax.dot_general(a, b, (((0,), (0,)), ((), ())), preferred_element_type=F32)


def nt(a, b):
    return lax.dot_general(a, b, (((1,), (1,)), ((), ())), preferred_element_type=F32)


def body(
    tokens, cotangent, prefix_len, attn_gain, w_query, w_key, w_value, w_out, mlp_gain, w_gate, w_up, w_down
):
    n_dp = lax.axis_size("dp")
    n_seq = lax.axis_size("seq")
    both = ("dp", "seq")
    micro, span, width = tokens.shape
    shard = w_query.shape[0]
    ff_block = w_down.shape[0]
    length = span * n_seq
    rows = micro * span
    group_heads = HEADS // n_seq
    repeat = max(1, n_seq // KV_HEADS)
    kv_here = max(1, KV_HEADS // n_seq)
    q_cols = group_heads * HEAD_DIM
    kv_cols = kv_here * HEAD_DIM
    s_index = lax.axis_index("seq")

    def spread(blocks):
        cols = blocks.shape[2]
        mine = lax.all_to_all(blocks, "seq", split_axis=0, concat_axis=0, tiled=True)
        return lax.all_gather(mine.reshape(n_seq * shard, cols), "dp", axis=0, tiled=True)

    def kv_blocks(w):
        w = w.reshape(shard, -1, 1, kv_cols)
        w = jnp.broadcast_to(w, (shard, n_seq // repeat, repeat, kv_cols))
        return w.reshape(shard, n_seq, kv_cols)

    qkv_blocks = jnp.concatenate(
        [w_query.reshape(shard, n_seq, q_cols), kv_blocks(w_key), kv_blocks(w_value)], axis=2
    ).transpose(1, 0, 2)
    wqkv = spread(qkv_blocks)

    def ff_blocks(w):
        return (
            w.reshape(shard, n_dp, n_seq, ff_block)
            .transpose(2, 0, 1, 3)
            .reshape(n_seq, shard, n_dp * ff_block)
        )

    gains = lax.all_gather(jnp.stack([attn_gain, mlp_gain]), both, axis=1, tiled=True).astype(F32)
    gain_attn, gain_mlp = gains[0], gains[1]
    w_out_all = lax.all_gather(w_out, both, axis=0, tiled=True)
    wo = lax.dynamic_slice_in_dim(w_out_all, s_index * q_cols, q_cols, 0)
    wg = spread(ff_blocks(w_gate))
    wu = spread(ff_blocks(w_up))
    wd = lax.all_gather(w_down, "dp", axis=0, tiled=True)

    def gather_rows(values):
        return lax.all_gather(values, "seq", axis=0, tiled=True)

    def scatter_rows(values):
        return lax.psum_scatter(
            values.astype(BF16), "seq", scatter_dimension=0, tiled=True
        ).astype(F32)

    tok = tokens.reshape(rows, width).astype(F32)
    cot = cotangent.reshape(rows, width)
    normed = gather_rows(rms_norm(tok, gain_attn).astype(BF16))
    cot_all = gather_rows(cot)

    def heads(values, count):
        return (
            values.reshape(n_seq, micro, span, count, HEAD_DIM)
            .transpose(1, 3, 0, 2, 4)
            .reshape(micro, count, length, HEAD_DIM)
        )

    def unheads(values):
        count = values.shape[1]
        return (
            values.reshape(micro, count, n_seq, span, HEAD_DIM)
            .transpose(2, 0, 3, 1, 4)
            .reshape(n_seq * rows, count * HEAD_DIM)
        )

    positions = jnp.arange(length, dtype=jnp.int32)
    cos_table, sin_table = rope_table(positions, HEAD_DIM)
    scale = 1.0 / math.sqrt(HEAD_DIM)
    qkv = nn(normed, wqkv)
    query = rotate(heads(qkv[:, :q_cols], group_heads), cos_table, sin_table).astype(BF16)
    key = rotate(heads(qkv[:, q_cols : q_cols + kv_cols], kv_here), cos_table, sin_table).astype(BF16)
    value = heads(qkv[:, q_cols + kv_cols :], kv_here).astype(BF16)
    per = group_heads // kv_here
    query = query.reshape(micro, kv_here, per, length, HEAD_DIM)
    allowed = (positions[None, :] <= positions[:, None])[None] | (
        positions[None, None, :] < prefix_len[:, None, None]
    )
    scores = jnp.einsum("mkgqd,mkjd->mkgqj", query, key, preferred_element_type=F32) * scale
    scores = jnp.where(allowed[:, None, None], scores, NEGATIVE)
    probs = jax.nn.softmax(scores, axis=-1)
    probs_low = probs.astype(BF16)
    mixed_heads = jnp.einsum("mkgqj,mkjd->mkgqd", probs_low, value, preferred_element_type=F32)
    mixed = unheads(mixed_heads.reshape(micro, group_heads, length, HEAD_DIM)).astype(BF16)
    hidden = tok + scatter_rows(nn(mixed, wo))

    normed_mlp = gather_rows(rms_norm(hidden, gain_mlp).astype(BF16))
    gate = nn(normed_mlp, wg)
    up = nn(normed_mlp, wu)
    activated = swiglu(gate, up).astype(BF16)
    block_out = (hidden + scatter_rows(nn(activated, wd))).astype(BF16)

    grad_act = nt(cot_all, wd)
    grad_gate, grad_up = jax.vjp(swiglu, gate, up)[1](grad_act)
    grad_gate = grad_gate.astype(BF16)
    grad_up = grad_up.astype(BF16)
    grad_normed_mlp = scatter_rows(nt(grad_gate, wg) + nt(grad_up, wu))
    grad_hidden_part, grad_mlp_gain = jax.vjp(rms_norm, hidden, gain_mlp)[1](grad_normed_mlp)
    grad_hidden = cot.astype(F32) + grad_hidden_part
    branch = gather_rows(grad_hidden.astype(BF16))

    def collect(grad):
        cols = grad.shape[1]
        mine = lax.psum_scatter(grad.astype(BF16), "dp", scatter_dimension=0, tiled=True)
        return lax.all_to_all(
            mine.reshape(n_seq, shard, cols), "seq", split_axis=0, concat_axis=0, tiled=True
        )

    def ff_unblocks(blocks):
        return (
            blocks.reshape(n_seq, shard, n_dp, ff_block)
            .transpose(1, 2, 0, 3)
            .reshape(shard, n_dp * n_seq * ff_block)
            .astype(F32)
        )

    w_gate_grad = ff_unblocks(collect(tn(normed_mlp, grad_gate)))
    w_up_grad = ff_unblocks(collect(tn(normed_mlp, grad_up)))
    w_down_grad = lax.psum_scatter(
        tn(activated, cot_all).astype(BF16), "dp", scatter_dimension=0, tiled=True
    ).astype(F32)

    grad_mixed = heads(nt(branch, wo), group_heads).astype(BF16)
    grad_mixed = grad_mixed.reshape(micro, kv_here, per, length, HEAD_DIM)
    out_grad = tn(mixed, branch).astype(BF16)
    ratio = n_seq // n_dp
    out_blocks = out_grad.reshape(1, n_dp, shard, width)
    slot = lax.broadcasted_iota(jnp.int32, (ratio, 1, 1, 1), 0)
    out_blocks = jnp.where(slot == s_index % ratio, out_blocks, 0).reshape(n_seq, shard, width)
    out_blocks = lax.all_to_all(out_blocks, "seq", split_axis=0, concat_axis=0, tiled=True)
    out_blocks = out_blocks.reshape(n_dp, ratio, shard, width)
    out_blocks = lax.dynamic_index_in_dim(out_blocks, s_index // n_dp, 1, keepdims=False)
    w_out_grad = lax.psum_scatter(
        out_blocks.reshape(n_dp * shard, width), "dp", scatter_dimension=0, tiled=True
    ).astype(F32)

    grad_probs = jnp.einsum("mkgqd,mkjd->mkgqj", grad_mixed, value, preferred_element_type=F32)
    delta = jnp.sum(probs * grad_probs, axis=-1, keepdims=True)
    grad_scores = (probs * (grad_probs - delta)).astype(BF16)
    grad_query = jnp.einsum("mkgqj,mkjd->mkgqd", grad_scores, key, preferred_element_type=F32) * scale
    grad_key = jnp.einsum("mkgqj,mkgqd->mkjd", grad_scores, query, preferred_element_type=F32) * scale
    grad_value = jnp.einsum("mkgqj,mkgqd->mkjd", probs_low, grad_mixed, preferred_element_type=F32)
    grad_query = grad_query.reshape(micro, group_heads, length, HEAD_DIM)
    grad_qkv = jnp.concatenate(
        [
            unheads(rotate_back(grad_query, cos_table, sin_table)),
            unheads(rotate_back(grad_key, cos_table, sin_table)),
            unheads(grad_value),
        ],
        axis=1,
    ).astype(BF16)
    grad_normed = scatter_rows(nt(grad_qkv, wqkv))
    tokens_part, grad_attn_gain = jax.vjp(rms_norm, tok, gain_attn)[1](grad_normed)
    input_grad = grad_hidden + tokens_part

    qkv_grad = collect(tn(normed, grad_qkv)).transpose(1, 0, 2).astype(F32)
    w_query_grad = qkv_grad[:, :, :q_cols].reshape(shard, -1)

    def kv_grad(values):
        return values.reshape(shard, n_seq // repeat, repeat, kv_cols).sum(axis=2).reshape(shard, -1)

    w_key_grad = kv_grad(qkv_grad[:, :, q_cols : q_cols + kv_cols])
    w_value_grad = kv_grad(qkv_grad[:, :, q_cols + kv_cols :])
    gain_grads = lax.psum_scatter(
        jnp.stack([grad_attn_gain, grad_mlp_gain]), both, scatter_dimension=1, tiled=True
    )
    return (
        block_out.reshape(micro, span, width),
        input_grad.reshape(micro, span, width),
        gain_grads[0],
        w_query_grad,
        w_key_grad,
        w_value_grad,
        w_out_grad,
        gain_grads[1],
        w_gate_grad,
        w_up_grad,
        w_down_grad,
    )


def solution(mesh):
    rows = P("dp", "seq", None)
    vec = P(("dp", "seq"))
    mat = P(("dp", "seq"), None)
    in_specs = (rows, rows, P("dp"), vec, mat, mat, mat, mat, vec, mat, mat, mat)
    out_specs = (rows, rows, vec, mat, mat, mat, mat, vec, mat, mat, mat)
    return jax.shard_map(body, mesh=mesh, in_specs=in_specs, out_specs=out_specs, check_vma=False)
```

time: 4440 us -> 1140 us (0.26)
  waiting for transfers between devices: 3030 us -> 704 us
  matrix products: 573 us -> 142 us
  local copies, waits for them, and re-layouts: 366 us -> 56.4 us
  other arithmetic: 282 us -> 34 us
    reduce_scatter x1 -> x9, waiting for transfers between devices: 2450 us -> 179 us  [the longest x4 163 us: scatter_rows(): lax.psum_scatter(values.astype(BF16), 'seq', scatter_dimension=0, tiled=T...]
    dot_general x154 -> x20, matrix products: 573 us -> 134 us  [the longest x5 38.8 us: nt(): lax.dot_general(a, b, (((1,), (1,)), ((), ())), preferred_element_type=F32)]
    all_gather x7 -> x9, waiting for transfers between devices: 577 us -> 315 us  [the longest x4 163 us: gather_rows(): return lax.all_gather(values, 'seq', axis=0, tiled=True)]
    add x5 -> x2, other arithmetic: 229 us -> 3.18 us  [the longest x1 3.17 us: body(): input_grad = grad_hidden + tokens_part]
    reshape x9 -> x21, local copies, waits for them, and re-layouts: 166 us -> 17.7 us  [the longest x2 3.85 us: body(): grad_query = grad_query.reshape(micro, group_heads, length, HEAD_DIM)]
    all_to_all x0 -> x4, blocking collectives: none -> 131 us  [the longest x3 100 us: spread(): lax.all_to_all(blocks, 'seq', split_axis=0, concat_axis=0, tiled=True)]
    unnamed x16 -> x20, waiting for transfers between devices: 8.47 us -> 134 us
    concatenate x2 -> x4, local copies, waits for them, and re-layouts: 88.8 us -> 3.99 us  [rotate_back(): turned = jnp.concatenate([sined[..., half:], -sined[..., :half]], axis=-1)]
  transfers between devices with their start and end apart: 12 -> 22, of which waited for: 8 -> 17; matrix products, arithmetic and copies ran while one was open for 12% -> 16% of each run, Pallas kernels for 0% -> 0%
where the time goes in v1:
time: 1140 us; the launch traced here: 1130 us
  waiting for transfers between devices  704 us (62%)
  blocking collectives  171 us (15%)
  matrix products  142 us (12%)
  local copies, waits for them, and re-layouts  56.4 us (5%)
  other arithmetic  34 us (3%)
  between operations  15.2 us (1%)
  starting transfers between devices  12.4 us (1%)
    reduce_scatter x4, waiting for transfers between devices, scatter_rows(): lax.psum_scatter(values.astype(BF16), 'seq', scatter_dimension=0, tiled=T...  163 us
    all_gather x4, waiting for transfers between devices, gather_rows(): return lax.all_gather(values, 'seq', axis=0, tiled=True)  163 us
    unnamed x20, waiting for transfers between devices  134 us
    all_to_all x3, blocking collectives, spread(): lax.all_to_all(blocks, 'seq', split_axis=0, concat_axis=0, tiled=True)  100 us
    all_gather x3, waiting for transfers between devices, spread(): lax.all_gather(mine.reshape(n_seq * shard, cols), 'dp', axis=0, tiled=True)  60.6 us
    all_to_all x1, waiting for transfers between devices, body(): lax.all_to_all(out_blocks, 'seq', split_axis=0, concat_axis=0, tiled=True)  48.9 us
    all_gather x1, waiting for transfers between devices, body(): w_out_all = lax.all_gather(w_out, both, axis=0, tiled=True)  46.8 us
    all_gather x1, waiting for transfers between devices, body(): wd = lax.all_gather(w_down, 'dp', axis=0, tiled=True)  44.7 us
  transfers between devices with their start and end apart: 22, of which 17 were waited for; matrix products, arithmetic and copies ran while one was open for 16% of the time, Pallas kernels for 0%

profile of v1, /device:TPU:0, one launch (start us, length us, event | category | flops | bytes accessed | tf_op | source)
XLA Modules:
  0.0 1134.0 jit_solution(4990478946950480249)
XLA Ops:
  10.4 18.8 %all_to_all.35 = bf16[8,64,384]{2,1,0:T(8,128)(2,1)} all-to-all(bf16[8,64,384]{2,1,0:T(8,128)(2,1)S(1)} %copy.115), channel_id=1, replica_groups=mesh['dp'=4,'seq'=8] {'seq'}, dimensions={0} | all-to-all | bytes 786432 | tf_op jit(solution)/shard_map/all_to_all | solution.py:88
  30.0 39.3 %all-gather = bf16[32,64,2]{1,2,0:T(2,128)(2,1)S(1)} all-gather(bf16[1,64,2]{1,2,0:T(2,128)(2,1)S(1)} %maximum_bitcast_fusion.1), channel_id=1, replica_groups=mesh['dp'=4,'seq'=8] {'dp','seq'}, dimensions={0}, use_global_device_ids=true | all-gather | bytes 8448 | tf_op jit(solution)/shard_map/all_gather | solution.py:108
  74.4 40.4 %all-gather.11.cloned.1.call-done = bf16[1024,2048]{1,0:T(8,128)(2,1)} async-done(((bf16[128,2048]{1,0:T(8,128)(2,1)}), bf16[1024,2048]{1,0:T(8,128)(2,1)}) %all-gather.11.cloned.1.call-update) | async-done | bytes 4194320 | tf_op jit(solution)/shard_map/all_gather | solution.py:117
  114.8 4.5 fusion.65
  123.2 3.0 reshape.403
  127.7 1.9 reshape.404
  132.8 7.5 fusion.64
  140.4 4.5 fusion.14
  147.1 46.8 %all-gather.15.cloned.1.call-done = bf16[2048,2048]{1,0:T(8,128)(2,1)} async-done(((bf16[64,2048]{1,0:T(8,128)(2,1)}), bf16[2048,2048]{1,0:T(8,128)(2,1)}) %all-gather.15.cloned.1.call-update) | async-done | bytes 8388624 | tf_op jit(solution)/shard_map/all_gather | solution.py:110
  193.9 4.5 convolution_convert_fusion.1
  200.0 47.4 %all_to_all.36 = bf16[8,64,1024]{2,1,0:T(8,128)(2,1)} all-to-all(bf16[8,64,1024]{2,1,0:T(8,128)(2,1)S(1)} %reshape.409), channel_id=1, replica_groups=mesh['dp'=4,'seq'=8] {'seq'}, dimensions={0} | all-to-all | bytes 2097152 | tf_op jit(solution)/shard_map/all_to_all | solution.py:88
  247.4 17.0 %reduce-scatter.13.cloned.1.call-done = bf16[128,2048]{1,0:T(8,128)(2,1)} async-done(((bf16[1024,2048]{1,0:T(8,128)(2,1)}), bf16[128,2048]{1,0:T(8,128)(2,1)}) %reduce-scatter.13.cloned.1.call-update) | async-done | bytes 524304 | tf_op jit(solution)/shard_map/reduce_scatter | solution.py:120
  265.7 2.0 multiply_convert_fusion.3
  269.3 34.2 %all_to_all.37 = bf16[8,64,1024]{2,1,0:T(8,128)(2,1)} all-to-all(bf16[8,64,1024]{2,1,0:T(8,128)(2,1)S(1)} %reshape.412), channel_id=1, replica_groups=mesh['dp'=4,'seq'=8] {'seq'}, dimensions={0} | all-to-all | bytes 2097152 | tf_op jit(solution)/shard_map/all_to_all | solution.py:88
  305.5 17.3 %all-gather.19.cloned.1.call-done = bf16[2048,1024]{1,0:T(8,128)(2,1)} async-done(((bf16[512,1024]{1,0:T(8,128)(2,1)}), bf16[2048,1024]{1,0:T(8,128)(2,1)}) %all-gather.19.cloned.1.call-update) | async-done | bytes 4194320 | tf_op jit(solution)/shard_map/all_gather | solution.py:89
  322.8 49.2 %all-gather.17.cloned.1.call-done = bf16[1024,2048]{1,0:T(8,128)(2,1)} async-done(((bf16[128,2048]{1,0:T(8,128)(2,1)}), bf16[1024,2048]{1,0:T(8,128)(2,1)}) %all-gather.17.cloned.1.call-update) | async-done | bytes 4194320 | tf_op jit(solution)/shard_map/all_gather | solution.py:117
  372.0 10.0 fusion.66
  382.0 43.3 %all-gather.21.cloned.1.call-done = bf16[2048,1024]{1,0:T(8,128)(2,1)} async-done(((bf16[512,1024]{1,0:T(8,128)(2,1)}), bf16[2048,1024]{1,0:T(8,128)(2,1)}) %all-gather.21.cloned.1.call-update) | async-done | bytes 4194320 | tf_op jit(solution)/shard_map/all_gather | solution.py:89
  425.3 9.9 fusion.67
  435.2 44.7 %all-gather.23.cloned.1.call-done = bf16[1024,2048]{1,0:T(8,128)(2,1)} async-done(((bf16[256,2048]{1,0:T(8,128)(2,1)}), bf16[1024,2048]{1,0:T(8,128)(2,1)}) %all-gather.23.cloned.1.call-update) | async-done | bytes 4194320 | tf_op jit(solution)/shard_map/all_gather | solution.py:114
  479.9 48.8 %all-gather.25.cloned.1.call-done = bf16[1024,2048]{1,0:T(8,128)(2,1)} async-done(((bf16[128,2048]{1,0:T(8,128)(2,1)}), bf16[1024,2048]{1,0:T(8,128)(2,1)}) %all-gather.25.cloned.1.call-update) | async-done | bytes 4194320 | tf_op jit(solution)/shard_map/all_gather | solution.py:117
  528.7 14.7 %multiply_convert_fusion.1 = (bf16[1024,1024]{1,0:T(8,128)(2,1)}, bf16[1024,1024]{1,0:T(8,128)(2,1)}, bf16[1024,1024]{1,0:T(8,128)(2,1)}) fusion(f32[1024,1024]{1,0:T(8,128)} %fusion.66, f32[1024,1024]{1,0:T(8,128)} %fusion.67, bf16[1024,2048]{1,0:T(8,128)(2,1)} %all-gather.25.cloned.1.call-done, bf16[1024,2048]{1,0:T(8,128)(2,1)} %all-gather.23.cloned.1.call-done), kind=kOutput, calls=%fused_computation.11 | convolution fusion | flops 4311744512 | bytes 23068672 | tf_op jit(solution)/shard_map/dot_general | solution.py:65
  543.3 6.5 fusion.68
  549.8 7.8 add_convert_fusion
  557.7 48.8 %reduce-scatter.17.cloned.1.call-done = bf16[128,2048]{1,0:T(8,128)(2,1)} async-done(((bf16[1024,2048]{1,0:T(8,128)(2,1)}), bf16[128,2048]{1,0:T(8,128)(2,1)}) %reduce-scatter.17.cloned.1.call-update) | async-done | bytes 524304 | tf_op jit(solution)/shard_map/reduce_scatter | solution.py:120
  608.1 2.3 fusion.59
  610.5 9.4 convolution_convert_fusion.4
  621.5 8.4 convolution_convert_fusion.3
  631.6 24.3 %all-gather.27.cloned.1.call-done = bf16[1024,2048]{1,0:T(8,128)(2,1)} async-done(((bf16[128,2048]{1,0:T(8,128)(2,1)}), bf16[1024,2048]{1,0:T(8,128)(2,1)}) %all-gather.27.cloned.1.call-update) | async-done | bytes 4194320 | tf_op jit(solution)/shard_map/all_gather | solution.py:117
  655.9 3.8 convolution_convert_fusion.8
  661.6 5.8 multiply_reduce_fusion
  667.4 4.8 multiply_convert_fusion
  672.3 2.3 broadcast_multiply_fusion.1
  674.9 1.8 copy.127
  676.9 1.8 copy.128
  678.7 1.6 reshape.416
  680.4 2.2 copy.126
  682.6 4.4 fusion.38
  687.7 3.8 convolution_bitcast_fusion
  692.4 5.1 fusion.24
  698.2 5.8 convolution_convert_fusion.6
  704.3 9.4 convolution_convert_fusion.2
  714.8 3.5 convolution_convert_fusion.7
  719.7 3.6 all-to-all-start.4
  723.4 48.9 %all-to-all-done.4 = bf16[8,64,2048]{2,1,0:T(8,128)(2,1)S(1)} async-done(((bf16[8,64,2048]{2,1,0:T(8,128)(2,1)}), bf16[8,64,2048]{2,1,0:T(8,128)(2,1)S(1)}, u32[]{:S(2)}, u32[]{:S(2)}) %all-to-all-start.4) | async-done | bytes 2097184 | tf_op jit(solution)/shard_map/all_to_all | solution.py:207
  773.5 6.0 convolution_convert_fusion
  781.1 8.5 convolution_convert_fusion.5
  789.6 3.6 all-to-all-start.5
  793.3 26.5 %all-to-all-done.5 = bf16[8,64,1024]{2,1,0:T(8,128)(2,1)S(1)} async-done(((bf16[8,64,1024]{2,1,0:T(8,128)(2,1)}), bf16[8,64,1024]{2,1,0:T(8,128)(2,1)S(1)}, u32[]{:S(2)}, u32[]{:S(2)}) %all-to-all-start.5) | async-done | bytes 1048608 | tf_op jit(solution)/shard_map/all_to_all | solution.py:182
  819.7 30.8 %all_to_all.38 = bf16[8,64,1024]{2,1,0:T(8,128)(2,1)} all-to-all(bf16[8,64,1024]{2,1,0:T(8,128)(2,1)} %bitcast.243), channel_id=1, replica_groups=mesh['dp'=4,'seq'=8] {'seq'}, dimensions={0} | all-to-all | bytes 2097152 | tf_op jit(solution)/shard_map/all_to_all | solution.py:182
  850.6 3.5 all-to-all-start.3
  854.3 1.8 reduce-scatter.29.cloned.1.call-done
  856.1 2.8 convert_element_type.247
  858.9 2.0 reshape.436
  862.1 2.5 copy.158
  864.6 2.0 reshape.437
  867.8 2.5 copy.159
  873.4 14.0 %reduce-scatter.23.cloned.1.call-done = bf16[64,2048]{1,0:T(8,128)(2,1)} async-done(((bf16[256,2048]{1,0:T(8,128)(2,1)}), bf16[64,2048]{1,0:T(8,128)(2,1)}) %reduce-scatter.23.cloned.1.call-update) | async-done | bytes 262160 | tf_op jit(solution)/shard_map/reduce_scatter | solution.py:210
  887.4 1.8 convert_element_type.235
  889.1 50.4 %reduce-scatter.19.cloned.1.call-done = bf16[128,2048]{1,0:T(8,128)(2,1)} async-done(((bf16[1024,2048]{1,0:T(8,128)(2,1)}), bf16[128,2048]{1,0:T(8,128)(2,1)}) %reduce-scatter.19.cloned.1.call-update) | async-done | bytes 524304 | tf_op jit(solution)/shard_map/reduce_scatter | solution.py:120
  939.6 1.6 fusion.30
  942.6 47.3 %reduce-scatter.15.cloned.1.call-done = bf16[128,2048]{1,0:T(8,128)(2,1)} async-done(((bf16[1024,2048]{1,0:T(8,128)(2,1)}), bf16[128,2048]{1,0:T(8,128)(2,1)}) %reduce-scatter.15.cloned.1.call-update) | async-done | bytes 524304 | tf_op jit(solution)/shard_map/reduce_scatter | solution.py:120
  989.9 3.2 fusion.32
  993.1 132.1 %reduce-scatter.31.cloned.1.call-done = f32[64,2]{1,0:T(8,128)} async-done(((f32[2048,2]{1,0:T(8,128)}), f32[64,2]{1,0:T(8,128)}) %reduce-scatter.31.cloned.1.call-update) | async-done | bytes 528
  (214 shorter events, 50.3 us)
Async XLA Ops:
  7.2 62.2 %copy-start.1 = (bf16[2,64,2048]{2,1,0:T(8,128)(2,1)S(1)}, bf16[2,64,2048]{2,1,0:T(8,128)(2,1)}, u32[]{:S(2)}) copy-start(bf16[2,64,2048]{2,1,0:T(8,128)(2,1)} %param.12) | copy-start | bytes 1572868
  7.2 66.0 %copy-start.34 = (s32[2]{0:T(128)S(1)}, s32[2]{0:T(128)}, u32[]{:S(2)}) copy-start(s32[2]{0:T(128)} %param.14) | copy-start | bytes 28
  7.2 67.2 %all-gather.13.cloned.1.call-start = ((), (), s32[]{:S(2)}) async-start(), calls=%async_computation.18 | async-start | bytes 1966080 | tf_op jit(solution)/shard_map/all_gather | solution.py:89
  29.2 85.5 %all-gather.11.cloned.1.call-start = ((), (), s32[]{:S(2)}) async-start(), calls=%async_computation.17 | async-start | bytes 4718592 | tf_op jit(solution)/shard_map/all_gather | solution.py:117
  69.6 0.5 copy-start.37
  70.2 1.8 copy-start.28
  70.2 1.8 copy-start.21
  71.2 122.7 %all-gather.15.cloned.1.call-start = ((), (), s32[]{:S(2)}) async-start(), calls=%async_computation.19 | async-start | bytes 8650752 | tf_op jit(solution)/shard_map/all_gather | solution.py:110
  71.9 192.5 %reduce-scatter.13.cloned.1.call-start = ((), (), s32[]{:S(2)}) async-start(), calls=%async_computation.20 | async-start | bytes 4718592 | tf_op jit(solution)/shard_map/reduce_scatter | solution.py:120
  72.0 47.3 %copy-start.32 = (f32[32]{0:T(128)}, f32[32]{0:T(128)S(1)}, u32[]{:S(2)}) copy-start(f32[32]{0:T(128)S(1)} %compare_select_fusion.1) | copy-start | bytes 388
  126.2 5.5 copy-start.12
  126.2 5.5 copy-start.11
  132.8 7.6 copy-start.9
  132.8 7.6 copy-start.23
  140.4 4.5 copy-start.24
  147.1 51.3 %copy-start.7 = (bf16[1024,256]{1,0:T(8,128)(2,1)}, bf16[1024,256]{1,0:T(8,128)(2,1)S(1)}, u32[]{:S(2)}) copy-start(bf16[1024,256]{1,0:T(8,128)(2,1)S(1)} %convert_element_type.209) | copy-start | bytes 1572868
  147.1 51.4 %copy-start.13 = (bf16[64,8192]{1,0:T(8,128)(2,1)S(1)}, bf16[64,8192]{1,0:T(8,128)(2,1)}, u32[]{:S(2)}) copy-start(bf16[64,8192]{1,0:T(8,128)(2,1)} %param.21) | copy-start | bytes 3145732
  198.5 124.3 %all-gather.19.cloned.1.call-start = ((), (), s32[]{:S(2)}) async-start(), calls=%async_computation.22 | async-start | bytes 5242880 | tf_op jit(solution)/shard_map/all_gather | solution.py:89
  200.0 67.9 %copy-start.14 = (bf16[64,8192]{1,0:T(8,128)(2,1)S(1)}, bf16[64,8192]{1,0:T(8,128)(2,1)}, u32[]{:S(2)}) copy-start(bf16[64,8192]{1,0:T(8,128)(2,1)} %param.22) | copy-start | bytes 3145732
  247.4 124.6 %all-gather.17.cloned.1.call-start = ((), (), s32[]{:S(2)}) async-start(), calls=%async_computation.21 | async-start | bytes 4718592 | tf_op jit(solution)/shard_map/all_gather | solution.py:117
  265.7 342.4 %copy-start.26 = (f32[128]{0:T(128)}, f32[128]{0:T(128)S(1)}, u32[]{:S(2)}) copy-start(f32[128]{0:T(128)S(1)} %fusion.54) | copy-start | bytes 1540
  267.8 157.5 %all-gather.21.cloned.1.call-start = ((), (), s32[]{:S(2)}) async-start(), calls=%async_computation.23 | async-start | bytes 5242880 | tf_op jit(solution)/shard_map/all_gather | solution.py:89
  303.6 176.3 %all-gather.23.cloned.1.call-start = ((), (), s32[]{:S(2)}) async-start(), calls=%async_computation.24 | async-start | bytes 5242880 | tf_op jit(solution)/shard_map/all_gather | solution.py:114
  304.3 224.4 %all-gather.25.cloned.1.call-start = ((), (), s32[]{:S(2)}) async-start(), calls=%async_computation.26 | async-start | bytes 4718592 | tf_op jit(solution)/shard_map/all_gather | solution.py:117
  305.1 301.5 %reduce-scatter.17.cloned.1.call-start = ((), (), s32[]{:S(2)}) async-start(), calls=%async_computation.27 | async-start | bytes 4718592 | tf_op jit(solution)/shard_map/reduce_scatter | solution.py:120
  528.7 14.7 %copy-start.35 = (bf16[2048,1024]{1,0:T(8,128)(2,1)S(1)}, bf16[2048,1024]{1,0:T(8,128)(2,1)}, u32[]{:S(2)}) copy-start(bf16[2048,1024]{1,0:T(8,128)(2,1)} %all-gather.19.cloned.1.call-done) | copy-start | bytes 12582916
  543.3 6.5 copy-start.36
  557.7 48.9 %copy-start.2 = (bf16[128,2048]{1,0:T(8,128)(2,1)S(1)}, bf16[128,2048]{1,0:T(8,128)(2,1)}, u32[]{:S(2)}) copy-start(bf16[128,2048]{1,0:T(8,128)(2,1)} %reduce-scatter.13.cloned.1.call-done) | copy-start | bytes 1572868
  557.7 50.5 %copy-start.3 = (bf16[2,64,2048]{2,1,0:T(8,128)(2,1)S(1)}, bf16[2,64,2048]{2,1,0:T(8,128)(2,1)}, u32[]{:S(2)}) copy-start(bf16[2,64,2048]{2,1,0:T(8,128)(2,1)} %param.13) | copy-start | bytes 1572868
  557.7 98.2 %all-gather.27.cloned.1.call-start = ((), (), s32[]{:S(2)}) async-start(), calls=%async_computation.28 | async-start | bytes 4718592 | tf_op jit(solution)/shard_map/all_gather | solution.py:117
  608.1 11.8 %copy-start.30 = (f32[128]{0:T(128)}, f32[128]{0:T(128)S(1)}, u32[]{:S(2)}) copy-start(f32[128]{0:T(128)S(1)} %multiply_multiply_fusion.1) | copy-start | bytes 1540
  610.4 179.2 %reduce-scatter.25.cloned.1.call-start = ((), (), s32[]{:S(2)}) async-start(), calls=%async_computation.32 | async-start | bytes 5242880 | tf_op jit(solution)/shard_map/reduce_scatter | solution.py:181
  619.9 1.6 copy-start.40
  619.9 173.3 %reduce-scatter.27.cloned.1.call-start = ((), (), s32[]{:S(2)}) async-start(), calls=%async_computation.33 | async-start | bytes 5242880 | tf_op jit(solution)/shard_map/reduce_scatter | solution.py:181
  629.9 0.7 copy-start.33
  629.9 220.7 %reduce-scatter.21.cloned.1.call-start = ((), (), s32[]{:S(2)}) async-start(), calls=%async_computation.30 | async-start | bytes 1966080 | tf_op jit(solution)/shard_map/reduce_scatter | solution.py:181
  661.6 5.8 copy-start.16
  661.6 5.8 copy-start.25
  667.4 4.8 copy-start.18
  672.2 2.5 copy-start
  682.6 5.1 copy-start.10
  687.0 4.6 copy-start.19
  687.7 10.5 copy-start.15
  687.7 4.7 copy-start.17
  698.2 5.9 copy-start.20
  704.1 152.0 %reduce-scatter.29.cloned.1.call-start = ((), (), s32[]{:S(2)}) async-start(), calls=%async_computation.34 | async-start | bytes 5242880 | tf_op jit(solution)/shard_map/reduce_scatter | solution.py:196
  713.7 1.0 copy-start.8
  719.7 52.6 %all-to-all-start.4 = ((bf16[8,64,2048]{2,1,0:T(8,128)(2,1)}), bf16[8,64,2048]{2,1,0:T(8,128)(2,1)S(1)}, u32[]{:S(2)}, u32[]{:S(2)}) async-start(bf16[8,64,2048]{2,1,0:T(8,128)(2,1)} %bitcast_select_fusion), calls=%async_computation.9 | async-start | bytes 4194304 | tf_op jit(solution)/shard_map/all_to_all | solution.py:207
  723.4 164.0 %reduce-scatter.23.cloned.1.call-start = ((), (), s32[]{:S(2)}) async-start(), calls=%async_computation.31 | async-start | bytes 1310720 | tf_op jit(solution)/shard_map/reduce_scatter | solution.py:210
  773.4 166.1 %reduce-scatter.19.cloned.1.call-start = ((), (), s32[]{:S(2)}) async-start(), calls=%async_computation.29 | async-start | bytes 4718592 | tf_op jit(solution)/shard_map/reduce_scatter | solution.py:120
  779.5 1.6 copy-start.39
  779.5 210.4 %reduce-scatter.15.cloned.1.call-start = ((), (), s32[]{:S(2)}) async-start(), calls=%async_computation.25 | async-start | bytes 4718592 | tf_op jit(solution)/shard_map/reduce_scatter | solution.py:120
  789.6 30.1 %all-to-all-start.5 = ((bf16[8,64,1024]{2,1,0:T(8,128)(2,1)}), bf16[8,64,1024]{2,1,0:T(8,128)(2,1)S(1)}, u32[]{:S(2)}, u32[]{:S(2)}) async-start(bf16[8,64,1024]{2,1,0:T(8,128)(2,1)} %bitcast.242), calls=%async_computation.12 | async-start | bytes 2097152 | tf_op jit(solution)/shard_map/all_to_all | solution.py:182
  819.7 36.3 %copy-start.6 = (bf16[8,64,1024]{2,1,0:T(8,128)(2,1)}, bf16[8,64,1024]{2,1,0:T(8,128)(2,1)S(1)}, u32[]{:S(2)}) copy-start(bf16[8,64,1024]{2,1,0:T(8,128)(2,1)S(1)} %all-to-all-done.5) | copy-start | bytes 3145732
  850.6 19.8 %all-to-all-start.3 = ((bf16[8,64,384]{2,1,0:T(8,128)(2,1)}), bf16[8,64,384]{2,1,0:T(8,128)(2,1)S(1)}, u32[]{:S(2)}, u32[]{:S(2)}) async-start(bf16[8,64,384]{2,1,0:T(8,128)(2,1)} %bitcast.251), calls=%async_computation.8 | async-start | bytes 786432 | tf_op jit(solution)/shard_map/all_to_all | solution.py:182
  854.1 271.1 %reduce-scatter.31.cloned.1.call-start = ((), (), s32[]{:S(2)}) async-start(), calls=%async_computation.35 | async-start | bytes 1081344
  870.4 69.2 %copy-start.22 = (f32[1,2048]{1,0:T(1,128)S(1)}, f32[1,2048]{1,0:T(1,128)}, u32[]{:S(2)}) copy-start(f32[1,2048]{1,0:T(1,128)} %copy-done.21) | copy-start | bytes 24580
  870.4 69.2 %copy-start.29 = (f32[128]{0:T(128)S(1)}, f32[128]{0:T(128)}, u32[]{:S(2)}) copy-start(f32[128]{0:T(128)} %copy-done.28) | copy-start | bytes 1540
  870.4 72.2 %copy-start.38 = (f32[128]{0:T(128)S(1)}, f32[128]{0:T(128)}, u32[]{:S(2)}) copy-start(f32[128]{0:T(128)} %copy-done.37) | copy-start | bytes 1540
  870.5 119.4 %copy-start.4 = (bf16[2,64,2048]{2,1,0:T(8,128)(2,1)S(1)}, bf16[2,64,2048]{2,1,0:T(8,128)(2,1)}, u32[]{:S(2)}) copy-start(bf16[2,64,2048]{2,1,0:T(8,128)(2,1)} %param.13) | copy-start | bytes 1572868
  870.5 119.4 %copy-start.5 = (bf16[128,2048]{1,0:T(8,128)(2,1)S(1)}, bf16[128,2048]{1,0:T(8,128)(2,1)}, u32[]{:S(2)}) copy-start(bf16[128,2048]{1,0:T(8,128)(2,1)} %reduce-scatter.17.cloned.1.call-done) | copy-start | bytes 1572868
  870.5 119.4 %copy-start.27 = (f32[128]{0:T(128)S(1)}, f32[128]{0:T(128)}, u32[]{:S(2)}) copy-start(f32[128]{0:T(128)} %copy-done.26) | copy-start | bytes 1540
  870.5 119.4 %copy-start.31 = (f32[128]{0:T(128)S(1)}, f32[128]{0:T(128)}, u32[]{:S(2)}) copy-start(f32[128]{0:T(128)} %copy-done.30) | copy-start | bytes 1540
Sparse Core Ops, SparseCore 0:
  29.4 29.9 all-gather.12
  71.3 43.4 all-gather.10
  117.8 76.1 all-gather.14
  198.6 65.8 reduce-scatter.12
  266.1 56.6 all-gather.18
  324.8 47.1 all-gather.16
  373.8 51.4 all-gather.20
  427.1 52.6 all-gather.22
  481.5 47.1 all-gather.24
  557.8 48.7 reduce-scatter.16
  610.6 45.2 all-gather.26
  658.7 51.4 reduce-scatter.24
  713.4 52.6 reduce-scatter.26
  769.5 30.9 reduce-scatter.20
  803.3 52.6 reduce-scatter.28
  859.7 27.6 reduce-scatter.22
  889.5 50.0 reduce-scatter.18
  941.7 48.1 reduce-scatter.14
  992.1 132.9 reduce-scatter.30

commit v2 on v1

v2 whole, which is shorter than its diff:
```python
import functools
import math

import jax
import jax.numpy as jnp
from jax import lax
from jax.experimental import pallas as pl
from jax.experimental.pallas import tpu as pltpu
from jax.sharding import PartitionSpec as P

HEADS = 32
KV_HEADS = 8
HEAD_DIM = 64
EPSILON = 1e-05
THETA = 500000.0
NEGATIVE = -1e30
BF16 = jnp.bfloat16
F32 = jnp.float32
MESH = pl.DeviceIdType.MESH
TILE = 256
QUERY_TILE = 256
VMEM_LIMIT = 60 << 20


def rope_table(positions, head_size):
    half_size = head_size // 2
    index_half = jnp.arange(half_size, dtype=jnp.float32)
    inverse = jnp.power(THETA, -2.0 * index_half / head_size)
    wavelength = 2.0 * math.pi / inverse
    smooth = (8192.0 / wavelength - 1.0) / 3.0
    blended = (1.0 - smooth) * inverse / 32.0 + smooth * inverse
    inverse = jnp.where(
        wavelength < 2048.0, inverse, jnp.where(wavelength > 8192.0, inverse / 32.0, blended)
    )
    angles = positions.astype(jnp.float32)[:, None] * inverse[None, :]
    cos_table = jnp.concatenate([jnp.cos(angles), jnp.cos(angles)], axis=1)
    sin_table = jnp.concatenate([jnp.sin(angles), jnp.sin(angles)], axis=1)
    return (cos_table, sin_table)


def nn(a, b):
    return jnp.dot(a, b, preferred_element_type=F32)


def tn(a, b):
    return lax.dot_general(a, b, (((0,), (0,)), ((), ())), preferred_element_type=F32)


def nt(a, b):
    return lax.dot_general(a, b, (((1,), (1,)), ((), ())), preferred_element_type=F32)


class Line:
    def __init__(self, n_seq):
        self.n_line = n_seq // 2
        self.last = self.n_line - 1
        self.s = lax.axis_index("seq")
        self.c = lax.rem(self.s, 2)
        self.l = lax.div(self.s, 2)
        self.sibling = self.s + 1 - 2 * self.c
        self.right = jnp.minimum(self.s + 2, n_seq - 2 + self.c)
        self.left = jnp.maximum(self.s - 2, self.c)
        self.has_right = self.l < self.last
        self.has_left = self.l > 0

    def greet(self):
        barrier = pltpu.get_barrier_semaphore()
        pl.semaphore_signal(barrier, 1, device_id={"seq": self.sibling}, device_id_type=MESH)

        @pl.when(self.has_right)
        def _():
            pl.semaphore_signal(barrier, 1, device_id={"seq": self.right}, device_id_type=MESH)

        @pl.when(self.has_left)
        def _():
            pl.semaphore_signal(barrier, 1, device_id={"seq": self.left}, device_id_type=MESH)

        pl.semaphore_wait(barrier, jnp.where(self.has_right & self.has_left, 3, 2))

    def order(self, j):
        near = jnp.minimum(self.l, self.last - self.l)
        half = lax.div(j + 1, 2)
        both = jnp.where(lax.rem(j, 2) == 1, self.l - half, self.l + half)
        far = jnp.where(self.l <= self.last - self.l, j, self.last - j)
        return jnp.where(j <= 2 * near, both, far)


def remote(src, dst, send, recv, seq):
    return pltpu.make_async_remote_copy(
        src_ref=src, dst_ref=dst, send_sem=send, recv_sem=recv, device_id={"seq": seq}, device_id_type=MESH
    )


class Gather:
    def __init__(self, line, full, send_z, send_c, recv):
        self.line, self.full, self.send_z, self.send_c, self.recv = line, full, send_z, send_c, recv

    @staticmethod
    def sems(n_seq):
        n_line = n_seq // 2
        return [
            pltpu.SemaphoreType.DMA((n_line + 1,)),
            pltpu.SemaphoreType.DMA((n_line,)),
            pltpu.SemaphoreType.DMA((n_seq,)),
        ]

    def copy(self, index, send, seq):
        return remote(self.full.at[index], self.full.at[index], send, self.recv.at[index], seq)

    def begin(self):
        n = self.line
        pl.when(n.has_right)(lambda: self.copy(n.s, self.send_z.at[n.l], n.right).start())
        pl.when(n.has_left)(lambda: self.copy(n.s, self.send_z.at[n.n_line], n.left).start())
        self.copy(n.s, self.send_c.at[n.l], n.sibling).start()

    def visit(self, chip):
        n = self.line
        mine = 2 * chip + n.c

        @pl.when(chip != n.l)
        def _():
            self.copy(mine, self.send_c.at[chip], n.sibling).wait_recv()
            pl.when((chip < n.l) & n.has_right)(
                lambda: self.copy(mine, self.send_z.at[chip], n.right).start()
            )
            pl.when((chip > n.l) & n.has_left)(
                lambda: self.copy(mine, self.send_z.at[chip], n.left).start()
            )
            self.copy(mine, self.send_c.at[chip], n.sibling).start()

        self.copy(2 * chip + 1 - n.c, self.send_c.at[chip], n.sibling).wait_recv()

    def end(self):
        n = self.line

        @pl.loop(0, n.n_line)
        def _(chip):
            mine = 2 * chip + n.c
            self.copy(mine, self.send_c.at[chip], n.sibling).wait_send()
            pl.when((chip <= n.l) & n.has_right)(
                lambda: self.copy(mine, self.send_z.at[chip], n.right).wait_send()
            )
            pl.when((chip > n.l) & n.has_left)(
                lambda: self.copy(mine, self.send_z.at[chip], n.left).wait_send()
            )

        pl.when(n.has_left)(lambda: self.copy(n.s, self.send_z.at[n.n_line], n.left).wait_send())


class Scatter:
    def __init__(self, line, part, sib, rcv, send_z, send_c, recv_z, recv_c):
        self.line, self.part, self.sib, self.rcv = line, part, sib, rcv
        self.send_z, self.send_c, self.recv_z, self.recv_c = send_z, send_c, recv_z, recv_c

    @staticmethod
    def sems(n_seq):
        n_line = n_seq // 2
        return [
            pltpu.SemaphoreType.DMA((n_line,)),
            pltpu.SemaphoreType.DMA((n_line,)),
            pltpu.SemaphoreType.DMA((n_line + 1,)),
            pltpu.SemaphoreType.DMA((n_line,)),
        ]

    @staticmethod
    def buffers(n_seq, rows, width):
        n_line = n_seq // 2
        return [
            pltpu.VMEM((n_line, rows, width), BF16),
            pltpu.VMEM((n_line + 1, rows, width), BF16),
        ]

    def across(self, chip):
        n = self.line
        return remote(
            self.part.at[2 * chip + 1 - n.c],
            self.sib.at[chip],
            self.send_c.at[chip],
            self.recv_c.at[chip],
            n.sibling,
        )

    def hop(self, chip, slot, seq):
        n = self.line
        return remote(
            self.part.at[2 * chip + n.c],
            self.rcv.at[slot],
            self.send_z.at[chip],
            self.recv_z.at[slot],
            seq,
        )

    def begin(self):
        n = self.line

        @pl.loop(0, n.n_line)
        def _(j):
            half = lax.div(j, 2)
            self.across(jnp.where(lax.rem(j, 2) == 0, n.last - half, half)).start()

    def add(self, chip, source):
        mine = 2 * chip + self.line.c
        self.part[mine] = (self.part[mine].astype(F32) + source.astype(F32)).astype(BF16)

    def step(self, time):
        n = self.line

        @pl.when(n.l <= time)
        def _():
            chip = n.last - time + n.l
            self.across(chip).wait_recv()
            self.add(chip, self.sib[chip])

            @pl.when(n.has_left)
            def _():
                self.hop(chip, chip, n.right).wait_recv()
                self.add(chip, self.rcv[chip])

            self.hop(chip, chip, n.right).start()

        @pl.when(n.last - n.l <= time)
        def _():
            chip = time - n.last + n.l
            self.across(chip).wait_recv()
            self.add(chip, self.sib[chip])

            @pl.when(n.has_right)
            def _():
                self.hop(chip, chip, n.left).wait_recv()
                self.add(chip, self.rcv[chip])

            self.hop(chip, jnp.where(chip == n.l - 1, n.n_line, chip), n.left).start()

    def finish(self, out):
        n = self.line
        mine = 2 * n.l + n.c
        self.across(n.l).wait_recv()
        out[...] = self.part[mine].astype(F32) + self.sib[n.l].astype(F32)

        @pl.when(n.has_left)
        def _():
            self.hop(n.l, n.l, n.right).wait_recv()
            out[...] += self.rcv[n.l].astype(F32)

        @pl.when(n.has_right)
        def _():
            self.hop(n.l, n.n_line, n.left).wait_recv()
            out[...] += self.rcv[n.n_line].astype(F32)

        @pl.loop(0, n.n_line)
        def _(chip):
            self.across(chip).wait_send()
            pl.when(chip > n.l)(lambda: self.hop(chip, chip, n.right).wait_send())
            pl.when(chip < n.l)(lambda: self.hop(chip, chip, n.left).wait_send())


def spread_work(units, slots, index):
    return (units * index // slots, units * (index + 1) // slots)


class Spread:
    def __init__(self, line, n_dp, blocks, dst, own_sem, send_z, send_xy, recv):
        self.line, self.n_dp, self.blocks, self.dst = line, n_dp, blocks, dst
        self.own_sem, self.send_z, self.send_xy, self.recv = own_sem, send_z, send_xy, recv
        self.n_seq = 2 * line.n_line
        self.d = lax.axis_index("dp")

    @staticmethod
    def sems(n_seq, n_dp):
        return [
            pltpu.SemaphoreType.DMA((1,)),
            pltpu.SemaphoreType.DMA((n_seq,)),
            pltpu.SemaphoreType.DMA((n_seq, n_dp)),
            pltpu.SemaphoreType.DMA((n_dp, n_seq)),
        ]

    def hop(self, t):
        n = self.line
        return pltpu.make_async_remote_copy(
            src_ref=self.blocks.at[t],
            dst_ref=self.dst.at[self.d, n.s],
            send_sem=self.send_z.at[t],
            recv_sem=self.recv.at[self.d, n.s],
            device_id={"seq": t},
            device_id_type=MESH,
        )

    def own(self):
        n = self.line
        return pltpu.make_async_copy(self.blocks.at[n.s], self.dst.at[self.d, n.s], self.own_sem.at[0])

    def over(self, source, k, own=False):
        return pltpu.make_async_remote_copy(
            src_ref=self.blocks.at[self.line.s] if own else self.dst.at[self.d, source],
            dst_ref=self.dst.at[self.d, source],
            send_sem=self.send_xy.at[source, k],
            recv_sem=self.recv.at[self.d, source],
            device_id={"dp": lax.rem(self.d + k, self.n_dp)},
            device_id_type=MESH,
        )

    def landed(self, d, source):
        return pltpu.make_async_remote_copy(
            src_ref=self.dst.at[d, source],
            dst_ref=self.dst.at[d, source],
            send_sem=self.send_z.at[0],
            recv_sem=self.recv.at[d, source],
            device_id={"dp": d},
            device_id_type=MESH,
        )

    def begin(self):
        n = self.line

        @pl.loop(1, self.n_seq)
        def _(j):
            self.hop(lax.rem(n.s + j, self.n_seq)).start()

        self.own().start()

    def forward_own(self):
        for k in range(1, self.n_dp):
            self.over(self.line.s, k, True).start()

    def forward(self, first, end):
        n = self.line

        @pl.loop(first, end)
        def _(j):
            source = lax.rem(n.s - j + self.n_seq, self.n_seq)
            self.landed(self.d, source).wait_recv()
            for k in range(1, self.n_dp):
                self.over(source, k).start()

    def arrive(self):
        for k in range(1, self.n_dp):
            owner = lax.rem(self.d + k, self.n_dp)

            @pl.loop(0, self.n_seq)
            def _(source):
                self.landed(owner, source).wait_recv()

        self.own().wait()

    def end(self):
        n = self.line

        @pl.loop(0, self.n_seq)
        def _(j):
            pl.when(j != n.s)(lambda: self.hop(j).wait_send())
            for k in range(1, self.n_dp):
                self.over(j, k).wait_send()


class Copies:
    def __init__(self, n_dp, own, dst, own_sem, send, recv):
        self.n_dp, self.own_ref, self.dst = n_dp, own, dst
        self.own_sem, self.send, self.recv = own_sem, send, recv
        self.d = lax.axis_index("dp")

    @staticmethod
    def sems(n_dp):
        return [
            pltpu.SemaphoreType.DMA((1,)),
            pltpu.SemaphoreType.DMA((n_dp,)),
            pltpu.SemaphoreType.DMA((n_dp,)),
        ]

    def copy(self, k, slot):
        return pltpu.make_async_remote_copy(
            src_ref=self.own_ref,
            dst_ref=self.dst.at[slot],
            send_sem=self.send.at[k],
            recv_sem=self.recv.at[slot],
            device_id={"dp": lax.rem(self.d + k, self.n_dp)},
            device_id_type=MESH,
        )

    def begin(self):
        for k in range(1, self.n_dp):
            self.copy(k, self.d).start()
        pltpu.make_async_copy(self.own_ref, self.dst.at[self.d], self.own_sem.at[0]).start()

    def end(self):
        for k in range(1, self.n_dp):
            self.copy(k, lax.rem(self.d + k, self.n_dp)).wait()
        pltpu.make_async_copy(self.own_ref, self.dst.at[self.d], self.own_sem.at[0]).wait()


class OutRows:
    def __init__(self, line, n_dp, own, dst, own_sem, send_z, send_xy, recv):
        self.line, self.n_dp, self.own_ref, self.dst = line, n_dp, own, dst
        self.own_sem, self.send_z, self.send_xy, self.recv = own_sem, send_z, send_xy, recv
        self.n_seq = 2 * line.n_line
        self.ratio = self.n_seq // n_dp
        self.d = lax.axis_index("dp")
        block = self.d * self.n_seq + line.s
        self.target = lax.div(block, n_dp)
        self.slot = lax.rem(block, n_dp)
        self.source_d = lax.div(line.s, self.ratio)
        self.source_s = lax.rem(line.s, self.ratio) * n_dp

    @staticmethod
    def sems(n_dp):
        return [
            pltpu.SemaphoreType.DMA((1,)),
            pltpu.SemaphoreType.DMA((1,)),
            pltpu.SemaphoreType.DMA((n_dp, n_dp)),
            pltpu.SemaphoreType.DMA((n_dp,)),
        ]

    def hop(self):
        return pltpu.make_async_remote_copy(
            src_ref=self.own_ref,
            dst_ref=self.dst.at[self.slot],
            send_sem=self.send_z.at[0],
            recv_sem=self.recv.at[self.slot],
            device_id={"seq": self.target},
            device_id_type=MESH,
        )

    def own(self):
        return pltpu.make_async_copy(self.own_ref, self.dst.at[self.slot], self.own_sem.at[0])

    def over(self, slot, k):
        return pltpu.make_async_remote_copy(
            src_ref=self.dst.at[slot],
            dst_ref=self.dst.at[slot],
            send_sem=self.send_xy.at[slot, k],
            recv_sem=self.recv.at[slot],
            device_id={"dp": lax.rem(self.d + k, self.n_dp)},
            device_id_type=MESH,
        )

    def begin(self):
        stays = self.target == self.line.s
        pl.when(stays)(lambda: self.own().start())
        pl.when(jnp.logical_not(stays))(lambda: self.hop().start())

    def forward(self):
        @pl.when(self.source_d == self.d)
        def _():
            for slot in range(self.n_dp):
                mine = self.source_s + slot == self.line.s
                pl.when(mine)(lambda: self.own().wait())
                pl.when(jnp.logical_not(mine))(lambda: self.over(slot, 1).wait_recv())
                for k in range(1, self.n_dp):
                    self.over(slot, k).start()

    def arrive(self):
        @pl.when(self.source_d != self.d)
        def _():
            for slot in range(self.n_dp):
                self.over(slot, 1).wait_recv()

    def end(self):
        pl.when(self.target != self.line.s)(lambda: self.hop().wait_send())

        @pl.when(self.source_d == self.d)
        def _():
            for slot in range(self.n_dp):
                for k in range(1, self.n_dp):
                    self.over(slot, k).wait_send()


def greet_all(line, n_dp):
    barrier = pltpu.get_barrier_semaphore()
    n_seq = 2 * line.n_line
    d = lax.axis_index("dp")
    for j in range(1, n_seq):
        pl.semaphore_signal(barrier, 1, device_id={"seq": lax.rem(line.s + j, n_seq)}, device_id_type=MESH)
    for k in range(1, n_dp):
        pl.semaphore_signal(barrier, 1, device_id={"dp": lax.rem(d + k, n_dp)}, device_id_type=MESH)
    pl.semaphore_wait(barrier, n_seq + n_dp - 2)


def turn(values, lanes_low):
    half = HEAD_DIM // 2
    width = values.shape[-1]
    return jnp.where(
        lanes_low, pltpu.roll(values, width - half, values.ndim - 1), pltpu.roll(values, half, values.ndim - 1)
    )


def low_lanes(shape):
    return lax.rem(lax.broadcasted_iota(jnp.int32, shape, len(shape) - 1), HEAD_DIM) < HEAD_DIM // 2


def head_lanes(kv, h, q_cols):
    wide = jnp.concatenate([kv] * (q_cols // (2 * HEAD_DIM)), axis=1).astype(F32)
    swapped = pltpu.roll(wide, HEAD_DIM, 1)
    here = lax.div(lax.broadcasted_iota(jnp.int32, wide.shape, 1), HEAD_DIM) == h
    even = lax.rem(h, 2) == 0
    key = jnp.where(here, jnp.where(even, wide, swapped), 0.0).astype(BF16)
    value = jnp.where(here, jnp.where(even, swapped, wide), 0.0).astype(BF16)
    return key, value


def attention_kernel(
    n_seq, n_dp, prefix_ref, tok_ref, cot_ref, cos_ref, sin_ref, qkvb_hbm, gub_hbm, wo_own, wd_own,
    hidden_ref, nmlp_ref, q_ref, kv_ref, mixed_ref, normed_hbm, cot_hbm, wqkv_hbm, wo_hbm, wgu_hbm, wd_hbm,
    full, cot, wqkv, wo, acc, part, sib, rcv, save_sem, *sems,
):
    n = Line(n_seq)
    rows, width = tok_ref.shape
    micro, length, q_cols = q_ref.shape
    span = rows // micro
    cols_all = wqkv.shape[3]
    pair = 2 * rows
    tok = tok_ref[...].astype(F32)
    full[n.s] = (tok * lax.rsqrt(jnp.mean(tok * tok, axis=1, keepdims=True) + EPSILON)).astype(BF16)
    cot[n.s] = cot_ref[...]

    gather = Gather(n, full, *sems[0:3])
    gather_cot = Gather(n, cot, *sems[3:6])
    scatter = Scatter(n, part, sib, rcv, *sems[6:10])
    qkv_w = Spread(n, n_dp, qkvb_hbm, wqkv, *sems[10:14])
    gu_w = Spread(n, n_dp, gub_hbm, wgu_hbm, *sems[14:18])
    out_w = OutRows(n, n_dp, wo_own, wo, *sems[18:22])
    down_w = Copies(n_dp, wd_own, wd_hbm, *sems[22:25])

    greet_all(n, n_dp)
    qkv_w.begin()
    gather.begin()
    out_w.begin()
    qkv_w.forward_own()
    qkv_w.forward(1, n_seq)
    out_w.forward()
    down_w.begin()
    for j in range(n.n_line):
        gather.visit(n.order(j))
    gu_w.begin()
    gu_w.forward_own()
    qkv_w.arrive()

    saves = [
        pltpu.make_async_copy(full, normed_hbm, save_sem.at[0]),
        pltpu.make_async_copy(wqkv, wqkv_hbm, save_sem.at[1]),
    ]
    for save in saves:
        save.start()

    low = low_lanes((span, cols_all))

    @pl.loop(0, n.n_line)
    def _(chip):
        two = pl.ds(pl.multiple_of(2 * chip, 2), 2)
        value = nn(full[two].reshape(pair, width), wqkv[...].reshape(width, cols_all))
        for core in range(2):
            at = pl.ds(pl.multiple_of((2 * chip + core) * span, span), span)
            cos, sin = cos_ref[at, :], sin_ref[at, :]
            for m in range(micro):
                block = value[(core * micro + m) * span : (core * micro + m + 1) * span]
                turned = (block * cos + turn(block, low) * sin).astype(BF16)
                q_ref[m, at, :] = turned[:, :q_cols]
                kv_ref[m, at, :] = turned[:, q_cols:]

    scale = 1.0 / math.sqrt(HEAD_DIM)
    q_tile = min(length, QUERY_TILE)

    @pl.loop(0, micro)
    def _(m):
        prefix = prefix_ref[m]

        @pl.loop(0, q_cols // HEAD_DIM)
        def _(h):
            key, val = head_lanes(kv_ref[m], h, q_cols)

            @pl.loop(0, length // q_tile)
            def _(i):
                at = pl.ds(pl.multiple_of(i * q_tile, q_tile), q_tile)
                scores = nt(q_ref[m, at, :], key) * scale
                query_pos = i * q_tile + lax.broadcasted_iota(jnp.int32, scores.shape, 0)
                key_pos = lax.broadcasted_iota(jnp.int32, scores.shape, 1)
                scores = jnp.where((key_pos <= query_pos) | (key_pos < prefix), scores, NEGATIVE)
                weights = jnp.exp(scores - jnp.max(scores, axis=1, keepdims=True))
                total = jnp.sum(weights, axis=1, keepdims=True)
                mixed = nn((weights / total).astype(BF16), val)

                @pl.when(h == 0)
                def _():
                    acc[at, :] = mixed

                @pl.when(h > 0)
                def _():
                    acc[at, :] += mixed

        mixed_ref[m] = acc[...].astype(BF16)

    out_w.arrive()
    pltpu.make_async_copy(wo, wo_hbm, save_sem.at[2]).start()
    for m in range(micro):

        @pl.loop(0, width // TILE)
        def _(w):
            cols = pl.ds(pl.multiple_of(w * TILE, TILE), TILE)
            value = nn(mixed_ref[m], wo[:, :, cols].reshape(q_cols, TILE))
            part[:, m * span : (m + 1) * span, cols] = value.astype(BF16).reshape(n_seq, span, TILE)

    scatter.begin()
    gather_cot.begin()
    gather_cot.visit(n.l)
    for time in range(n.last):
        scatter.step(time)
        gather_cot.visit(n.order(time + 1))
        first, end = spread_work(n_seq - 1, n.last, time)
        gu_w.forward(first + 1, end + 1)
    pltpu.make_async_copy(cot, cot_hbm, save_sem.at[3]).start()
    scatter.finish(hidden_ref)
    hidden = hidden_ref[...] + tok_ref[...].astype(F32)
    hidden_ref[...] = hidden
    nmlp_ref[...] = (hidden * lax.rsqrt(jnp.mean(hidden * hidden, axis=1, keepdims=True) + EPSILON)).astype(BF16)
    gu_w.arrive()
    down_w.end()
    for save in saves:
        save.wait()
    pltpu.make_async_copy(wo, wo_hbm, save_sem.at[2]).wait()
    pltpu.make_async_copy(cot, cot_hbm, save_sem.at[3]).wait()
    gather.end()
    gather_cot.end()
    qkv_w.end()
    gu_w.end()
    out_w.end()


def attention_call(prefix, tok, cot, cos, sin, qkvb, gub, wo_own, wd_own, n_seq, n_dp):
    rows, width = tok.shape
    micro = prefix.shape[0]
    length = cos.shape[0]
    shard, qkv_cols = qkvb.shape[1:]
    gu_cols = gub.shape[2]
    q_cols = width // n_seq
    ff_block = wd_own.shape[0]
    every = n_seq * rows
    any_spec = pl.BlockSpec(memory_space=pl.ANY)
    vmem = pl.BlockSpec(memory_space=pltpu.VMEM)
    outs = [
        ((rows, width), F32, vmem),
        ((rows, width), BF16, vmem),
        ((micro, length, q_cols), BF16, vmem),
        ((micro, length, 2 * HEAD_DIM), BF16, vmem),
        ((micro, length, q_cols), BF16, vmem),
        ((n_seq, rows, width), BF16, any_spec),
        ((n_seq, rows, width), BF16, any_spec),
        ((n_dp, n_seq, shard, qkv_cols), BF16, any_spec),
        ((n_dp, shard, width), BF16, any_spec),
        ((n_dp, n_seq, shard, gu_cols), BF16, any_spec),
        ((n_dp, ff_block, width), BF16, any_spec),
    ]
    return pl.pallas_call(
        functools.partial(attention_kernel, n_seq, n_dp),
        out_shape=tuple(jax.ShapeDtypeStruct(s, t) for s, t, _ in outs),
        in_specs=[pl.BlockSpec(memory_space=pltpu.SMEM)] + [vmem] * 4 + [any_spec] * 4,
        out_specs=tuple(spec for _, _, spec in outs),
        scratch_shapes=[
            pltpu.VMEM((n_seq, rows, width), BF16),
            pltpu.VMEM((n_seq, rows, width), BF16),
            pltpu.VMEM((n_dp, n_seq, shard, qkv_cols), BF16),
            pltpu.VMEM((n_dp, shard, width), BF16),
            pltpu.VMEM((length, q_cols), F32),
            pltpu.VMEM((n_seq, rows, width), BF16),
            *Scatter.buffers(n_seq, rows, width),
            pltpu.SemaphoreType.DMA((4,)),
            *Gather.sems(n_seq),
            *Gather.sems(n_seq),
            *Scatter.sems(n_seq),
            *Spread.sems(n_seq, n_dp),
            *Spread.sems(n_seq, n_dp),
            *OutRows.sems(n_dp),
            *Copies.sems(n_dp),
        ],
        compiler_params=pltpu.CompilerParams(
            collective_id=2, has_side_effects=True, vmem_limit_bytes=VMEM_LIMIT
        ),
        cost_estimate=pl.CostEstimate(flops=10**10, bytes_accessed=40 << 20, transcendentals=0),
        name="attention",
    )(prefix, tok, cot, cos, sin, qkvb, gub, wo_own, wd_own)


def mlp_kernel(
    n_seq, x_ref, cot_hbm, wgu_hbm, wd_hbm,
    gnm_ref, pout_hbm, dwg_hbm, dwu_hbm, dwd_hbm,
    full, cot, wgu, wd, act, gg, gu, part, sib, rcv, stage_gu, stage_rows, load_sem, gu_sem, rows_sem, *sems,
):
    n = Line(n_seq)
    rows, width = x_ref.shape
    ff = wd.shape[0]
    pair = 2 * rows
    loads = [
        pltpu.make_async_copy(src, dst, load_sem.at[i])
        for i, (src, dst) in enumerate(
            [(wgu_hbm, wgu), (cot_hbm, cot), (wd_hbm, wd)]
        )
    ]
    for load in loads:
        load.start()
    full[n.s] = x_ref[...]
    n.greet()
    gather = Gather(n, full, *sems[:3])
    scatter = Scatter(n, part, sib, rcv, *sems[3:7])
    gather.begin()
    for load in loads:
        load.wait()

    @pl.loop(0, n.n_line)
    def _(j):
        chip = n.order(j)
        gather.visit(chip)
        at = pl.ds(pl.multiple_of(chip * pair, pair), pair)
        two = pl.ds(pl.multiple_of(2 * chip, 2), 2)

        @pl.loop(0, ff // TILE)
        def _(f):
            cols = pl.ds(pl.multiple_of(f * TILE, TILE), TILE)
            x = full[two].reshape(pair, width)
            gate = nn(x, wgu[:, cols])
            up = nn(x, wgu[:, pl.ds(pl.multiple_of(ff + f * TILE, TILE), TILE)])
            grad = nt(cot[two].reshape(pair, width), wd[cols, :])
            sig = jax.nn.sigmoid(gate)
            silu = gate * sig
            act[at, cols] = (silu * up).astype(BF16)
            gg[at, cols] = (grad * up * (sig + silu * (1.0 - sig))).astype(BF16)
            gu[at, cols] = (grad * silu).astype(BF16)

        @pl.loop(0, width // TILE)
        def _(w):
            cols = pl.ds(pl.multiple_of(w * TILE, TILE), TILE)
            value = nt(gg[at, :], wgu[cols, :ff]) + nt(gu[at, :], wgu[cols, ff:])
            part[two, :, cols] = value.astype(BF16).reshape(2, rows, TILE)

    scatter.begin()

    def gate_up_grads(first, end):
        @pl.loop(first, end)
        def _(w):
            slot = lax.rem(w, 2)
            cols = pl.ds(pl.multiple_of(w * TILE, TILE), TILE)
            x = full[:, :, cols].reshape(n_seq * rows, TILE)
            for i, (src, dst) in enumerate([(gg, dwg_hbm), (gu, dwu_hbm)]):
                copy = pltpu.make_async_copy(
                    stage_gu.at[slot, i], dst.at[cols, :], gu_sem.at[slot, i]
                )
                pl.when(w >= 2)(lambda: copy.wait())
                stage_gu[slot, i] = tn(x, src[...]).astype(BF16)
                copy.start()

    def down_grads(first, end):
        @pl.loop(first, end)
        def _(f):
            slot = lax.rem(f, 2)
            cols = pl.ds(pl.multiple_of(f * TILE, TILE), TILE)
            copy = pltpu.make_async_copy(stage_rows.at[slot], dwd_hbm.at[cols, :], rows_sem.at[slot])
            pl.when(f >= 2)(lambda: copy.wait())
            for w in range(0, width, 2 * TILE):
                span = cot[:, :, w : w + 2 * TILE].reshape(n_seq * rows, 2 * TILE)
                stage_rows[slot, :, w : w + 2 * TILE] = tn(act[:, cols], span).astype(BF16)
            copy.start()

    def out_parts(first, end):
        @pl.loop(first, end)
        def _(chip):
            slot = lax.rem(chip, 2)
            at = pl.ds(pl.multiple_of(chip * pair, pair), pair)
            two = pl.ds(pl.multiple_of(2 * chip, 2), 2)
            copies = [
                pltpu.make_async_copy(
                    stage_rows.at[slot, pl.ds(i * rows, rows)], pout_hbm.at[2 * chip + i], rows_sem.at[slot + 2 + 2 * i]
                )
                for i in range(2)
            ]

            @pl.when(chip >= 2)
            def _():
                for copy in copies:
                    copy.wait()

            for w in range(0, width, 2 * TILE):
                stage_rows[slot, :pair, w : w + 2 * TILE] = nn(act[at, :], wd[:, w : w + 2 * TILE]).astype(BF16)
            for copy in copies:
                copy.start()

    def drain_down():
        for slot in range(2):
            pltpu.make_async_copy(stage_rows.at[slot], dwd_hbm.at[pl.ds(0, TILE), :], rows_sem.at[slot]).wait()

    def drain_out():
        for slot in range(2):
            for i in range(2):
                pltpu.make_async_copy(
                    stage_rows.at[slot, pl.ds(i * rows, rows)], pout_hbm.at[i], rows_sem.at[slot + 2 + 2 * i]
                ).wait()

    def drain_gate_up():
        for slot in range(2):
            for i, dst in enumerate([dwg_hbm, dwu_hbm]):
                pltpu.make_async_copy(stage_gu.at[slot, i], dst.at[pl.ds(0, TILE), :], gu_sem.at[slot, i]).wait()

    last = n.last
    for time in range(last):
        scatter.step(time)
        gate_up_grads(*spread_work(width // TILE, last, time))
        if time == last - 2:
            down_grads(0, ff // TILE)
            drain_down()
        if time == last - 1:
            out_parts(0, n.n_line)
            drain_out()
    drain_gate_up()
    scatter.finish(gnm_ref)
    gather.end()


def mlp_call(x, cot, wgu, wd, n_seq):
    rows, width = x.shape
    ff = wd.shape[0]
    every = n_seq * rows
    any_spec = pl.BlockSpec(memory_space=pl.ANY)
    vmem = pl.BlockSpec(memory_space=pltpu.VMEM)
    return pl.pallas_call(
        functools.partial(mlp_kernel, n_seq),
        out_shape=(
            jax.ShapeDtypeStruct((rows, width), F32),
            jax.ShapeDtypeStruct((n_seq, rows, width), BF16),
            jax.ShapeDtypeStruct((width, ff), BF16),
            jax.ShapeDtypeStruct((width, ff), BF16),
            jax.ShapeDtypeStruct((ff, width), BF16),
        ),
        in_specs=[vmem] + [any_spec] * 3,
        out_specs=(vmem,) + (any_spec,) * 4,
        scratch_shapes=[
            pltpu.VMEM((n_seq, rows, width), BF16),
            pltpu.VMEM((n_seq, rows, width), BF16),
            pltpu.VMEM((width, 2 * ff), BF16),
            pltpu.VMEM((ff, width), BF16),
            pltpu.VMEM((every, ff), BF16),
            pltpu.VMEM((every, ff), BF16),
            pltpu.VMEM((every, ff), BF16),
            pltpu.VMEM((n_seq, rows, width), BF16),
            *Scatter.buffers(n_seq, rows, width),
            pltpu.VMEM((2, 2, TILE, ff), BF16),
            pltpu.VMEM((2, TILE, width), BF16),
            pltpu.SemaphoreType.DMA((3,)),
            pltpu.SemaphoreType.DMA((2, 2)),
            pltpu.SemaphoreType.DMA((6,)),
            *Gather.sems(n_seq),
            *Scatter.sems(n_seq),
        ],
        compiler_params=pltpu.CompilerParams(
            collective_id=1, has_side_effects=True, vmem_limit_bytes=VMEM_LIMIT
        ),
        cost_estimate=pl.CostEstimate(flops=18 * every * width * ff, bytes_accessed=40 << 20, transcendentals=0),
        name="mlp",
    )(x, cot, wgu, wd)


def backward_kernel(
    n_seq, prefix_ref, branch_ref, q_ref, kv_ref, mixed_ref, cos_ref, sin_ref, pout_hbm, normed_hbm, wqkv_hbm, wo_hbm,
    ge_ref, sum_ref, dqkv_ref, dwo_ref,
    full, normed, wqkv, wo, gm, acc_q, acc_k, acc_v, gqkv, part, sib, rcv, sib_o, rcv_o, load_sem, *sems,
):
    n = Line(n_seq)
    rows, width = branch_ref.shape
    micro, length, q_cols = q_ref.shape
    span = rows // micro
    pair = 2 * rows
    loads = [
        pltpu.make_async_copy(src, dst, load_sem.at[i])
        for i, (src, dst) in enumerate(
            [(pout_hbm, part), (wo_hbm, wo), (normed_hbm, normed), (wqkv_hbm, wqkv)]
        )
    ]
    for load in loads:
        load.start()
    full[n.s] = branch_ref[...]
    gather = Gather(n, full, *sems[0:3])
    scatter = Scatter(n, part, sib, rcv, *sems[3:7])
    scatter_out = Scatter(n, part, sib_o, rcv_o, *sems[7:11])
    n.greet()
    gather.begin()
    loads[0].wait()
    scatter_out.begin()
    loads[1].wait()

    for j in range(n.n_line):
        chip = n.order(j)
        gather.visit(chip)
        two = pl.ds(pl.multiple_of(2 * chip, 2), 2)
        value = nt(full[two].reshape(pair, width), wo[...].reshape(q_cols, width)).astype(BF16)
        for core in range(2):
            at = pl.ds(pl.multiple_of((2 * chip + core) * span, span), span)
            for m in range(micro):
                gm[m, at, :] = value[(core * micro + m) * span : (core * micro + m + 1) * span]
        if j < n.last:
            scatter_out.step(j)

    scale = 1.0 / math.sqrt(HEAD_DIM)
    q_tile = min(length, QUERY_TILE)
    low = low_lanes((length, q_cols + 2 * HEAD_DIM))
    loads[2].wait()
    loads[3].wait()

    @pl.loop(0, micro)
    def _(m):
        prefix = prefix_ref[m]
        for ref in (acc_q, acc_k, acc_v):
            ref[...] = jnp.zeros_like(ref)

        @pl.loop(0, q_cols // HEAD_DIM)
        def _(h):
            key, val = head_lanes(kv_ref[m], h, q_cols)
            here = lax.div(lax.broadcasted_iota(jnp.int32, (length, q_cols), 1), HEAD_DIM) == h

            @pl.loop(0, length // q_tile)
            def _(i):
                at = pl.ds(pl.multiple_of(i * q_tile, q_tile), q_tile)
                query, grad = q_ref[m, at, :], gm[m, at, :]
                scores = nt(key, query) * scale
                key_pos = lax.broadcasted_iota(jnp.int32, scores.shape, 0)
                query_pos = i * q_tile + lax.broadcasted_iota(jnp.int32, scores.shape, 1)
                scores = jnp.where((key_pos <= query_pos) | (key_pos < prefix), scores, NEGATIVE)
                weights = jnp.exp(scores - jnp.max(scores, axis=0, keepdims=True))
                probs = weights / jnp.sum(weights, axis=0, keepdims=True)
                grad_probs = nt(val, grad)
                delta = jnp.sum(probs * grad_probs, axis=0, keepdims=True)
                grad_scores = (probs * (grad_probs - delta)).astype(BF16)
                acc_q[at, :] += tn(grad_scores, key)
                acc_k[...] += jnp.where(here, nn(grad_scores, query), 0.0)
                acc_v[...] += jnp.where(here, nn(probs.astype(BF16), grad), 0.0)

        def fold(ref):
            total = ref[:, : 2 * HEAD_DIM]
            for w in range(2 * HEAD_DIM, q_cols, 2 * HEAD_DIM):
                total = total + ref[:, w : w + 2 * HEAD_DIM]
            return total + pltpu.roll(total, HEAD_DIM, 1)

        first = lax.broadcasted_iota(jnp.int32, (length, 2 * HEAD_DIM), 1) < HEAD_DIM
        grads = jnp.concatenate([acc_q[...] * scale, jnp.where(first, fold(acc_k) * scale, fold(acc_v))], axis=1)
        gqkv[m] = (grads * cos_ref[...] - turn(grads, low) * sin_ref[...]).astype(BF16)

    scatter_out.finish(sum_ref)
    for m in range(micro):

        @pl.loop(0, width // TILE)
        def _(w):
            at = pl.ds(pl.multiple_of(w * TILE, TILE), TILE)
            value = nt(gqkv[m], wqkv[at, :])
            part[:, m * span : (m + 1) * span, at] = value.astype(BF16).reshape(n_seq, span, TILE)

    scatter.begin()

    def weight_grads(first, end):
        @pl.loop(first, end)
        def _(w):
            cols = pl.ds(pl.multiple_of(w * TILE, TILE), TILE)
            d_out = jnp.zeros((q_cols, TILE), F32)
            d_qkv = jnp.zeros((TILE, q_cols + 2 * HEAD_DIM), F32)
            for m in range(micro):
                mine = slice(m * span, (m + 1) * span)
                d_out = d_out + tn(mixed_ref[m], full[:, mine, cols].reshape(length, TILE))
                d_qkv = d_qkv + tn(normed[:, mine, cols].reshape(length, TILE), gqkv[m])
            dwo_ref[:, cols] = d_out.astype(BF16)
            dqkv_ref[cols, :] = d_qkv.astype(BF16)

    for time in range(n.last):
        scatter.step(time)
        weight_grads(*spread_work(width // TILE, n.last, time))
    scatter.finish(ge_ref)
    gather.end()


def backward_call(prefix, branch, q, kv, mixed, cos, sin, pout, normed, wqkv, wo, n_seq):
    rows, width = branch.shape
    micro, length, q_cols = q.shape
    qkv_cols = q_cols + 2 * HEAD_DIM
    any_spec = pl.BlockSpec(memory_space=pl.ANY)
    vmem = pl.BlockSpec(memory_space=pltpu.VMEM)
    line_rows = pltpu.VMEM((n_seq, rows, width), BF16)
    return pl.pallas_call(
        functools.partial(backward_kernel, n_seq),
        out_shape=(
            jax.ShapeDtypeStruct((rows, width), F32),
            jax.ShapeDtypeStruct((rows, width), F32),
            jax.ShapeDtypeStruct((width, qkv_cols), BF16),
            jax.ShapeDtypeStruct((q_cols, width), BF16),
        ),
        in_specs=[pl.BlockSpec(memory_space=pltpu.SMEM)] + [vmem] * 6 + [any_spec] * 4,
        out_specs=(vmem,) * 4,
        scratch_shapes=[
            line_rows,
            line_rows,
            pltpu.VMEM((width, qkv_cols), BF16),
            pltpu.VMEM(wo.shape, BF16),
            pltpu.VMEM((micro, length, q_cols), BF16),
            pltpu.VMEM((length, q_cols), F32),
            pltpu.VMEM((length, q_cols), F32),
            pltpu.VMEM((length, q_cols), F32),
            pltpu.VMEM((micro, length, qkv_cols), BF16),
            line_rows,
            *Scatter.buffers(n_seq, rows, width),
            *Scatter.buffers(n_seq, rows, width),
            pltpu.SemaphoreType.DMA((4,)),
            *Gather.sems(n_seq),
            *Scatter.sems(n_seq),
            *Scatter.sems(n_seq),
        ],
        compiler_params=pltpu.CompilerParams(
            collective_id=3, has_side_effects=True, vmem_limit_bytes=VMEM_LIMIT
        ),
        cost_estimate=pl.CostEstimate(flops=10**10, bytes_accessed=40 << 20, transcendentals=0),
        name="backward",
    )(prefix, branch, q, kv, mixed, cos, sin, pout, normed, wqkv, wo)


def body(
    tokens, cotangent, prefix_len, attn_gain, w_query, w_key, w_value, w_out, mlp_gain, w_gate, w_up, w_down
):
    n_dp = lax.axis_size("dp")
    n_seq = lax.axis_size("seq")
    both = ("dp", "seq")
    micro, span, width = tokens.shape
    shard = w_query.shape[0]
    ff_block = w_down.shape[0]
    length = span * n_seq
    rows = micro * span
    repeat = n_seq // KV_HEADS
    q_cols = HEADS // n_seq * HEAD_DIM

    gain_attn, gain_mlp = attn_gain.astype(F32), mlp_gain.astype(F32)

    def kv_blocks(w):
        w = w.reshape(shard, KV_HEADS, 1, HEAD_DIM)
        return jnp.broadcast_to(w, (shard, KV_HEADS, repeat, HEAD_DIM)).reshape(shard, n_seq, HEAD_DIM)

    def scaled(blocks, gain):
        return (blocks.astype(F32) * gain[:, None, None]).astype(BF16).transpose(1, 0, 2)

    qkv_blocks = scaled(
        jnp.concatenate([w_query.reshape(shard, n_seq, q_cols), kv_blocks(w_key), kv_blocks(w_value)], axis=2),
        gain_attn,
    )

    def ff_blocks(w):
        w = w.reshape(shard, n_dp, n_seq, ff_block).transpose(0, 2, 1, 3)
        return w.reshape(shard, n_seq, n_dp * ff_block)

    gu_blocks = scaled(jnp.concatenate([ff_blocks(w_gate), ff_blocks(w_up)], axis=2), gain_mlp)

    cos_one, sin_one = rope_table(jnp.arange(length, dtype=jnp.int32), HEAD_DIM)
    half = HEAD_DIM // 2
    sin_one = jnp.concatenate([-sin_one[:, :half], sin_one[:, half:]], axis=1)
    count = q_cols // HEAD_DIM + 1
    cos = jnp.concatenate([jnp.tile(cos_one, (1, count)), jnp.ones((length, HEAD_DIM), F32)], axis=1)
    sin = jnp.concatenate([jnp.tile(sin_one, (1, count)), jnp.zeros((length, HEAD_DIM), F32)], axis=1)

    tok = tokens.reshape(rows, width)
    cot = cotangent.reshape(rows, width)
    hidden, normed_mlp, q, kv, mixed, normed_all, cot_all, wqkv, wo, wgu, wd = attention_call(
        prefix_len, tok, cot, cos, sin, qkv_blocks, gu_blocks, w_out, w_down, n_seq, n_dp
    )
    ge_mlp, out_part, dwg, dwu, dwd = mlp_call(
        normed_mlp, cot_all, wgu.reshape(width, -1), wd.reshape(-1, width), n_seq
    )

    def norm_back(u, ge):
        r = lax.rsqrt(jnp.mean(u * u, axis=1, keepdims=True) + EPSILON)
        return r * ge - u * (r * r * r * jnp.mean(u * ge, axis=1, keepdims=True)), jnp.sum(ge * u * r, axis=0)

    back, gain_mlp_part = norm_back(hidden, ge_mlp)
    grad_hidden = cot.astype(F32) + back
    ge_attn, out_sum, dqkv, dwo = backward_call(
        prefix_len, grad_hidden.astype(BF16), q, kv, mixed, cos, sin, out_part, normed_all,
        wqkv.reshape(width, -1), wo.reshape(-1, width), n_seq,
    )
    block_out = (hidden + out_sum).astype(BF16)
    back, gain_attn_part = norm_back(tok.astype(F32), ge_attn)
    input_grad = grad_hidden + back

    def collect(grad):
        cols = grad.shape[1]
        mine = lax.psum_scatter(grad, "dp", scatter_dimension=0, tiled=True)
        return lax.all_to_all(
            mine.reshape(n_seq, shard, cols), "seq", split_axis=0, concat_axis=0, tiled=True
        ).astype(F32)

    def ff_unblocks(blocks):
        blocks = blocks * gain_mlp[None, :, None]
        blocks = blocks.reshape(n_seq, shard, n_dp, ff_block).transpose(1, 2, 0, 3)
        return blocks.reshape(shard, n_dp * n_seq * ff_block)

    w_gate_grad = ff_unblocks(collect(dwg))
    w_up_grad = ff_unblocks(collect(dwu))
    w_down_grad = lax.psum_scatter(dwd, "dp", scatter_dimension=0, tiled=True).astype(F32)

    s_index = lax.axis_index("seq")
    ratio = n_seq // n_dp
    out_blocks = dwo.reshape(1, n_dp, shard, width)
    slot = lax.broadcasted_iota(jnp.int32, (ratio, 1, 1, 1), 0)
    out_blocks = jnp.where(slot == s_index % ratio, out_blocks, 0).reshape(n_seq, shard, width)
    out_blocks = lax.all_to_all(out_blocks, "seq", split_axis=0, concat_axis=0, tiled=True)
    out_blocks = out_blocks.reshape(n_dp, ratio, shard, width)
    out_blocks = lax.dynamic_index_in_dim(out_blocks, s_index // n_dp, 1, keepdims=False)
    w_out_grad = lax.psum_scatter(
        out_blocks.reshape(n_dp * shard, width), "dp", scatter_dimension=0, tiled=True
    ).astype(F32)

    qkv_grad = collect(dqkv).transpose(1, 0, 2) * gain_attn[:, None, None]
    w_query_grad = qkv_grad[:, :, :q_cols].reshape(shard, -1)

    def kv_grad(values):
        return values.reshape(shard, KV_HEADS, repeat, HEAD_DIM).sum(axis=2).reshape(shard, -1)

    w_key_grad = kv_grad(qkv_grad[:, :, q_cols : q_cols + HEAD_DIM])
    w_value_grad = kv_grad(qkv_grad[:, :, q_cols + HEAD_DIM :])
    gain_parts = jnp.stack([gain_attn_part, gain_mlp_part], axis=1).reshape(n_dp * n_seq, shard, 2)
    gain_grads = lax.all_to_all(gain_parts, both, split_axis=0, concat_axis=0, tiled=True).sum(axis=0)
    return (
        block_out.reshape(micro, span, width),
        input_grad.reshape(micro, span, width),
        gain_grads[:, 0] / gain_attn,
        w_query_grad,
        w_key_grad,
        w_value_grad,
        w_out_grad,
        gain_grads[:, 1] / gain_mlp,
        w_gate_grad,
        w_up_grad,
        w_down_grad,
    )


def solution(mesh):
    rows = P("dp", "seq", None)
    vec = P(("dp", "seq"))
    mat = P(("dp", "seq"), None)
    in_specs = (rows, rows, P("dp"), vec, mat, mat, mat, mat, vec, mat, mat, mat)
    out_specs = (rows, rows, vec, mat, mat, mat, mat, vec, mat, mat, mat)
    return jax.shard_map(body, mesh=mesh, in_specs=in_specs, out_specs=out_specs, check_vma=False)
```

time: 1140 us -> 743 us (0.65)
  waiting for transfers between devices: 704 us -> 168 us
  Pallas kernels: 0 us -> 452 us
  blocking collectives: 171 us -> 27.6 us
  matrix products: 142 us -> 0 us
  local copies, waits for them, and re-layouts: 56.4 us -> 31.4 us
    pallas_call x0 -> x3, Pallas kernels: none -> 452 us  [the longest x1 224 us: attention_call(): pl.pallas_call(functools.partial(attention_kernel, n_seq, n_dp), out_shap...]
    all_gather x9 -> x0, waiting for transfers between devices: 315 us -> none  [the longest x4 163 us: gather_rows(): return lax.all_gather(values, 'seq', axis=0, tiled=True)]
    dot_general x20 -> x0, matrix products: 134 us -> none  [the longest x5 38.8 us: nt(): lax.dot_general(a, b, (((1,), (1,)), ((), ())), preferred_element_type=F32)]
    unnamed x20 -> x5, waiting for transfers between devices: 134 us -> 1.93 us
    all_to_all x3 -> x1, blocking collectives: 100 us -> 11.7 us  [body(): lax.all_to_all(gain_parts, both, split_axis=0, concat_axis=0, tiled=True)]
    reduce_scatter x8 -> x4, waiting for transfers between devices: 165 us -> 101 us  [the longest x1 54.1 us: body(): lax.psum_scatter(dwd, 'dp', scatter_dimension=0, tiled=True).astype(F32)]
    all_gather x1 -> x0, blocking collectives: 39.3 us -> none  [body(): lax.all_gather(jnp.stack([attn_gain, mlp_gain]), both, axis=1, tiled=True)]
    all_to_all x2, waiting for transfers between devices: 26.5 us -> 0.01 us  [collect(): lax.all_to_all(mine.reshape(n_seq, shard, cols), 'seq', split_axis=0, con...]
  transfers between devices with their start and end apart: 22 -> 8, of which waited for: 17 -> 4; matrix products, arithmetic and copies ran while one was open for 16% -> 3% of each run, Pallas kernels for 0% -> 0%
where the time goes in v2:
time: 743 us; the launch traced here: 734 us
  Pallas kernels  452 us (61%)
  waiting for transfers between devices  168 us (23%)
  local copies, waits for them, and re-layouts  31.4 us (4%)
  blocking collectives  27.6 us (4%)
  other arithmetic  26.8 us (4%)
  between operations  14.7 us (2%)
  starting transfers between devices  13.8 us (2%)
    pallas_call x1, Pallas kernels, attention_call(): pl.pallas_call(functools.partial(attention_kernel, n_seq, n_dp), out_shap...  224 us
    pallas_call x1, Pallas kernels, backward_call(): pl.pallas_call(functools.partial(backward_kernel, n_seq), out_shape=(jax....  127 us
    pallas_call x1, Pallas kernels, mlp_call(): pl.pallas_call(functools.partial(mlp_kernel, n_seq), out_shape=(jax.Shape...  100 us
    reduce_scatter x1, waiting for transfers between devices, body(): lax.psum_scatter(dwd, 'dp', scatter_dimension=0, tiled=True).astype(F32)  54.1 us
    all_to_all x1, waiting for transfers between devices, body(): lax.all_to_all(out_blocks, 'seq', split_axis=0, concat_axis=0, tiled=True)  49 us
    reduce_scatter x3, waiting for transfers between devices, collect(): mine = lax.psum_scatter(grad, 'dp', scatter_dimension=0, tiled=True)  47.3 us
    reduce_scatter x1, waiting for transfers between devices, body(): lax.psum_scatter(out_blocks.reshape(n_dp * shard, width), 'dp', scatter_d...  16.1 us
    all_to_all x1, blocking collectives, collect(): lax.all_to_all(mine.reshape(n_seq, shard, cols), 'seq', split_axis=0, con...  15.9 us
  transfers between devices with their start and end apart: 8, of which 4 were waited for; matrix products, arithmetic and copies ran while one was open for 3% of the time, Pallas kernels for 0%

profile of v2, /device:TPU:0, one launch (start us, length us, event | category | flops | bytes accessed | tf_op | source)
XLA Modules:
  0.0 734.3 jit_solution(2470473093659254895)
XLA Ops:
  7.3 0.3 fusion.5
  7.7 1.2 copy.42
  8.9 1.2 copy.43
  10.1 0.3 copy.57
  10.4 0.4 copy.66
  10.8 0.8 reshape.212
  11.6 0.3 copy.58
  11.9 0.4 copy.65
  12.3 0.8 reshape.214
  13.2 0.1 reshape_reshape.6
  13.3 0.1 reshape_reshape.7
  13.5 2.1 concatenate.20.cos_ref
  15.6 0.9 concatenate.22.sin_ref
  16.5 2.0 fusion.gub_hbm
  18.5 0.9 fusion.4.qkvb_hbm
  19.4 224.5 %attention.1 = (f32[128,2048]{1,0:T(8,128)}, bf16[128,2048]{1,0:T(8,128)(2,1)}, bf16[2,512,256]{2,1,0:T(8,128)(2,1)}, bf16[2,512,128]{2,1,0:T(8,128)(2,1)}, bf16...) custom-call(s32[2]{0:T(128)} %prefix_ref.3, ...), custom_call_target="tpu_custom_call" | custom-call | flops 10000000000 | bytes 41943040 | tf_op jit(solution)/shard_map/attention/pallas_call | solution.py:650
  243.9 1.4 multiply_reduce_fusion.3
  245.3 100.0 %mlp.1 = (f32[128,2048]{1,0:T(8,128)}, bf16[8,128,2048]{2,1,0:T(8,128)(2,1)}, bf16[2048,1024]{1,0:T(8,128)(2,1)}, bf16[2048,1024]{1,0:T(8,128)(2,1)}, bf16[1024,2048]{1,0:T(8,128)(2,1)}) custom-call(bf16[128,2048]{1,0:T(8,128)(2,1)} %get-tuple-element.32.x_ref, bf16[8,128,2048]{2,1,0:T(8,128)(2,1)} %get-tuple-element.33.cot_hbm, ...), custom_call_target="tpu_custom_call" | custom-call | flops 38654705664 | bytes 41943040 | tf_op jit(solution)/shard_map/mlp/pallas_call | solution.py:819
  345.3 1.5 multiply_reduce_fusion
  347.0 1.1 fusion.8.branch_ref
  348.0 127.1 %backward.1 = (f32[128,2048]{1,0:T(8,128)}, f32[128,2048]{1,0:T(8,128)}, bf16[2048,384]{1,0:T(8,128)(2,1)}, bf16[256,2048]{1,0:T(8,128)(2,1)}) custom-call(s32[2]{0:T(128)} %prefix_ref.3, bf16[128,2048]{1,0:T(8,128)(2,1)} %fusion.8.branch_ref, bf16[2,512,256]{2,1,0:T(8,128)(2,1)} %get-tuple-element.37.q_ref, bf16[2,512,128]{2,1,0:T(8,128)(2,1)} %get-tuple-element.38.kv_ref, ...), custom_call_target="tpu_custom_call" | custom-call | flops 10000000000 | bytes 41943040 | tf_op jit(solution)/shard_map/backward/pallas_call | solution.py:978
  475.2 0.7 reduce-scatter.10.cloned.1.call-update
  476.0 0.7 reduce-scatter.12.cloned.1.call-update
  476.7 0.1 broadcast_in_dim.41
  476.8 0.1 broadcast_in_dim.42
  476.9 2.7 bitcast_select_fusion
  479.6 4.4 all-to-all-start.2
  484.1 49.0 %all-to-all-done.2 = bf16[8,64,2048]{2,1,0:T(8,128)(2,1)} async-done(((bf16[8,64,2048]{2,1,0:T(8,128)(2,1)}), bf16[8,64,2048]{2,1,0:T(8,128)(2,1)}, u32[]{:S(2)}, u32[]{:S(2)}) %all-to-all-start.2) | async-done | bytes 2097184 | tf_op jit(solution)/shard_map/all_to_all | solution.py:1099
  533.1 2.4 constant_dynamic-slice_fusion
  535.5 0.5 reduce-scatter.14.cloned.1.call-update
  536.1 0.5 copy-done.2
  536.6 0.2 multiply_reduce_fusion.2
  536.8 0.1 rsqrt.27
  536.9 1.9 multiply_reduce_fusion.1
  539.0 0.1 reshape.233
  539.1 11.7 %all_to_all.25 = f32[32,1,128]{2,1,0:T(1,128)S(1)} all-to-all(f32[32,1,128]{2,1,0:T(1,128)S(1)} %reshape.233), channel_id=1, replica_groups=mesh['dp'=4,'seq'=8] {'dp','seq'}, dimensions={0} | all-to-all | bytes 32768 | tf_op jit(solution)/shard_map/all_to_all | solution.py:1115
  550.8 15.9 %all_to_all.26 = bf16[8,64,384]{2,1,0:T(8,128)(2,1)S(1)} all-to-all(bf16[8,64,384]{2,1,0:T(8,128)(2,1)} %bitcast.94), channel_id=1, replica_groups=mesh['dp'=4,'seq'=8] {'seq'}, dimensions={0} | all-to-all | bytes 786432 | tf_op jit(solution)/shard_map/all_to_all | solution.py:1081
  566.7 4.2 all-to-all-start.3
  571.0 47.3 %reduce-scatter.12.cloned.1.call-done = bf16[512,1024]{1,0:T(8,128)(2,1)} async-done(((bf16[2048,1024]{1,0:T(8,128)(2,1)}), bf16[512,1024]{1,0:T(8,128)(2,1)}) %reduce-scatter.12.cloned.1.call-update) | async-done | bytes 1048592 | tf_op jit(solution)/shard_map/reduce_scatter | solution.py:1080
  618.2 4.9 all-to-all-start.4
  623.2 0.7 fusion.7
  623.8 3.1 fusion.2
  627.0 0.5 broadcast.172
  627.5 0.7 reduce.1
  628.2 0.1 reshape.234
  628.3 1.2 bitcast_divide_fusion
  629.5 0.8 multiply_bitcast_fusion
  630.4 0.8 copy.56
  631.2 0.1 fusion.9
  631.3 0.2 copy.51
  631.5 0.8 reshape.223
  632.3 0.2 copy.52
  632.4 0.8 reshape.224
  633.2 16.1 %reduce-scatter.8.cloned.1.call-done = bf16[64,2048]{1,0:T(8,128)(2,1)} async-done(((bf16[256,2048]{1,0:T(8,128)(2,1)}), bf16[64,2048]{1,0:T(8,128)(2,1)}) %reduce-scatter.8.cloned.1.call-update) | async-done | bytes 262160 | tf_op jit(solution)/shard_map/reduce_scatter | solution.py:1102
  649.3 1.8 convert_element_type.76
  651.1 54.1 %reduce-scatter.14.cloned.1.call-done = bf16[256,2048]{1,0:T(8,128)(2,1)} async-done(((bf16[1024,2048]{1,0:T(8,128)(2,1)}), bf16[256,2048]{1,0:T(8,128)(2,1)}) %reduce-scatter.14.cloned.1.call-update) | async-done | bytes 1048592 | tf_op jit(solution)/shard_map/reduce_scatter | solution.py:1092
  705.2 2.8 convert_element_type.79
  708.0 3.6 convert_multiply_fusion
  711.5 3.2 reshape.228
  714.7 2.8 copy.53
  717.5 2.5 copy.59
  720.0 2.0 reshape.231
  722.0 2.8 copy.54
  724.8 2.5 copy.60
  (66 shorter events, 1.0 us)
Async XLA Ops:
  7.2 543.7 %reduce-scatter.6.cloned.1.call-start = ((), (), s32[]{:S(2)}) async-start(), calls=%async_computation.10 | async-start | bytes 1966080 | tf_op jit(solution)/shard_map/reduce_scatter | solution.py:1080
  7.6 2.5 copy-start.17
  7.6 2.5 copy-start.5
  10.1 6.4 copy-start.11
  10.4 1.2 copy-start.6
  11.8 1.2 copy-start.16
  11.9 1.3 copy-start.7
  11.9 1.3 copy-start.8
  11.9 1.5 copy-start.9
  13.1 2.5 copy-start.3
  13.1 5.4 copy-start.13
  245.3 101.6 %copy-start.10 = (f32[128]{0:T(128)}, f32[128]{0:T(128)S(1)}, u32[]{:S(2)}) copy-start(f32[128]{0:T(128)S(1)} %add_rsqrt_fusion.1) | copy-start | bytes 1540
  245.3 100.0 %copy-start = (f32[128,2048]{1,0:T(8,128)S(1)}, f32[128,2048]{1,0:T(8,128)}, u32[]{:S(2)}) copy-start(f32[128,2048]{1,0:T(8,128)} %get-tuple-element.31) | copy-start | bytes 3145732
  345.3 1.6 copy-start.1
  345.3 1.7 copy-start.4
  347.0 128.2 %copy-start.14 = (f32[128]{0:T(128)}, f32[128]{0:T(128)S(1)}, u32[]{:S(2)}) copy-start(f32[128]{0:T(128)S(1)} %fusion.6) | copy-start | bytes 1540
  475.2 91.6 %reduce-scatter.10.cloned.1.call-start = ((), (), s32[]{:S(2)}) async-start(), calls=%async_computation.12 | async-start | bytes 5242880 | tf_op jit(solution)/shard_map/reduce_scatter | solution.py:1080
  475.9 142.3 %reduce-scatter.12.cloned.1.call-start = ((), (), s32[]{:S(2)}) async-start(), calls=%async_computation.13 | async-start | bytes 5242880 | tf_op jit(solution)/shard_map/reduce_scatter | solution.py:1080
  479.6 53.5 %all-to-all-start.2 = ((bf16[8,64,2048]{2,1,0:T(8,128)(2,1)}), bf16[8,64,2048]{2,1,0:T(8,128)(2,1)}, u32[]{:S(2)}, u32[]{:S(2)}) async-start(bf16[8,64,2048]{2,1,0:T(8,128)(2,1)} %bitcast_select_fusion), calls=%async_computation.3 | async-start | bytes 4194304 | tf_op jit(solution)/shard_map/all_to_all | solution.py:1099
  484.0 165.3 %reduce-scatter.8.cloned.1.call-start = ((), (), s32[]{:S(2)}) async-start(), calls=%async_computation.11 | async-start | bytes 1310720 | tf_op jit(solution)/shard_map/reduce_scatter | solution.py:1102
  535.5 169.7 %reduce-scatter.14.cloned.1.call-start = ((), (), s32[]{:S(2)}) async-start(), calls=%async_computation.14 | async-start | bytes 5242880 | tf_op jit(solution)/shard_map/reduce_scatter | solution.py:1092
  535.5 1.0 copy-start.2
  536.9 2.0 copy-start.15
  566.7 51.5 %all-to-all-start.3 = ((bf16[8,64,1024]{2,1,0:T(8,128)(2,1)}), bf16[8,64,1024]{2,1,0:T(8,128)(2,1)}, u32[]{:S(2)}, u32[]{:S(2)}) async-start(bf16[8,64,1024]{2,1,0:T(8,128)(2,1)} %bitcast.90), calls=%async_computation.6 | async-start | bytes 2097152 | tf_op jit(solution)/shard_map/all_to_all | solution.py:1081
  618.2 89.7 %all-to-all-start.4 = ((bf16[8,64,1024]{2,1,0:T(8,128)(2,1)}), bf16[8,64,1024]{2,1,0:T(8,128)(2,1)}, u32[]{:S(2)}, u32[]{:S(2)}) async-start(bf16[8,64,1024]{2,1,0:T(8,128)(2,1)} %bitcast.89), calls=%async_computation.8 | async-start | bytes 2097152 | tf_op jit(solution)/shard_map/all_to_all | solution.py:1081
  632.4 75.5 %copy-start.12 = (f32[64]{0:T(128)S(1)}, f32[64]{0:T(128)}, u32[]{:S(2)}) copy-start(f32[64]{0:T(128)} %copy-done.11) | copy-start | bytes 772
Sparse Core Ops, SparseCore 0:
  475.3 31.2 reduce-scatter.5
  509.5 52.7 reduce-scatter.9
  565.6 52.6 reduce-scatter.11
  621.6 27.6 reduce-scatter.7
  652.4 52.7 reduce-scatter.13

commit v3 on v2

--- a/solution.py
+++ b/solution.py
@@ -63,8 +63,11 @@
         self.has_right = self.l < self.last
         self.has_left = self.l > 0
 
-    def greet(self):
+    def greet(self, n_dp):
         barrier = pltpu.get_barrier_semaphore()
+        d = lax.axis_index("dp")
+        for k in range(1, n_dp):
+            pl.semaphore_signal(barrier, 1, device_id={"dp": lax.rem(d + k, n_dp)}, device_id_type=MESH)
         pl.semaphore_signal(barrier, 1, device_id={"seq": self.sibling}, device_id_type=MESH)
 
         @pl.when(self.has_right)
@@ -75,7 +78,7 @@
         def _():
             pl.semaphore_signal(barrier, 1, device_id={"seq": self.left}, device_id_type=MESH)
 
-        pl.semaphore_wait(barrier, jnp.where(self.has_right & self.has_left, 3, 2))
+        pl.semaphore_wait(barrier, n_dp - 1 + jnp.where(self.has_right & self.has_left, 3, 2))
 
     def order(self, j):
         near = jnp.minimum(self.l, self.last - self.l)
@@ -387,83 +390,274 @@
         pltpu.make_async_copy(self.own_ref, self.dst.at[self.d], self.own_sem.at[0]).wait()
 
 
-class OutRows:
+class Relay:
+    def __init__(self, line, n_dp):
+        n_seq = 2 * line.n_line
+        self.n_dp = n_dp
+        self.d = lax.axis_index("dp")
+        block = self.d * n_seq + line.s
+        self.slot, self.target = lax.rem(block, n_dp), lax.div(block, n_dp)
+        block = line.s * n_dp + self.d
+        self.owner_d, self.owner_s = lax.div(block, n_seq), lax.rem(block, n_seq)
+        self.stays = (self.slot == self.d) & (self.target == line.s)
+        self.moves = jnp.logical_not(self.stays)
+
+    def to_relay(self, src, dst, send, recv):
+        return pltpu.make_async_remote_copy(
+            src_ref=src, dst_ref=dst, send_sem=send, recv_sem=recv,
+            device_id=(self.slot, self.target), device_id_type=MESH,
+        )
+
+    def to_owner(self, src, dst, send, recv):
+        return pltpu.make_async_remote_copy(
+            src_ref=src, dst_ref=dst, send_sem=send, recv_sem=recv,
+            device_id=(self.owner_d, self.owner_s), device_id_type=MESH,
+        )
+
+    def over(self, k, src, dst, send, recv):
+        return pltpu.make_async_remote_copy(
+            src_ref=src, dst_ref=dst, send_sem=send, recv_sem=recv,
+            device_id={"dp": lax.rem(self.d + k, self.n_dp)}, device_id_type=MESH,
+        )
+
+
+class OutRows(Relay):
     def __init__(self, line, n_dp, own, dst, own_sem, send_z, send_xy, recv):
-        self.line, self.n_dp, self.own_ref, self.dst = line, n_dp, own, dst
+        super().__init__(line, n_dp)
+        self.own_ref, self.dst = own, dst
         self.own_sem, self.send_z, self.send_xy, self.recv = own_sem, send_z, send_xy, recv
-        self.n_seq = 2 * line.n_line
-        self.ratio = self.n_seq // n_dp
-        self.d = lax.axis_index("dp")
-        block = self.d * self.n_seq + line.s
-        self.target = lax.div(block, n_dp)
-        self.slot = lax.rem(block, n_dp)
-        self.source_d = lax.div(line.s, self.ratio)
-        self.source_s = lax.rem(line.s, self.ratio) * n_dp
 
     @staticmethod
     def sems(n_dp):
         return [
             pltpu.SemaphoreType.DMA((1,)),
             pltpu.SemaphoreType.DMA((1,)),
-            pltpu.SemaphoreType.DMA((n_dp, n_dp)),
+            pltpu.SemaphoreType.DMA((n_dp,)),
             pltpu.SemaphoreType.DMA((n_dp,)),
         ]
 
     def hop(self):
-        return pltpu.make_async_remote_copy(
-            src_ref=self.own_ref,
-            dst_ref=self.dst.at[self.slot],
-            send_sem=self.send_z.at[0],
-            recv_sem=self.recv.at[self.slot],
-            device_id={"seq": self.target},
-            device_id_type=MESH,
-        )
+        return self.to_relay(self.own_ref, self.dst.at[self.slot], self.send_z.at[0], self.recv.at[self.slot])
 
     def own(self):
         return pltpu.make_async_copy(self.own_ref, self.dst.at[self.slot], self.own_sem.at[0])
 
-    def over(self, slot, k):
+    def copy(self, k):
+        return self.over(k, self.dst.at[self.d], self.dst.at[self.d], self.send_xy.at[k], self.recv.at[self.d])
+
+    def landed(self, slot):
+        return self.over(1, self.dst.at[slot], self.dst.at[slot], self.send_xy.at[1], self.recv.at[slot])
+
+    def begin(self):
+        pl.when(self.stays)(lambda: self.own().start())
+        pl.when(self.moves)(lambda: self.hop().start())
+
+    def forward(self):
+        pl.when(self.stays)(lambda: self.own().wait())
+        pl.when(self.moves)(lambda: self.landed(self.d).wait_recv())
+        for k in range(1, self.n_dp):
+            self.copy(k).start()
+
+    def arrive(self):
+        for k in range(1, self.n_dp):
+            self.landed(lax.rem(self.d + k, self.n_dp)).wait_recv()
+
+    def end(self):
+        pl.when(self.moves)(lambda: self.hop().wait_send())
+        for k in range(1, self.n_dp):
+            self.copy(k).wait_send()
+
+
+class OutSum(Relay):
+    def __init__(self, line, n_dp, src, land, final, own_sem, send_xy, recv_xy, send_z, recv_z):
+        super().__init__(line, n_dp)
+        self.src, self.land, self.final = src, land, final
+        self.own_sem, self.send_xy, self.recv_xy, self.send_z, self.recv_z = own_sem, send_xy, recv_xy, send_z, recv_z
+
+    @staticmethod
+    def sems(n_dp):
+        return [
+            pltpu.SemaphoreType.DMA((1,)),
+            pltpu.SemaphoreType.DMA((n_dp,)),
+            pltpu.SemaphoreType.DMA((n_dp,)),
+            pltpu.SemaphoreType.DMA((1,)),
+            pltpu.SemaphoreType.DMA((1,)),
+        ]
+
+    def copy(self, k):
+        return self.over(
+            k, self.src.at[lax.rem(self.d + k, self.n_dp)], self.land.at[self.d], self.send_xy.at[k], self.recv_xy.at[self.d]
+        )
+
+    def landed(self, owner):
+        return self.over(1, self.land.at[owner], self.land.at[owner], self.send_xy.at[1], self.recv_xy.at[owner])
+
+    def own(self):
+        return pltpu.make_async_copy(self.src.at[self.d], self.land.at[self.d], self.own_sem.at[0])
+
+    def hop(self):
+        return self.to_owner(self.land.at[self.d], self.final, self.send_z.at[0], self.recv_z.at[0])
+
+    def begin(self):
+        self.own().start()
+        for k in range(1, self.n_dp):
+            self.copy(k).start()
+
+    def reduce(self):
+        self.own().wait()
+        for k in range(1, self.n_dp):
+            self.landed(lax.rem(self.d + k, self.n_dp)).wait_recv()
+        total = self.land[0].astype(F32)
+        for owner in range(1, self.n_dp):
+            total = total + self.land[owner].astype(F32)
+        total = total.astype(BF16)
+
+        @pl.when(self.stays)
+        def _():
+            self.final[...] = total
+
+        @pl.when(self.moves)
+        def _():
+            self.land[self.d] = total
+            self.hop().start()
+
+    def end(self):
+        pl.when(self.moves)(lambda: self.hop().wait())
+        for k in range(1, self.n_dp):
+            self.copy(k).wait_send()
+
+
+class Collect:
+    def __init__(self, line, n_dp, src, land, final, own_sem, send_xy, recv_xy, send_z, recv_z):
+        self.line, self.n_dp, self.n_seq = line, n_dp, 2 * line.n_line
+        self.src, self.land, self.final = src, land, final
+        self.own_sem, self.send_xy, self.recv_xy, self.send_z, self.recv_z = own_sem, send_xy, recv_xy, send_z, recv_z
+        self.d = lax.axis_index("dp")
+
+    @staticmethod
+    def sems(n_seq, n_dp):
+        return [
+            pltpu.SemaphoreType.DMA((1,)),
+            pltpu.SemaphoreType.DMA((n_seq, n_dp)),
+            pltpu.SemaphoreType.DMA((n_dp, n_seq)),
+            pltpu.SemaphoreType.DMA((n_seq,)),
+            pltpu.SemaphoreType.DMA((n_seq,)),
+        ]
+
+    def over(self, t, k):
+        peer = lax.rem(self.d + k, self.n_dp)
         return pltpu.make_async_remote_copy(
-            src_ref=self.dst.at[slot],
-            dst_ref=self.dst.at[slot],
-            send_sem=self.send_xy.at[slot, k],
+            src_ref=self.src.at[peer, t],
+            dst_ref=self.land.at[self.d, t],
+            send_sem=self.send_xy.at[t, k],
+            recv_sem=self.recv_xy.at[self.d, t],
+            device_id={"dp": peer},
+            device_id_type=MESH,
+        )
+
+    def landed(self, owner, t):
+        return pltpu.make_async_remote_copy(
+            src_ref=self.land.at[owner, t],
+            dst_ref=self.land.at[owner, t],
+            send_sem=self.send_xy.at[t, 1],
+            recv_sem=self.recv_xy.at[owner, t],
+            device_id={"dp": owner},
+            device_id_type=MESH,
+        )
+
+    def own(self):
+        return pltpu.make_async_copy(self.src.at[self.d], self.land.at[self.d], self.own_sem.at[0])
+
+    def hop(self, t, slot):
+        return pltpu.make_async_remote_copy(
+            src_ref=self.land.at[self.d, t],
+            dst_ref=self.final.at[slot],
+            send_sem=self.send_z.at[t],
+            recv_sem=self.recv_z.at[slot],
+            device_id={"seq": t},
+            device_id_type=MESH,
+        )
+
+    def place(self, j):
+        return lax.rem(self.line.s + 1 + j, self.n_seq)
+
+    def begin(self):
+        self.own().start()
+
+        @pl.loop(0, self.n_seq)
+        def _(j):
+            for k in range(1, self.n_dp):
+                self.over(self.place(j), k).start()
+
+    def reduce(self, first, end):
+        if first == 0:
+            self.own().wait()
+
+        @pl.loop(first, end)
+        def _(j):
+            t = self.place(j)
+            for k in range(1, self.n_dp):
+                self.landed(lax.rem(self.d + k, self.n_dp), t).wait_recv()
+            total = self.land[0, t].astype(F32)
+            for owner in range(1, self.n_dp):
+                total = total + self.land[owner, t].astype(F32)
+            total = total.astype(BF16)
+
+            @pl.when(t == self.line.s)
+            def _():
+                self.final[t] = total
+
+            @pl.when(t != self.line.s)
+            def _():
+                self.land[self.d, t] = total
+                self.hop(t, self.line.s).start()
+
+    def end(self):
+        @pl.loop(0, self.n_seq)
+        def _(t):
+            pl.when(t != self.line.s)(lambda: self.hop(t, t).wait())
+            for k in range(1, self.n_dp):
+                self.over(t, k).wait_send()
+
+
+class RowSum:
+    def __init__(self, n_dp, src, land, own_sem, send, recv):
+        self.n_dp, self.src, self.land = n_dp, src, land
+        self.own_sem, self.send, self.recv = own_sem, send, recv
+        self.d = lax.axis_index("dp")
+
+    sems = Copies.sems
+
+    def copy(self, k, slot):
+        peer = lax.rem(self.d + k, self.n_dp)
+        return pltpu.make_async_remote_copy(
+            src_ref=self.src.at[peer],
+            dst_ref=self.land.at[slot],
+            send_sem=self.send.at[k],
             recv_sem=self.recv.at[slot],
-            device_id={"dp": lax.rem(self.d + k, self.n_dp)},
+            device_id={"dp": peer},
             device_id_type=MESH,
         )
 
+    def own(self):
+        return pltpu.make_async_copy(self.src.at[self.d], self.land.at[self.d], self.own_sem.at[0])
+
     def begin(self):
-        stays = self.target == self.line.s
-        pl.when(stays)(lambda: self.own().start())
-        pl.when(jnp.logical_not(stays))(lambda: self.hop().start())
-
-    def forward(self):
-        @pl.when(self.source_d == self.d)
-        def _():
-            for slot in range(self.n_dp):
-                mine = self.source_s + slot == self.line.s
-                pl.when(mine)(lambda: self.own().wait())
-                pl.when(jnp.logical_not(mine))(lambda: self.over(slot, 1).wait_recv())
-                for k in range(1, self.n_dp):
-                    self.over(slot, k).start()
-
-    def arrive(self):
-        @pl.when(self.source_d != self.d)
-        def _():
-            for slot in range(self.n_dp):
-                self.over(slot, 1).wait_recv()
-
-    def end(self):
-        pl.when(self.target != self.line.s)(lambda: self.hop().wait_send())
-
-        @pl.when(self.source_d == self.d)
-        def _():
-            for slot in range(self.n_dp):
-                for k in range(1, self.n_dp):
-                    self.over(slot, k).wait_send()
-
-
-def greet_all(line, n_dp):
+        self.own().start()
+        for k in range(1, self.n_dp):
+            self.copy(k, self.d).start()
+
+    def finish(self, out):
+        self.own().wait()
+        for k in range(1, self.n_dp):
+            self.copy(k, lax.rem(self.d + k, self.n_dp)).wait()
+        total = self.land[0].astype(F32)
+        for owner in range(1, self.n_dp):
+            total = total + self.land[owner].astype(F32)
+        out[...] = total
+
+
+def greet_all(line, n_dp, relay):
     barrier = pltpu.get_barrier_semaphore()
     n_seq = 2 * line.n_line
     d = lax.axis_index("dp")
@@ -471,7 +665,13 @@
         pl.semaphore_signal(barrier, 1, device_id={"seq": lax.rem(line.s + j, n_seq)}, device_id_type=MESH)
     for k in range(1, n_dp):
         pl.semaphore_signal(barrier, 1, device_id={"dp": lax.rem(d + k, n_dp)}, device_id_type=MESH)
-    pl.semaphore_wait(barrier, n_seq + n_dp - 2)
+
+    @pl.when(relay.moves)
+    def _():
+        for device in ((relay.slot, relay.target), (relay.owner_d, relay.owner_s)):
+            pl.semaphore_signal(barrier, 1, device_id=device, device_id_type=MESH)
+
+    pl.semaphore_wait(barrier, n_seq + n_dp - 2 + jnp.where(relay.moves, 2, 0))
 
 
 def turn(values, lanes_low):
@@ -519,7 +719,7 @@
     out_w = OutRows(n, n_dp, wo_own, wo, *sems[18:22])
     down_w = Copies(n_dp, wd_own, wd_hbm, *sems[22:25])
 
-    greet_all(n, n_dp)
+    greet_all(n, n_dp, out_w)
     qkv_w.begin()
     gather.begin()
     out_w.begin()
@@ -678,9 +878,9 @@
 
 
 def mlp_kernel(
-    n_seq, x_ref, cot_hbm, wgu_hbm, wd_hbm,
-    gnm_ref, pout_hbm, dwg_hbm, dwu_hbm, dwd_hbm,
-    full, cot, wgu, wd, act, gg, gu, part, sib, rcv, stage_gu, stage_rows, load_sem, gu_sem, rows_sem, *sems,
+    n_seq, n_dp, x_ref, cot_hbm, wgu_hbm, wd_hbm,
+    gnm_ref, pout_hbm, dgu_hbm, dwd_ref,
+    full, cot, wgu, wd, act, gg, gu, part, sib, rcv, dwd, land, stage_gu, stage_rows, load_sem, gu_sem, rows_sem, *sems,
 ):
     n = Line(n_seq)
     rows, width = x_ref.shape
@@ -695,9 +895,10 @@
     for load in loads:
         load.start()
     full[n.s] = x_ref[...]
-    n.greet()
+    n.greet(n_dp)
     gather = Gather(n, full, *sems[:3])
     scatter = Scatter(n, part, sib, rcv, *sems[3:7])
+    down = RowSum(n_dp, dwd, land, *sems[7:10])
     gather.begin()
     for load in loads:
         load.wait()
@@ -730,30 +931,29 @@
 
     scatter.begin()
 
+    owners = TILE // dwd.shape[1]
+
+    @pl.loop(0, ff // TILE)
+    def _(f):
+        cols = pl.ds(pl.multiple_of(f * TILE, TILE), TILE)
+        at = pl.ds(f * owners, owners)
+        for w in range(0, width, 2 * TILE):
+            span = cot[:, :, w : w + 2 * TILE].reshape(n_seq * rows, 2 * TILE)
+            value = tn(act[:, cols], span).astype(BF16)
+            dwd[at, :, w : w + 2 * TILE] = value.reshape(owners, dwd.shape[1], 2 * TILE)
+
+    down.begin()
+
     def gate_up_grads(first, end):
         @pl.loop(first, end)
         def _(w):
             slot = lax.rem(w, 2)
             cols = pl.ds(pl.multiple_of(w * TILE, TILE), TILE)
             x = full[:, :, cols].reshape(n_seq * rows, TILE)
-            for i, (src, dst) in enumerate([(gg, dwg_hbm), (gu, dwu_hbm)]):
-                copy = pltpu.make_async_copy(
-                    stage_gu.at[slot, i], dst.at[cols, :], gu_sem.at[slot, i]
-                )
-                pl.when(w >= 2)(lambda: copy.wait())
-                stage_gu[slot, i] = tn(x, src[...]).astype(BF16)
-                copy.start()
-
-    def down_grads(first, end):
-        @pl.loop(first, end)
-        def _(f):
-            slot = lax.rem(f, 2)
-            cols = pl.ds(pl.multiple_of(f * TILE, TILE), TILE)
-            copy = pltpu.make_async_copy(stage_rows.at[slot], dwd_hbm.at[cols, :], rows_sem.at[slot])
-            pl.when(f >= 2)(lambda: copy.wait())
-            for w in range(0, width, 2 * TILE):
-                span = cot[:, :, w : w + 2 * TILE].reshape(n_seq * rows, 2 * TILE)
-                stage_rows[slot, :, w : w + 2 * TILE] = tn(act[:, cols], span).astype(BF16)
+            copy = pltpu.make_async_copy(stage_gu.at[slot], dgu_hbm.at[cols, :], gu_sem.at[slot])
+            pl.when(w >= 2)(lambda: copy.wait())
+            stage_gu[slot, :, :ff] = tn(x, gg[...]).astype(BF16)
+            stage_gu[slot, :, ff:] = tn(x, gu[...]).astype(BF16)
             copy.start()
 
     def out_parts(first, end):
@@ -764,7 +964,7 @@
             two = pl.ds(pl.multiple_of(2 * chip, 2), 2)
             copies = [
                 pltpu.make_async_copy(
-                    stage_rows.at[slot, pl.ds(i * rows, rows)], pout_hbm.at[2 * chip + i], rows_sem.at[slot + 2 + 2 * i]
+                    stage_rows.at[slot, pl.ds(i * rows, rows)], pout_hbm.at[2 * chip + i], rows_sem.at[slot + 2 * i]
                 )
                 for i in range(2)
             ]
@@ -779,54 +979,42 @@
             for copy in copies:
                 copy.start()
 
-    def drain_down():
-        for slot in range(2):
-            pltpu.make_async_copy(stage_rows.at[slot], dwd_hbm.at[pl.ds(0, TILE), :], rows_sem.at[slot]).wait()
-
     def drain_out():
         for slot in range(2):
             for i in range(2):
                 pltpu.make_async_copy(
-                    stage_rows.at[slot, pl.ds(i * rows, rows)], pout_hbm.at[i], rows_sem.at[slot + 2 + 2 * i]
+                    stage_rows.at[slot, pl.ds(i * rows, rows)], pout_hbm.at[i], rows_sem.at[slot + 2 * i]
                 ).wait()
 
-    def drain_gate_up():
-        for slot in range(2):
-            for i, dst in enumerate([dwg_hbm, dwu_hbm]):
-                pltpu.make_async_copy(stage_gu.at[slot, i], dst.at[pl.ds(0, TILE), :], gu_sem.at[slot, i]).wait()
-
-    last = n.last
-    for time in range(last):
+    for time in range(n.last):
         scatter.step(time)
-        gate_up_grads(*spread_work(width // TILE, last, time))
-        if time == last - 2:
-            down_grads(0, ff // TILE)
-            drain_down()
-        if time == last - 1:
+        gate_up_grads(*spread_work(width // TILE, n.last, time))
+        if time == n.last - 1:
             out_parts(0, n.n_line)
             drain_out()
-    drain_gate_up()
+    for slot in range(2):
+        pltpu.make_async_copy(stage_gu.at[slot], dgu_hbm.at[pl.ds(0, TILE), :], gu_sem.at[slot]).wait()
     scatter.finish(gnm_ref)
+    down.finish(dwd_ref)
     gather.end()
 
 
-def mlp_call(x, cot, wgu, wd, n_seq):
+def mlp_call(x, cot, wgu, wd, n_seq, n_dp):
     rows, width = x.shape
     ff = wd.shape[0]
     every = n_seq * rows
     any_spec = pl.BlockSpec(memory_space=pl.ANY)
     vmem = pl.BlockSpec(memory_space=pltpu.VMEM)
     return pl.pallas_call(
-        functools.partial(mlp_kernel, n_seq),
+        functools.partial(mlp_kernel, n_seq, n_dp),
         out_shape=(
             jax.ShapeDtypeStruct((rows, width), F32),
             jax.ShapeDtypeStruct((n_seq, rows, width), BF16),
-            jax.ShapeDtypeStruct((width, ff), BF16),
-            jax.ShapeDtypeStruct((width, ff), BF16),
-            jax.ShapeDtypeStruct((ff, width), BF16),
+            jax.ShapeDtypeStruct((width, 2 * ff), BF16),
+            jax.ShapeDtypeStruct((ff // n_dp, width), F32),
         ),
         in_specs=[vmem] + [any_spec] * 3,
-        out_specs=(vmem,) + (any_spec,) * 4,
+        out_specs=(vmem, any_spec, any_spec, vmem),
         scratch_shapes=[
             pltpu.VMEM((n_seq, rows, width), BF16),
             pltpu.VMEM((n_seq, rows, width), BF16),
@@ -837,13 +1025,16 @@
             pltpu.VMEM((every, ff), BF16),
             pltpu.VMEM((n_seq, rows, width), BF16),
             *Scatter.buffers(n_seq, rows, width),
-            pltpu.VMEM((2, 2, TILE, ff), BF16),
+            pltpu.VMEM((n_dp, ff // n_dp, width), BF16),
+            pltpu.VMEM((n_dp, ff // n_dp, width), BF16),
+            pltpu.VMEM((2, TILE, 2 * ff), BF16),
             pltpu.VMEM((2, TILE, width), BF16),
             pltpu.SemaphoreType.DMA((3,)),
-            pltpu.SemaphoreType.DMA((2, 2)),
-            pltpu.SemaphoreType.DMA((6,)),
+            pltpu.SemaphoreType.DMA((2,)),
+            pltpu.SemaphoreType.DMA((4,)),
             *Gather.sems(n_seq),
             *Scatter.sems(n_seq),
+            *RowSum.sems(n_dp),
         ],
         compiler_params=pltpu.CompilerParams(
             collective_id=1, has_side_effects=True, vmem_limit_bytes=VMEM_LIMIT
@@ -854,9 +1045,11 @@
 
 
 def backward_kernel(
-    n_seq, prefix_ref, branch_ref, q_ref, kv_ref, mixed_ref, cos_ref, sin_ref, pout_hbm, normed_hbm, wqkv_hbm, wo_hbm,
-    ge_ref, sum_ref, dqkv_ref, dwo_ref,
-    full, normed, wqkv, wo, gm, acc_q, acc_k, acc_v, gqkv, part, sib, rcv, sib_o, rcv_o, load_sem, *sems,
+    n_seq, n_dp, prefix_ref, branch_ref, q_ref, kv_ref, mixed_ref, cos_ref, sin_ref, gains_ref,
+    pout_hbm, normed_hbm, wqkv_hbm, wo_hbm, dgu_hbm,
+    ge_ref, sum_ref, dqkv_out, dwo_out, dgate_ref, dup_ref,
+    full, tiles, wqkv, wo, gm, acc_q, acc_k, acc_v, gqkv, part, sib, rcv, sib_o, rcv_o,
+    land_gu, final_gu, dqkv, land_qkv, final_qkv, dwo, land_o, final_o, load_sem, tile_sem, *sems,
 ):
     n = Line(n_seq)
     rows, width = branch_ref.shape
@@ -866,7 +1059,7 @@
     loads = [
         pltpu.make_async_copy(src, dst, load_sem.at[i])
         for i, (src, dst) in enumerate(
-            [(pout_hbm, part), (wo_hbm, wo), (normed_hbm, normed), (wqkv_hbm, wqkv)]
+            [(pout_hbm, part), (wo_hbm, wo), (wqkv_hbm, wqkv)]
         )
     ]
     for load in loads:
@@ -875,11 +1068,16 @@
     gather = Gather(n, full, *sems[0:3])
     scatter = Scatter(n, part, sib, rcv, *sems[3:7])
     scatter_out = Scatter(n, part, sib_o, rcv_o, *sems[7:11])
-    n.greet()
+    gu_sum = Collect(n, n_dp, dgu_hbm, land_gu, final_gu, *sems[11:16])
+    qkv_sum = Collect(n, n_dp, dqkv, land_qkv, final_qkv, *sems[16:21])
+    out_sum = OutSum(n, n_dp, dwo, land_o, final_o, *sems[21:26])
+    greet_all(n, n_dp, out_sum)
     gather.begin()
     loads[0].wait()
     scatter_out.begin()
+    gu_sum.begin()
     loads[1].wait()
+    early = n_seq // 2
 
     for j in range(n.n_line):
         chip = n.order(j)
@@ -892,12 +1090,13 @@
                 gm[m, at, :] = value[(core * micro + m) * span : (core * micro + m + 1) * span]
         if j < n.last:
             scatter_out.step(j)
+        if j > 0:
+            gu_sum.reduce(*spread_work(early, n.last, j - 1))
 
     scale = 1.0 / math.sqrt(HEAD_DIM)
     q_tile = min(length, QUERY_TILE)
     low = low_lanes((length, q_cols + 2 * HEAD_DIM))
     loads[2].wait()
-    loads[3].wait()
 
     @pl.loop(0, micro)
     def _(m):
@@ -948,46 +1147,87 @@
 
     scatter.begin()
 
-    def weight_grads(first, end):
-        @pl.loop(first, end)
-        def _(w):
-            cols = pl.ds(pl.multiple_of(w * TILE, TILE), TILE)
-            d_out = jnp.zeros((q_cols, TILE), F32)
-            d_qkv = jnp.zeros((TILE, q_cols + 2 * HEAD_DIM), F32)
-            for m in range(micro):
-                mine = slice(m * span, (m + 1) * span)
-                d_out = d_out + tn(mixed_ref[m], full[:, mine, cols].reshape(length, TILE))
-                d_qkv = d_qkv + tn(normed[:, mine, cols].reshape(length, TILE), gqkv[m])
-            dwo_ref[:, cols] = d_out.astype(BF16)
-            dqkv_ref[cols, :] = d_qkv.astype(BF16)
-
+    shard = dwo.shape[1]
+
+    @pl.loop(0, width // TILE)
+    def _(w):
+        cols = pl.ds(pl.multiple_of(w * TILE, TILE), TILE)
+        d_out = jnp.zeros((q_cols, TILE), F32)
+        for m in range(micro):
+            d_out = d_out + tn(mixed_ref[m], full[:, m * span : (m + 1) * span, cols].reshape(length, TILE))
+        dwo[:, :, cols] = d_out.astype(BF16).reshape(n_dp, shard, TILE)
+
+    out_sum.begin()
+
+    half = n_seq // 2
+    depth = half * shard
+
+    def fetch(w):
+        cols = pl.ds(pl.multiple_of(w * depth, depth), depth)
+        slot = lax.rem(w, 2)
+        return pltpu.make_async_copy(normed_hbm.at[:, :, cols], tiles.at[slot], tile_sem.at[slot])
+
+    fetch(jnp.int32(0)).start()
+
+    @pl.loop(0, n_dp * 2)
+    def _(w):
+        pl.when(w + 1 < n_dp * 2)(lambda: fetch(w + 1).start())
+        fetch(w).wait()
+        slot = lax.rem(w, 2)
+        d_qkv = jnp.zeros((depth, q_cols + 2 * HEAD_DIM), F32)
+        for m in range(micro):
+            d_qkv = d_qkv + tn(tiles[slot, :, m * span : (m + 1) * span, :].reshape(length, depth), gqkv[m])
+        at = pl.ds(pl.multiple_of(lax.rem(w, 2) * half, half), half)
+        dqkv[lax.div(w, 2), at] = d_qkv.astype(BF16).reshape(half, shard, q_cols + 2 * HEAD_DIM)
+
+    qkv_sum.begin()
     for time in range(n.last):
         scatter.step(time)
-        weight_grads(*spread_work(width // TILE, n.last, time))
+        first, end = spread_work(n_seq - early, n.last, time)
+        gu_sum.reduce(early + first, early + end)
+    out_sum.reduce()
+    qkv_sum.reduce(0, n_seq)
     scatter.finish(ge_ref)
+    gu_sum.end()
+    ff_block = dgate_ref.shape[1] // (n_dp * n_seq)
+    gain = gains_ref[:, 2 * HEAD_DIM : 2 * HEAD_DIM + 1]
+    for t in range(n_seq):
+        for i, ref in enumerate((dgate_ref, dup_ref)):
+            for owner in range(n_dp):
+                cols = slice((owner * n_seq + t) * ff_block, (owner * n_seq + t + 1) * ff_block)
+                first = (i * n_dp + owner) * ff_block
+                ref[:, cols] = final_gu[t, :, first : first + ff_block].astype(F32) * gain
+    qkv_sum.end()
+    dqkv_out[...] = final_qkv[...].astype(F32) * gains_ref[:, :1][None]
+    out_sum.end()
+    dwo_out[...] = final_o[...].astype(F32)
     gather.end()
 
 
-def backward_call(prefix, branch, q, kv, mixed, cos, sin, pout, normed, wqkv, wo, n_seq):
+def backward_call(prefix, branch, q, kv, mixed, cos, sin, gains, pout, normed, wqkv, wo, dgu):
     rows, width = branch.shape
+    n_dp, n_seq, shard, gu_cols = dgu.shape
+    ff = gu_cols // 2 * n_seq
     micro, length, q_cols = q.shape
     qkv_cols = q_cols + 2 * HEAD_DIM
     any_spec = pl.BlockSpec(memory_space=pl.ANY)
     vmem = pl.BlockSpec(memory_space=pltpu.VMEM)
     line_rows = pltpu.VMEM((n_seq, rows, width), BF16)
     return pl.pallas_call(
-        functools.partial(backward_kernel, n_seq),
+        functools.partial(backward_kernel, n_seq, n_dp),
         out_shape=(
             jax.ShapeDtypeStruct((rows, width), F32),
             jax.ShapeDtypeStruct((rows, width), F32),
-            jax.ShapeDtypeStruct((width, qkv_cols), BF16),
-            jax.ShapeDtypeStruct((q_cols, width), BF16),
+            jax.ShapeDtypeStruct((n_seq, shard, qkv_cols), F32),
+            jax.ShapeDtypeStruct((shard, width), F32),
+            jax.ShapeDtypeStruct((shard, ff), F32),
+            jax.ShapeDtypeStruct((shard, ff), F32),
         ),
-        in_specs=[pl.BlockSpec(memory_space=pltpu.SMEM)] + [vmem] * 6 + [any_spec] * 4,
-        out_specs=(vmem,) * 4,
+        in_specs=[pl.BlockSpec(memory_space=pltpu.SMEM)] + [vmem] * 7 + [any_spec] * 5,
+        out_specs=(vmem,) * 6,
         scratch_shapes=[
             line_rows,
-            line_rows,
+            pltpu.VMEM((2, n_seq, rows, n_seq // 2 * shard), BF16),
             pltpu.VMEM((width, qkv_cols), BF16),
             pltpu.VMEM(wo.shape, BF16),
             pltpu.VMEM((micro, length, q_cols), BF16),
@@ -998,17 +1238,29 @@
             line_rows,
             *Scatter.buffers(n_seq, rows, width),
             *Scatter.buffers(n_seq, rows, width),
-            pltpu.SemaphoreType.DMA((4,)),
+            pltpu.VMEM((n_dp, n_seq, shard, gu_cols), BF16),
+            pltpu.VMEM((n_seq, shard, gu_cols), BF16),
+            pltpu.VMEM((n_dp, n_seq, shard, qkv_cols), BF16),
+            pltpu.VMEM((n_dp, n_seq, shard, qkv_cols), BF16),
+            pltpu.VMEM((n_seq, shard, qkv_cols), BF16),
+            pltpu.VMEM((n_dp, shard, width), BF16),
+            pltpu.VMEM((n_dp, shard, width), BF16),
+            pltpu.VMEM((shard, width), BF16),
+            pltpu.SemaphoreType.DMA((3,)),
+            pltpu.SemaphoreType.DMA((2,)),
             *Gather.sems(n_seq),
             *Scatter.sems(n_seq),
             *Scatter.sems(n_seq),
+            *Collect.sems(n_seq, n_dp),
+            *Collect.sems(n_seq, n_dp),
+            *OutSum.sems(n_dp),
         ],
         compiler_params=pltpu.CompilerParams(
             collective_id=3, has_side_effects=True, vmem_limit_bytes=VMEM_LIMIT
         ),
         cost_estimate=pl.CostEstimate(flops=10**10, bytes_accessed=40 << 20, transcendentals=0),
         name="backward",
-    )(prefix, branch, q, kv, mixed, cos, sin, pout, normed, wqkv, wo)
+    )(prefix, branch, q, kv, mixed, cos, sin, gains, pout, normed, wqkv, wo, dgu)
 
 
 def body(
@@ -1057,8 +1309,8 @@
     hidden, normed_mlp, q, kv, mixed, normed_all, cot_all, wqkv, wo, wgu, wd = attention_call(
         prefix_len, tok, cot, cos, sin, qkv_blocks, gu_blocks, w_out, w_down, n_seq, n_dp
     )
-    ge_mlp, out_part, dwg, dwu, dwd = mlp_call(
-        normed_mlp, cot_all, wgu.reshape(width, -1), wd.reshape(-1, width), n_seq
+    ge_mlp, out_part, dgu, w_down_grad = mlp_call(
+        normed_mlp, cot_all, wgu.reshape(width, -1), wd.reshape(-1, width), n_seq, n_dp
     )
 
     def norm_back(u, ge):
@@ -1067,43 +1319,18 @@
 
     back, gain_mlp_part = norm_back(hidden, ge_mlp)
     grad_hidden = cot.astype(F32) + back
-    ge_attn, out_sum, dqkv, dwo = backward_call(
-        prefix_len, grad_hidden.astype(BF16), q, kv, mixed, cos, sin, out_part, normed_all,
-        wqkv.reshape(width, -1), wo.reshape(-1, width), n_seq,
+    gains = jnp.concatenate(
+        [jnp.broadcast_to(g[:, None], (shard, 2 * HEAD_DIM)) for g in (gain_attn, gain_mlp)], axis=1
+    )
+    ge_attn, out_sum, qkv_grad, w_out_grad, w_gate_grad, w_up_grad = backward_call(
+        prefix_len, grad_hidden.astype(BF16), q, kv, mixed, cos, sin, gains, out_part, normed_all,
+        wqkv.reshape(width, -1), wo.reshape(-1, width), dgu.reshape(n_dp, n_seq, shard, -1),
     )
     block_out = (hidden + out_sum).astype(BF16)
     back, gain_attn_part = norm_back(tok.astype(F32), ge_attn)
     input_grad = grad_hidden + back
 
-    def collect(grad):
-        cols = grad.shape[1]
-        mine = lax.psum_scatter(grad, "dp", scatter_dimension=0, tiled=True)
-        return lax.all_to_all(
-            mine.reshape(n_seq, shard, cols), "seq", split_axis=0, concat_axis=0, tiled=True
-        ).astype(F32)
-
-    def ff_unblocks(blocks):
-        blocks = blocks * gain_mlp[None, :, None]
-        blocks = blocks.reshape(n_seq, shard, n_dp, ff_block).transpose(1, 2, 0, 3)
-        return blocks.reshape(shard, n_dp * n_seq * ff_block)
-
-    w_gate_grad = ff_unblocks(collect(dwg))
-    w_up_grad = ff_unblocks(collect(dwu))
-    w_down_grad = lax.psum_scatter(dwd, "dp", scatter_dimension=0, tiled=True).astype(F32)
-
-    s_index = lax.axis_index("seq")
-    ratio = n_seq // n_dp
-    out_blocks = dwo.reshape(1, n_dp, shard, width)
-    slot = lax.broadcasted_iota(jnp.int32, (ratio, 1, 1, 1), 0)
-    out_blocks = jnp.where(slot == s_index % ratio, out_blocks, 0).reshape(n_seq, shard, width)
-    out_blocks = lax.all_to_all(out_blocks, "seq", split_axis=0, concat_axis=0, tiled=True)
-    out_blocks = out_blocks.reshape(n_dp, ratio, shard, width)
-    out_blocks = lax.dynamic_index_in_dim(out_blocks, s_index // n_dp, 1, keepdims=False)
-    w_out_grad = lax.psum_scatter(
-        out_blocks.reshape(n_dp * shard, width), "dp", scatter_dimension=0, tiled=True
-    ).astype(F32)
-
-    qkv_grad = collect(dqkv).transpose(1, 0, 2) * gain_attn[:, None, None]
+    qkv_grad = qkv_grad.transpose(1, 0, 2)
     w_query_grad = qkv_grad[:, :, :q_cols].reshape(shard, -1)
 
     def kv_grad(values):

time: 743 us -> 577 us (0.78); the launches traced: 734 us -> 576 us
  waiting for transfers between devices: 168 us -> 0.01 us
  Pallas kernels: 452 us -> 518 us
  blocking collectives: 27.6 us -> 0 us
  between operations: 14.7 us -> 0.96 us
  other arithmetic: 26.8 us -> 15 us
    reduce_scatter x5 -> x0, waiting for transfers between devices: 117 us -> none  [the longest x1 54.1 us: body(): lax.psum_scatter(dwd, 'dp', scatter_dimension=0, tiled=True).astype(F32)]
    pallas_call x2, Pallas kernels: 227 us -> 296 us  [the longest x1 176 us: backward_call(): pl.pallas_call(functools.partial(backward_kernel, n_seq, n_dp), out_shape...]
    all_to_all x3 -> x1, waiting for transfers between devices: 49 us -> 0.01 us  [body(): lax.all_to_all(gain_parts, both, split_axis=0, concat_axis=0, tiled=True)]
    all_to_all x2 -> x0, blocking collectives: 27.6 us -> none  [the longest x1 15.9 us: collect(): lax.all_to_all(mine.reshape(n_seq, shard, cols), 'seq', split_axis=0, con...]
    reshape x4 -> x0, local copies, waits for them, and re-layouts: 10.7 us -> none  [ff_unblocks(): blocks = blocks.reshape(n_seq, shard, n_dp, ff_block).transpose(1, 2, 0, 3)]
  transfers between devices with their start and end apart: 8 -> 1, of which waited for: 4 -> 0; matrix products, arithmetic and copies ran while one was open for 3% -> 1% of each run, Pallas kernels for 0% -> 0%
where the time goes in v3:
time: 577 us; the launch traced here: 576 us
  Pallas kernels  518 us (90%)
  local copies, waits for them, and re-layouts  29 us (5%)
  other arithmetic  15 us (3%)
  starting transfers between devices  12.8 us (2%)
    pallas_call x1, Pallas kernels, attention_call(): pl.pallas_call(functools.partial(attention_kernel, n_seq, n_dp), out_shap...  222 us
    pallas_call x1, Pallas kernels, backward_call(): pl.pallas_call(functools.partial(backward_kernel, n_seq, n_dp), out_shape...  176 us
    pallas_call x1, Pallas kernels, mlp_call(): pl.pallas_call(functools.partial(mlp_kernel, n_seq, n_dp), out_shape=(jax...  119 us
    all_to_all x1, starting transfers between devices, body(): lax.all_to_all(gain_parts, both, split_axis=0, concat_axis=0, tiled=True)  12.8 us
  transfers between devices with their start and end apart: 1, of which 0 were waited for; matrix products, arithmetic and copies ran while one was open for 1% of the time, Pallas kernels for 0%

profile of v3, /device:TPU:0, one launch (start us, length us, event | category | flops | bytes accessed | tf_op | source)
XLA Modules:
  0.0 575.9 jit_solution(14812452069268625208)
XLA Ops:
  0.6 0.0 copy-start.9
  0.7 0.3 fusion.5
  1.0 0.1 tile.8
  1.1 0.3 copy.35
  1.4 0.1 tile.20
  1.5 1.2 copy.36
  2.6 0.0 copy-done.9
  2.6 0.3 copy.48
  2.9 0.4 copy.55
  3.3 0.0 copy-start.13
  3.3 0.0 copy-start.11
  3.3 0.8 reshape.178
  4.1 0.0 copy-start.12
  4.1 0.0 copy-start.2
  4.1 1.5 copy.49
  5.7 1.4 copy.54
  7.0 1.8 reshape.180
  8.8 0.0 copy-done.13
  8.9 1.7 copy.56
  10.5 0.0 copy-done.11
  10.5 0.8 reshape_reshape.6
  11.3 0.9 copy.38
  12.2 1.6 reshape_reshape.7
  13.9 1.0 copy.39
  14.9 0.0 copy-done.12
  14.9 0.2 multiply_reduce_fusion.2
  15.1 0.9 concatenate.23.cos_ref
  16.0 2.1 concatenate.25.sin_ref
  18.1 2.0 fusion.gub_hbm
  20.0 0.9 fusion.4.qkvb_hbm
  21.0 222.5 %attention.1 = (f32[128,2048]{1,0:T(8,128)}, bf16[128,2048]{1,0:T(8,128)(2,1)}, bf16[2,512,256]{2,1,0:T(8,128)(2,1)}, bf16[2,512,128]{2,1,0:T(8,128)(2,1)}, bf16...) custom-call(s32[2]{0:T(128)} %prefix_ref.3, ...), custom_call_target="tpu_custom_call" | custom-call | flops 10000000000 | bytes 41943040 | tf_op jit(solution)/shard_map/attention/pallas_call | solution.py:850
  243.5 1.4 multiply_reduce_fusion.3
  244.9 0.0 copy-start.6
  244.9 119.2 %mlp.1 = (f32[128,2048]{1,0:T(8,128)}, bf16[8,128,2048]{2,1,0:T(8,128)(2,1)}, bf16[2048,2048]{1,0:T(8,128)(2,1)}, f32[256,2048]{1,0:T(8,128)}) custom-call(bf16[128,2048]{1,0:T(8,128)(2,1)} %get-tuple-element.33.x_ref, bf16[8,128,2048]{2,1,0:T(8,128)(2,1)} %get-tuple-element.34.cot_hbm, bf16[2048,2048]{1,0:T(8,128)(2,1)} %bitcast.75, bf16[1024,2048]{1,0:T(8,128)(2,1)} %bitcast.76), custom_call_target="tpu_custom_call" | custom-call | flops 38654705664 | bytes 41943040 | tf_op jit(solution)/shard_map/mlp/pallas_call | solution.py:1008
  364.1 1.4 multiply_reduce_fusion
  365.5 2.3 fusion.8.branch_ref
  367.8 0.1 rsqrt.27
  367.9 0.1 broadcast_in_dim.4
  368.0 0.1 broadcast_in_dim.5
  368.1 0.6 pad_maximum_fusion.2.gains_ref
  368.7 176.4 %backward.1 = (f32[128,2048]{1,0:T(8,128)}, f32[128,2048]{1,0:T(8,128)}, f32[8,64,384]{2,1,0:T(8,128)}, f32[64,2048]{1,0:T(8,128)}, f32[64,8192]{1,0:T(8,128)}, /*index=5*/f32[64,8192]{1,0:T(8,128)}) custom-call(s32[2]{0:T(128)} %prefix_ref.3, bf16[128,2048]{1,0:T(8,128)(2,1)} %fusion.8.branch_ref, bf16[2,512,256]{2,1,0:T(8,128)(2,1)} %get-tuple-element.38.q_ref, ...), custom_call_target="tpu_custom_call" | custom-call | flops 10000000000 | bytes 41943040 | tf_op jit(solution)/shard_map/backward/pallas_call | solution.py:1216
  545.1 0.0 copy-done.3
  545.1 1.4 multiply_reduce_fusion.1
  546.5 0.1 stack.9
  546.6 0.1 stack.10
  546.7 0.7 reshape.191
  547.4 12.8 %all-to-all-start = ((f32[32,1,128]{2,1,0:T(1,128)}), f32[32,1,128]{2,1,0:T(1,128)S(1)}, u32[]{:S(2)}, u32[]{:S(2)}) async-start(f32[32,1,128]{2,1,0:T(1,128)} %reshape.191), calls=%async_computation | async-start | bytes 32768 | tf_op jit(solution)/shard_map/all_to_all | solution.py:1342
  560.3 1.1 slice_bitcast_fusion
  561.4 3.1 fusion.2
  564.5 0.1 fusion.9
  564.7 0.8 copy.47
  565.5 0.2 copy.44
  565.7 0.8 reshape.189
  566.4 0.2 copy.45
  566.6 0.8 reshape.190
  567.4 0.0 all-to-all-done
  567.4 0.5 broadcast.161
  567.9 0.7 reduce.1
  568.6 0.1 reshape.192
  568.7 0.5 bitcast_divide_fusion
  569.2 0.8 copy.62
  570.0 3.2 copy.63
  573.3 1.3 copy.64
  574.6 1.3 copy.65
  (29 shorter events, 0.2 us)
Async XLA Ops:
  0.6 2.0 copy-start.9
  3.3 5.5 copy-start.13
  3.3 7.2 %copy-start.11 = (bf16[64,512]{1,0:T(8,128)(2,1)S(1)}, bf16[64,512]{1,0:T(8,128)(2,1)}, u32[]{:S(2)}) copy-start(bf16[64,512]{1,0:T(8,128)(2,1)} %param.17) | copy-start | bytes 196612
  4.1 10.8 %copy-start.12 = (bf16[64]{0:T(256)(128)(2,1)S(1)}, bf16[64]{0:T(256)(128)(2,1)}, u32[]{:S(2)}) copy-start(bf16[64]{0:T(256)(128)(2,1)} %param.15) | copy-start | bytes 388
  4.1 10.8 %copy-start.2 = (bf16[2,64,2048]{2,1,0:T(8,128)(2,1)S(1)}, bf16[2,64,2048]{2,1,0:T(8,128)(2,1)}, u32[]{:S(2)}) copy-start(bf16[2,64,2048]{2,1,0:T(8,128)(2,1)} %param.12) | copy-start | bytes 1572868
  13.9 6.2 %copy-start.8 = (bf16[8,8,8,256]{3,2,0,1:T(8,128)(2,1)S(1)}, bf16[8,8,8,256]{3,2,0,1:T(8,128)(2,1)}, u32[]{:S(2)}) copy-start(bf16[8,8,8,256]{3,2,0,1:T(8,128)(2,1)} %copy.56) | copy-start | bytes 786436
  244.9 119.2 %copy-start = (f32[128,2048]{1,0:T(8,128)S(1)}, f32[128,2048]{1,0:T(8,128)}, u32[]{:S(2)}) copy-start(f32[128,2048]{1,0:T(8,128)} %get-tuple-element.32) | copy-start | bytes 3145732
  244.9 120.7 %copy-start.6 = (bf16[2,64,2048]{2,1,0:T(8,128)(2,1)S(1)}, bf16[2,64,2048]{2,1,0:T(8,128)(2,1)}, u32[]{:S(2)}) copy-start(bf16[2,64,2048]{2,1,0:T(8,128)(2,1)} %param.13) | copy-start | bytes 1572868
  368.7 176.4 %copy-start.3 = (bf16[2,64,2048]{2,1,0:T(8,128)(2,1)S(1)}, bf16[2,64,2048]{2,1,0:T(8,128)(2,1)}, u32[]{:S(2)}) copy-start(bf16[2,64,2048]{2,1,0:T(8,128)(2,1)} %param.12) | copy-start | bytes 1572868
  368.7 192.7 %copy-start.1 = (f32[128,2048]{1,0:T(8,128)S(1)}, f32[128,2048]{1,0:T(8,128)}, u32[]{:S(2)}) copy-start(f32[128,2048]{1,0:T(8,128)} %get-tuple-element.37) | copy-start | bytes 3145732
  547.4 20.0 %all-to-all-start = ((f32[32,1,128]{2,1,0:T(1,128)}), f32[32,1,128]{2,1,0:T(1,128)S(1)}, u32[]{:S(2)}, u32[]{:S(2)}) async-start(f32[32,1,128]{2,1,0:T(1,128)} %reshape.191), calls=%async_computation | async-start | bytes 32768 | tf_op jit(solution)/shard_map/all_to_all | solution.py:1342
  560.2 4.3 copy-start.7
  564.5 4.7 copy-start.10
  564.7 8.6 %copy-start.5 = (f32[64,8192]{1,0:T(8,128)S(1)}, f32[64,8192]{1,0:T(8,128)}, u32[]{:S(2)}) copy-start(f32[64,8192]{1,0:T(8,128)} %get-tuple-element.88) | copy-start | bytes 6291460
  570.0 4.5 copy-start.4

commit v4 on v3

--- a/solution.py
+++ b/solution.py
@@ -3,6 +3,7 @@
 
 import jax
 import jax.numpy as jnp
+import numpy as np
 from jax import lax
 from jax.experimental import pallas as pl
 from jax.experimental.pallas import tpu as pltpu
@@ -19,23 +20,28 @@
 MESH = pl.DeviceIdType.MESH
 TILE = 256
 QUERY_TILE = 256
-VMEM_LIMIT = 60 << 20
-
-
-def rope_table(positions, head_size):
-    half_size = head_size // 2
-    index_half = jnp.arange(half_size, dtype=jnp.float32)
-    inverse = jnp.power(THETA, -2.0 * index_half / head_size)
-    wavelength = 2.0 * math.pi / inverse
-    smooth = (8192.0 / wavelength - 1.0) / 3.0
-    blended = (1.0 - smooth) * inverse / 32.0 + smooth * inverse
-    inverse = jnp.where(
-        wavelength < 2048.0, inverse, jnp.where(wavelength > 8192.0, inverse / 32.0, blended)
-    )
-    angles = positions.astype(jnp.float32)[:, None] * inverse[None, :]
-    cos_table = jnp.concatenate([jnp.cos(angles), jnp.cos(angles)], axis=1)
-    sin_table = jnp.concatenate([jnp.sin(angles), jnp.sin(angles)], axis=1)
-    return (cos_table, sin_table)
+AHEAD = 4
+VMEM_LIMIT = 61 << 20
+
+
+def rope_tables(length, q_cols):
+    half = HEAD_DIM // 2
+    f32 = np.float32
+    index_half = np.arange(half, dtype=f32)
+    inverse = np.power(f32(THETA), f32(-2.0) * index_half / f32(HEAD_DIM)).astype(f32)
+    wavelength = (f32(2.0 * math.pi) / inverse).astype(f32)
+    smooth = ((f32(8192.0) / wavelength - f32(1.0)) / f32(3.0)).astype(f32)
+    blended = ((f32(1.0) - smooth) * inverse / f32(32.0) + smooth * inverse).astype(f32)
+    inverse = np.where(
+        wavelength < 2048.0, inverse, np.where(wavelength > 8192.0, inverse / f32(32.0), blended)
+    ).astype(f32)
+    angles = (np.arange(length, dtype=f32)[:, None] * inverse[None, :]).astype(f32)
+    cos, sin = np.cos(angles).astype(f32), np.sin(angles).astype(f32)
+    count = q_cols // HEAD_DIM + 1
+    ones, zeros = np.ones((length, HEAD_DIM), f32), np.zeros((length, HEAD_DIM), f32)
+    cos = np.concatenate([cos, cos] * count + [ones], axis=1)
+    sin = np.concatenate([-sin, sin] * count + [zeros], axis=1)
+    return jnp.asarray(cos), jnp.asarray(sin)
 
 
 def nn(a, b):
@@ -95,7 +101,8 @@
 
 
 class Gather:
-    def __init__(self, line, full, send_z, send_c, recv):
+    def __init__(self, line, full, send_z, send_c, recv, m=None):
+        self.m = m
         self.line, self.full, self.send_z, self.send_c, self.recv = line, full, send_z, send_c, recv
 
     @staticmethod
@@ -108,7 +115,8 @@
         ]
 
     def copy(self, index, send, seq):
-        return remote(self.full.at[index], self.full.at[index], send, self.recv.at[index], seq)
+        chunk = self.full.at[index] if self.m is None else self.full.at[self.m, index]
+        return remote(chunk, chunk, send, self.recv.at[index], seq)
 
     def begin(self):
         n = self.line
@@ -151,8 +159,9 @@
 
 
 class Scatter:
-    def __init__(self, line, part, sib, rcv, send_z, send_c, recv_z, recv_c):
-        self.line, self.part, self.sib, self.rcv = line, part, sib, rcv
+    def __init__(self, line, part, sib, rcv, send_z, send_c, recv_z, recv_c, m=None):
+        self.line, self.m = line, m
+        self.part, self.sib, self.rcv = part, sib, rcv
         self.send_z, self.send_c, self.recv_z, self.recv_c = send_z, send_c, recv_z, recv_c
 
     @staticmethod
@@ -166,18 +175,21 @@
         ]
 
     @staticmethod
-    def buffers(n_seq, rows, width):
+    def buffers(n_seq, rows, width, *lead):
         n_line = n_seq // 2
         return [
-            pltpu.VMEM((n_line, rows, width), BF16),
-            pltpu.VMEM((n_line + 1, rows, width), BF16),
+            pltpu.VMEM((*lead, n_line, rows, width), BF16),
+            pltpu.VMEM((*lead, n_line + 1, rows, width), BF16),
         ]
+
+    def at(self, index):
+        return index if self.m is None else (self.m, index)
 
     def across(self, chip):
         n = self.line
         return remote(
-            self.part.at[2 * chip + 1 - n.c],
-            self.sib.at[chip],
+            self.part.at[self.at(2 * chip + 1 - n.c)],
+            self.sib.at[self.at(chip)],
             self.send_c.at[chip],
             self.recv_c.at[chip],
             n.sibling,
@@ -186,8 +198,8 @@
     def hop(self, chip, slot, seq):
         n = self.line
         return remote(
-            self.part.at[2 * chip + n.c],
-            self.rcv.at[slot],
+            self.part.at[self.at(2 * chip + n.c)],
+            self.rcv.at[self.at(slot)],
             self.send_z.at[chip],
             self.recv_z.at[slot],
             seq,
@@ -202,7 +214,7 @@
             self.across(jnp.where(lax.rem(j, 2) == 0, n.last - half, half)).start()
 
     def add(self, chip, source):
-        mine = 2 * chip + self.line.c
+        mine = self.at(2 * chip + self.line.c)
         self.part[mine] = (self.part[mine].astype(F32) + source.astype(F32)).astype(BF16)
 
     def step(self, time):
@@ -212,12 +224,12 @@
         def _():
             chip = n.last - time + n.l
             self.across(chip).wait_recv()
-            self.add(chip, self.sib[chip])
+            self.add(chip, self.sib[self.at(chip)])
 
             @pl.when(n.has_left)
             def _():
                 self.hop(chip, chip, n.right).wait_recv()
-                self.add(chip, self.rcv[chip])
+                self.add(chip, self.rcv[self.at(chip)])
 
             self.hop(chip, chip, n.right).start()
 
@@ -225,30 +237,31 @@
         def _():
             chip = time - n.last + n.l
             self.across(chip).wait_recv()
-            self.add(chip, self.sib[chip])
+            self.add(chip, self.sib[self.at(chip)])
 
             @pl.when(n.has_right)
             def _():
                 self.hop(chip, chip, n.left).wait_recv()
-                self.add(chip, self.rcv[chip])
+                self.add(chip, self.rcv[self.at(chip)])
 
             self.hop(chip, jnp.where(chip == n.l - 1, n.n_line, chip), n.left).start()
 
-    def finish(self, out):
+    def finish(self, out, add=False):
         n = self.line
         mine = 2 * n.l + n.c
         self.across(n.l).wait_recv()
-        out[...] = self.part[mine].astype(F32) + self.sib[n.l].astype(F32)
+        value = self.part[self.at(mine)].astype(F32) + self.sib[self.at(n.l)].astype(F32)
+        out[...] = out[...] + value if add else value
 
         @pl.when(n.has_left)
         def _():
             self.hop(n.l, n.l, n.right).wait_recv()
-            out[...] += self.rcv[n.l].astype(F32)
+            out[...] += self.rcv[self.at(n.l)].astype(F32)
 
         @pl.when(n.has_right)
         def _():
             self.hop(n.l, n.n_line, n.left).wait_recv()
-            out[...] += self.rcv[n.n_line].astype(F32)
+            out[...] += self.rcv[self.at(n.n_line)].astype(F32)
 
         @pl.loop(0, n.n_line)
         def _(chip):
@@ -257,16 +270,32 @@
             pl.when(chip < n.l)(lambda: self.hop(chip, chip, n.left).wait_send())
 
 
+def norm_back(u, ge):
+    r = lax.rsqrt(jnp.mean(u * u, axis=1, keepdims=True) + EPSILON)
+    return r * ge - u * (r * r * r * jnp.mean(u * ge, axis=1, keepdims=True))
+
+
 def spread_work(units, slots, index):
     return (units * index // slots, units * (index + 1) // slots)
 
 
+class Square:
+    def __init__(self):
+        self.d = lax.axis_index("dp")
+        self.first = self.d + 1 - 2 * lax.rem(self.d, 2)
+        self.second = lax.rem(self.d + 2, 4)
+        self.across = 3 - self.d
+
+
 class Spread:
-    def __init__(self, line, n_dp, blocks, dst, own_sem, send_z, send_xy, recv):
+    def __init__(self, line, n_dp, relay, blocks, dst, own_sem, send_z, send_xy, recv, recv_half):
         self.line, self.n_dp, self.blocks, self.dst = line, n_dp, blocks, dst
-        self.own_sem, self.send_z, self.send_xy, self.recv = own_sem, send_z, send_xy, recv
+        self.relay = relay and n_dp == 4
+        self.own_sem, self.send_z, self.send_xy, self.recv, self.recv_half = own_sem, send_z, send_xy, recv, recv_half
         self.n_seq = 2 * line.n_line
         self.d = lax.axis_index("dp")
+        self.square = Square()
+        self.half = blocks.shape[1] // 2
 
     @staticmethod
     def sems(n_seq, n_dp):
@@ -275,7 +304,11 @@
             pltpu.SemaphoreType.DMA((n_seq,)),
             pltpu.SemaphoreType.DMA((n_seq, n_dp)),
             pltpu.SemaphoreType.DMA((n_dp, n_seq)),
+            pltpu.SemaphoreType.DMA((n_seq,)),
         ]
+
+    def source(self, j):
+        return lax.rem(self.line.s - j + self.n_seq, self.n_seq)
 
     def hop(self, t):
         n = self.line
@@ -292,56 +325,83 @@
         n = self.line
         return pltpu.make_async_copy(self.blocks.at[n.s], self.dst.at[self.d, n.s], self.own_sem.at[0])
 
-    def over(self, source, k, own=False):
+    def to_dp(self, src, dst, send, recv, peer):
         return pltpu.make_async_remote_copy(
-            src_ref=self.blocks.at[self.line.s] if own else self.dst.at[self.d, source],
-            dst_ref=self.dst.at[self.d, source],
-            send_sem=self.send_xy.at[source, k],
-            recv_sem=self.recv.at[self.d, source],
-            device_id={"dp": lax.rem(self.d + k, self.n_dp)},
-            device_id_type=MESH,
-        )
+            src_ref=src, dst_ref=dst, send_sem=send, recv_sem=recv, device_id={"dp": peer}, device_id_type=MESH
+        )
+
+    def over(self, source, own=False):
+        src = self.blocks.at[self.line.s] if own else self.dst.at[self.d, source]
+        peers = [lax.rem(self.d + k, self.n_dp) for k in range(1, self.n_dp)]
+        if self.relay:
+            peers = [self.square.first, self.square.second]
+        return [
+            self.to_dp(src, self.dst.at[self.d, source], self.send_xy.at[source, k + 1], self.recv.at[self.d, source], peer)
+            for k, peer in enumerate(peers)
+        ]
 
     def landed(self, d, source):
-        return pltpu.make_async_remote_copy(
-            src_ref=self.dst.at[d, source],
-            dst_ref=self.dst.at[d, source],
-            send_sem=self.send_z.at[0],
-            recv_sem=self.recv.at[d, source],
-            device_id={"dp": d},
-            device_id_type=MESH,
-        )
-
-    def begin(self):
+        block = self.dst.at[d, source]
+        return self.to_dp(block, block, self.send_z.at[0], self.recv.at[d, source], d)
+
+    def halves(self, source):
+        low, high = pl.ds(0, self.half), pl.ds(self.half, self.half)
+        one = self.dst.at[self.square.first, source, low]
+        two = self.dst.at[self.square.second, source, high]
+        return (
+            self.to_dp(one, one, self.send_xy.at[source, 3], self.recv.at[self.square.first, source], self.square.second),
+            self.to_dp(two, two, self.send_xy.at[source, 0], self.recv_half.at[source], self.square.first),
+        )
+
+    def pass_on(self, j):
+        if not self.relay:
+            return
+
+        @pl.when(j < self.n_seq)
+        def _():
+            source = self.source(j)
+            one, two = self.halves(source)
+            self.landed(self.square.first, source).wait_recv()
+            one.start()
+            self.landed(self.square.second, source).wait_recv()
+            two.start()
+
+    def begin(self, end):
         n = self.line
 
-        @pl.loop(1, self.n_seq)
+        @pl.loop(1, end)
         def _(j):
             self.hop(lax.rem(n.s + j, self.n_seq)).start()
 
         self.own().start()
 
+    def forward_one(self, j, ahead):
+        n = self.line
+
+        @pl.when(j < self.n_seq)
+        def _():
+            pl.when(j + ahead < self.n_seq)(lambda: self.hop(lax.rem(n.s + j + ahead, self.n_seq)).start())
+            source = self.source(j)
+            self.landed(self.d, source).wait_recv()
+            for copy in self.over(source):
+                copy.start()
+
     def forward_own(self):
-        for k in range(1, self.n_dp):
-            self.over(self.line.s, k, True).start()
-
-    def forward(self, first, end):
-        n = self.line
-
-        @pl.loop(first, end)
-        def _(j):
-            source = lax.rem(n.s - j + self.n_seq, self.n_seq)
-            self.landed(self.d, source).wait_recv()
-            for k in range(1, self.n_dp):
-                self.over(source, k).start()
+        for copy in self.over(self.line.s, True):
+            copy.start()
 
     def arrive(self):
-        for k in range(1, self.n_dp):
-            owner = lax.rem(self.d + k, self.n_dp)
-
-            @pl.loop(0, self.n_seq)
-            def _(source):
-                self.landed(owner, source).wait_recv()
+        @pl.loop(0, self.n_seq)
+        def _(source):
+            if self.relay:
+                low, high = pl.ds(0, self.half), pl.ds(self.half, self.half)
+                one = self.dst.at[self.square.across, source, low]
+                two = self.dst.at[self.square.across, source, high]
+                self.to_dp(one, one, self.send_z.at[0], self.recv.at[self.square.across, source], self.d).wait_recv()
+                self.to_dp(two, two, self.send_z.at[0], self.recv_half.at[source], self.d).wait_recv()
+            else:
+                for k in range(1, self.n_dp):
+                    self.landed(lax.rem(self.d + k, self.n_dp), source).wait_recv()
 
         self.own().wait()
 
@@ -351,8 +411,11 @@
         @pl.loop(0, self.n_seq)
         def _(j):
             pl.when(j != n.s)(lambda: self.hop(j).wait_send())
-            for k in range(1, self.n_dp):
-                self.over(j, k).wait_send()
+            for copy in self.over(j):
+                copy.wait_send()
+            if self.relay:
+                for copy in self.halves(j):
+                    copy.wait_send()
 
 
 class Copies:
@@ -360,34 +423,76 @@
         self.n_dp, self.own_ref, self.dst = n_dp, own, dst
         self.own_sem, self.send, self.recv = own_sem, send, recv
         self.d = lax.axis_index("dp")
+        self.relay = n_dp == 4
+        self.square = Square()
+        self.half = own.shape[0] // 2
 
     @staticmethod
     def sems(n_dp):
         return [
             pltpu.SemaphoreType.DMA((1,)),
             pltpu.SemaphoreType.DMA((n_dp,)),
-            pltpu.SemaphoreType.DMA((n_dp,)),
+            pltpu.SemaphoreType.DMA((n_dp + 1,)),
         ]
 
-    def copy(self, k, slot):
+    def copy(self, src, slot, part, send, recv, peer):
         return pltpu.make_async_remote_copy(
-            src_ref=self.own_ref,
-            dst_ref=self.dst.at[slot],
-            send_sem=self.send.at[k],
-            recv_sem=self.recv.at[slot],
-            device_id={"dp": lax.rem(self.d + k, self.n_dp)},
+            src_ref=src,
+            dst_ref=self.dst.at[slot] if part is None else self.dst.at[slot, part],
+            send_sem=self.send.at[send],
+            recv_sem=self.recv.at[recv],
+            device_id={"dp": peer},
             device_id_type=MESH,
         )
 
+    def direct(self):
+        peers = [lax.rem(self.d + k, self.n_dp) for k in range(1, self.n_dp)]
+        if self.relay:
+            peers = [self.square.first, self.square.second]
+        return [self.copy(self.own_ref, self.d, None, k + 1, self.d, peer) for k, peer in enumerate(peers)]
+
+    def landed(self, slot):
+        return self.copy(self.dst.at[slot], slot, None, 0, slot, slot)
+
+    def halves(self):
+        q = self.square
+        low, high = pl.ds(0, self.half), pl.ds(self.half, self.half)
+        return (
+            self.copy(self.dst.at[q.first, low], q.first, low, 3, q.first, q.second),
+            self.copy(self.dst.at[q.second, high], q.second, high, 0, self.n_dp, q.first),
+        )
+
+    def own(self):
+        return pltpu.make_async_copy(self.own_ref, self.dst.at[self.d], self.own_sem.at[0])
+
     def begin(self):
-        for k in range(1, self.n_dp):
-            self.copy(k, self.d).start()
-        pltpu.make_async_copy(self.own_ref, self.dst.at[self.d], self.own_sem.at[0]).start()
+        for copy in self.direct():
+            copy.start()
+        self.own().start()
+
+    def pass_on(self):
+        if not self.relay:
+            return
+        one, two = self.halves()
+        self.landed(self.square.first).wait_recv()
+        one.start()
+        self.landed(self.square.second).wait_recv()
+        two.start()
 
     def end(self):
-        for k in range(1, self.n_dp):
-            self.copy(k, lax.rem(self.d + k, self.n_dp)).wait()
-        pltpu.make_async_copy(self.own_ref, self.dst.at[self.d], self.own_sem.at[0]).wait()
+        for copy in self.direct():
+            copy.wait_send()
+        if self.relay:
+            low, high = pl.ds(0, self.half), pl.ds(self.half, self.half)
+            across = self.square.across
+            self.copy(self.dst.at[across, low], across, low, 0, across, across).wait_recv()
+            self.copy(self.dst.at[across, high], across, high, 0, self.n_dp, across).wait_recv()
+            for copy in self.halves():
+                copy.wait_send()
+        else:
+            for k in range(1, self.n_dp):
+                self.landed(lax.rem(self.d + k, self.n_dp)).wait_recv()
+        self.own().wait()
 
 
 class Relay:
@@ -581,13 +686,17 @@
     def place(self, j):
         return lax.rem(self.line.s + 1 + j, self.n_seq)
 
-    def begin(self):
+    def begin(self, ahead):
+        self.ahead = ahead
         self.own().start()
 
-        @pl.loop(0, self.n_seq)
+        @pl.loop(0, ahead)
         def _(j):
-            for k in range(1, self.n_dp):
-                self.over(self.place(j), k).start()
+            self.send(j)
+
+    def send(self, j):
+        for k in range(1, self.n_dp):
+            self.over(self.place(j), k).start()
 
     def reduce(self, first, end):
         if first == 0:
@@ -596,6 +705,7 @@
         @pl.loop(first, end)
         def _(j):
             t = self.place(j)
+            pl.when(j + self.ahead < self.n_seq)(lambda: self.send(j + self.ahead))
             for k in range(1, self.n_dp):
                 self.landed(lax.rem(self.d + k, self.n_dp), t).wait_recv()
             total = self.land[0, t].astype(F32)
@@ -626,7 +736,13 @@
         self.own_sem, self.send, self.recv = own_sem, send, recv
         self.d = lax.axis_index("dp")
 
-    sems = Copies.sems
+    @staticmethod
+    def sems(n_dp):
+        return [
+            pltpu.SemaphoreType.DMA((1,)),
+            pltpu.SemaphoreType.DMA((n_dp,)),
+            pltpu.SemaphoreType.DMA((n_dp,)),
+        ]
 
     def copy(self, k, slot):
         peer = lax.rem(self.d + k, self.n_dp)
@@ -666,6 +782,10 @@
     for k in range(1, n_dp):
         pl.semaphore_signal(barrier, 1, device_id={"dp": lax.rem(d + k, n_dp)}, device_id_type=MESH)
 
+    if relay is None:
+        pl.semaphore_wait(barrier, n_seq + n_dp - 2)
+        return
+
     @pl.when(relay.moves)
     def _():
         for device in ((relay.slot, relay.target), (relay.owner_d, relay.owner_s)):
@@ -690,16 +810,52 @@
     wide = jnp.concatenate([kv] * (q_cols // (2 * HEAD_DIM)), axis=1).astype(F32)
     swapped = pltpu.roll(wide, HEAD_DIM, 1)
     here = lax.div(lax.broadcasted_iota(jnp.int32, wide.shape, 1), HEAD_DIM) == h
-    even = lax.rem(h, 2) == 0
-    key = jnp.where(here, jnp.where(even, wide, swapped), 0.0).astype(BF16)
-    value = jnp.where(here, jnp.where(even, swapped, wide), 0.0).astype(BF16)
-    return key, value
+    key, value = (wide, swapped) if h % 2 == 0 else (swapped, wide)
+    key = jnp.where(here, key * (1.0 / math.sqrt(HEAD_DIM)), 0.0).astype(BF16)
+    return key, jnp.where(here, value, 0.0).astype(BF16)
+
+
+def hidden_keys(first, second, prefix, query_axis):
+    query, key = (first, second) if query_axis == 0 else (second, first)
+    return jnp.where((key <= query) | (key < prefix), 0.0, NEGATIVE)
+
+
+def bias_shape(length):
+    return (length, length) if length <= 2 * QUERY_TILE else (8, 128)
+
+
+def fill_bias(bias, prefix, query_axis, length):
+    if bias.shape[0] != length:
+        return
+    tile = min(length, QUERY_TILE)
+
+    @pl.loop(0, length // tile)
+    def _(i):
+        at = pl.ds(pl.multiple_of(i * tile, tile), tile)
+        first = i * tile + lax.broadcasted_iota(jnp.int32, (tile, length), 0)
+        second = lax.broadcasted_iota(jnp.int32, (tile, length), 1)
+        bias[at, :] = hidden_keys(first, second, prefix, query_axis)
+
+
+def bias_tile(bias, prefix, query_axis, length, tile, i):
+    at = pl.ds(pl.multiple_of(i * tile, tile), tile)
+    if bias.shape[0] == length:
+        return bias[at, :] if query_axis == 0 else bias[:, at]
+    shape = (tile, length) if query_axis == 0 else (length, tile)
+    first = lax.broadcasted_iota(jnp.int32, shape, 0)
+    second = lax.broadcasted_iota(jnp.int32, shape, 1)
+    if query_axis == 0:
+        first = first + i * tile
+    else:
+        second = second + i * tile
+    return hidden_keys(first, second, prefix, query_axis)
 
 
 def attention_kernel(
-    n_seq, n_dp, prefix_ref, tok_ref, cot_ref, cos_ref, sin_ref, qkvb_hbm, gub_hbm, wo_own, wd_own,
+    n_seq, n_dp, prefix_ref, tok_ref, cot_ref, cos_ref, sin_ref, gains_ref,
+    w_query_ref, w_key_ref, w_value_ref, w_gate_ref, w_up_ref, wo_own, wd_own,
     hidden_ref, nmlp_ref, q_ref, kv_ref, mixed_ref, normed_hbm, cot_hbm, wqkv_hbm, wo_hbm, wgu_hbm, wd_hbm,
-    full, cot, wqkv, wo, acc, part, sib, rcv, save_sem, *sems,
+    full, cot, wqkv, wo, acc, part, sib, rcv, qkvb, gub, bias, save_sem, *sems,
 ):
     n = Line(n_seq)
     rows, width = tok_ref.shape
@@ -708,129 +864,161 @@
     cols_all = wqkv.shape[3]
     pair = 2 * rows
     tok = tok_ref[...].astype(F32)
-    full[n.s] = (tok * lax.rsqrt(jnp.mean(tok * tok, axis=1, keepdims=True) + EPSILON)).astype(BF16)
+    normed = (tok * lax.rsqrt(jnp.mean(tok * tok, axis=1, keepdims=True) + EPSILON)).astype(BF16)
+    for m in range(micro):
+        full[m, n.s] = normed[m * span : (m + 1) * span]
     cot[n.s] = cot_ref[...]
 
-    gather = Gather(n, full, *sems[0:3])
-    gather_cot = Gather(n, cot, *sems[3:6])
-    scatter = Scatter(n, part, sib, rcv, *sems[6:10])
-    qkv_w = Spread(n, n_dp, qkvb_hbm, wqkv, *sems[10:14])
-    gu_w = Spread(n, n_dp, gub_hbm, wgu_hbm, *sems[14:18])
-    out_w = OutRows(n, n_dp, wo_own, wo, *sems[18:22])
-    down_w = Copies(n_dp, wd_own, wd_hbm, *sems[22:25])
+    sems = list(sems)
+    take = lambda count: [sems.pop(0) for _ in range(count)]
+    gathers = [Gather(n, full, *take(3), m=m) for m in range(micro)]
+    scatters = [Scatter(n, part, sib, rcv, *take(4), m=m) for m in range(micro)]
+    gather_cot = Gather(n, cot, *take(3))
+    qkv_w = Spread(n, n_dp, False, qkvb, wqkv, *take(5))
+    gu_w = Spread(n, n_dp, True, gub, wgu_hbm, *take(5))
+    out_w = OutRows(n, n_dp, wo_own, wo, *take(4))
+    down_w = Copies(n_dp, wd_own, wd_hbm, *take(3))
+
+    repeat = n_seq // KV_HEADS
+    ff_block = wd_own.shape[0]
+    gain_attn = gains_ref[:, :1]
+    gain_mlp = gains_ref[:, 2 * HEAD_DIM : 2 * HEAD_DIM + 1]
+    for t in range(n_seq):
+        head = slice(t // repeat * HEAD_DIM, (t // repeat + 1) * HEAD_DIM)
+        qkvb[t, :, :q_cols] = (w_query_ref[:, t * q_cols : (t + 1) * q_cols].astype(F32) * gain_attn).astype(BF16)
+        key_value = jnp.concatenate([w_key_ref[:, head], w_value_ref[:, head]], axis=1)
+        qkvb[t, :, q_cols:] = (key_value.astype(F32) * gain_attn).astype(BF16)
 
     greet_all(n, n_dp, out_w)
-    qkv_w.begin()
-    gather.begin()
+    qkv_w.begin(n_seq)
+    gathers[0].begin()
     out_w.begin()
     qkv_w.forward_own()
-    qkv_w.forward(1, n_seq)
+    for i, ref in enumerate((w_gate_ref, w_up_ref)):
+        for owner in range(n_dp):
+            for t in range(n_seq):
+                cols = slice((owner * n_seq + t) * ff_block, (owner * n_seq + t + 1) * ff_block)
+                first = (i * n_dp + owner) * ff_block
+                gub[t, :, first : first + ff_block] = (ref[:, cols].astype(F32) * gain_mlp).astype(BF16)
+
+    @pl.loop(1, n_seq)
+    def _(j):
+        qkv_w.forward_one(j, n_seq)
+
     out_w.forward()
+    gathers[1].begin()
     down_w.begin()
+    gu_w.forward_own()
     for j in range(n.n_line):
-        gather.visit(n.order(j))
-    gu_w.begin()
-    gu_w.forward_own()
+        gathers[0].visit(n.order(j))
     qkv_w.arrive()
-
-    saves = [
-        pltpu.make_async_copy(full, normed_hbm, save_sem.at[0]),
-        pltpu.make_async_copy(wqkv, wqkv_hbm, save_sem.at[1]),
-    ]
-    for save in saves:
-        save.start()
+    pltpu.make_async_copy(wqkv, wqkv_hbm, save_sem.at[1]).start()
+    gu_w.begin(1 + AHEAD)
 
     low = low_lanes((span, cols_all))
-
-    @pl.loop(0, n.n_line)
-    def _(chip):
-        two = pl.ds(pl.multiple_of(2 * chip, 2), 2)
-        value = nn(full[two].reshape(pair, width), wqkv[...].reshape(width, cols_all))
-        for core in range(2):
-            at = pl.ds(pl.multiple_of((2 * chip + core) * span, span), span)
-            cos, sin = cos_ref[at, :], sin_ref[at, :]
-            for m in range(micro):
-                block = value[(core * micro + m) * span : (core * micro + m + 1) * span]
-                turned = (block * cos + turn(block, low) * sin).astype(BF16)
+    half_line = length // span // 2
+    heads = q_cols // HEAD_DIM
+    q_tile = min(length, QUERY_TILE)
+    steps = n.last
+
+    def project(m):
+        @pl.loop(0, 2)
+        def _(i):
+            some = pl.ds(pl.multiple_of(i * half_line, half_line), half_line)
+            value = nn(full[m, some].reshape(half_line * span, width), wqkv[...].reshape(width, cols_all))
+            for k in range(half_line):
+                at = pl.ds(pl.multiple_of((i * half_line + k) * span, span), span)
+                block = value[k * span : (k + 1) * span]
+                turned = (block * cos_ref[at, :] + turn(block, low) * sin_ref[at, :]).astype(BF16)
                 q_ref[m, at, :] = turned[:, :q_cols]
                 kv_ref[m, at, :] = turned[:, q_cols:]
 
-    scale = 1.0 / math.sqrt(HEAD_DIM)
-    q_tile = min(length, QUERY_TILE)
-
-    @pl.loop(0, micro)
-    def _(m):
-        prefix = prefix_ref[m]
-
-        @pl.loop(0, q_cols // HEAD_DIM)
-        def _(h):
-            key, val = head_lanes(kv_ref[m], h, q_cols)
-
-            @pl.loop(0, length // q_tile)
-            def _(i):
-                at = pl.ds(pl.multiple_of(i * q_tile, q_tile), q_tile)
-                scores = nt(q_ref[m, at, :], key) * scale
-                query_pos = i * q_tile + lax.broadcasted_iota(jnp.int32, scores.shape, 0)
-                key_pos = lax.broadcasted_iota(jnp.int32, scores.shape, 1)
-                scores = jnp.where((key_pos <= query_pos) | (key_pos < prefix), scores, NEGATIVE)
-                weights = jnp.exp(scores - jnp.max(scores, axis=1, keepdims=True))
-                total = jnp.sum(weights, axis=1, keepdims=True)
-                mixed = nn((weights / total).astype(BF16), val)
-
-                @pl.when(h == 0)
-                def _():
-                    acc[at, :] = mixed
-
-                @pl.when(h > 0)
-                def _():
-                    acc[at, :] += mixed
-
+    def attend(m, h):
+        key, val = head_lanes(kv_ref[m], h, q_cols)
+
+        @pl.loop(0, length // q_tile)
+        def _(i):
+            at = pl.ds(pl.multiple_of(i * q_tile, q_tile), q_tile)
+            scores = nt(q_ref[m, at, :], key) + bias_tile(bias, prefix_ref[m], 0, length, q_tile, i)
+            weights = jnp.exp(scores - jnp.max(scores, axis=1, keepdims=True))
+            inverse = 1.0 / jnp.sum(weights, axis=1, keepdims=True)
+            mixed = nn((weights * inverse).astype(BF16), val)
+            if h == 0:
+                acc[at, :] = mixed
+            else:
+                acc[at, :] += mixed
+
+    sent = passed = 0
+    for m in range(micro):
+        project(m)
+        fill_bias(bias, prefix_ref[m], 0, length)
+        for h in range(heads):
+            if m + 1 < micro:
+                for j in range(*spread_work(n.n_line, heads, h)):
+                    gathers[m + 1].visit(n.order(j))
+            if m > 0:
+                if h == 0:
+                    down_w.pass_on()
+                for time in range(*spread_work(steps, heads, h)):
+                    scatters[m - 1].step(time)
+                    sent += 1
+                    gu_w.forward_one(sent, AHEAD)
+            attend(m, h)
         mixed_ref[m] = acc[...].astype(BF16)
-
-    out_w.arrive()
-    pltpu.make_async_copy(wo, wo_hbm, save_sem.at[2]).start()
-    for m in range(micro):
+        if m == 0:
+            out_w.arrive()
+            pltpu.make_async_copy(wo, wo_hbm, save_sem.at[2]).start()
 
         @pl.loop(0, width // TILE)
         def _(w):
             cols = pl.ds(pl.multiple_of(w * TILE, TILE), TILE)
             value = nn(mixed_ref[m], wo[:, :, cols].reshape(q_cols, TILE))
-            part[:, m * span : (m + 1) * span, cols] = value.astype(BF16).reshape(n_seq, span, TILE)
-
-    scatter.begin()
-    gather_cot.begin()
+            part[m, :, :, cols] = value.astype(BF16).reshape(n_seq, span, TILE)
+
+        scatters[m].begin()
+        if m == 0:
+            gather_cot.begin()
+
+    pltpu.make_async_copy(full, normed_hbm, save_sem.at[0]).start()
     gather_cot.visit(n.l)
+    rest = n_seq - 1 - sent
     for time in range(n.last):
-        scatter.step(time)
+        scatters[-1].step(time)
+        for j in range(*spread_work(rest, n.last, time)):
+            gu_w.forward_one(sent + 1 + j, AHEAD)
         gather_cot.visit(n.order(time + 1))
-        first, end = spread_work(n_seq - 1, n.last, time)
-        gu_w.forward(first + 1, end + 1)
+        for j in range(*spread_work(n_seq, n.last, time)):
+            gu_w.pass_on(j)
     pltpu.make_async_copy(cot, cot_hbm, save_sem.at[3]).start()
-    scatter.finish(hidden_ref)
+    for m in range(micro):
+        at = slice(m * span, (m + 1) * span)
+        scatters[m].finish(hidden_ref.at[at])
     hidden = hidden_ref[...] + tok_ref[...].astype(F32)
     hidden_ref[...] = hidden
     nmlp_ref[...] = (hidden * lax.rsqrt(jnp.mean(hidden * hidden, axis=1, keepdims=True) + EPSILON)).astype(BF16)
     gu_w.arrive()
     down_w.end()
-    for save in saves:
-        save.wait()
+    pltpu.make_async_copy(full, normed_hbm, save_sem.at[0]).wait()
+    pltpu.make_async_copy(wqkv, wqkv_hbm, save_sem.at[1]).wait()
     pltpu.make_async_copy(wo, wo_hbm, save_sem.at[2]).wait()
     pltpu.make_async_copy(cot, cot_hbm, save_sem.at[3]).wait()
-    gather.end()
+    for gather in gathers:
+        gather.end()
     gather_cot.end()
     qkv_w.end()
     gu_w.end()
     out_w.end()
 
 
-def attention_call(prefix, tok, cot, cos, sin, qkvb, gub, wo_own, wd_own, n_seq, n_dp):
+def attention_call(prefix, tok, cot, cos, sin, gains, w_query, w_key, w_value, w_gate, w_up, wo_own, wd_own, n_seq, n_dp):
     rows, width = tok.shape
     micro = prefix.shape[0]
     length = cos.shape[0]
-    shard, qkv_cols = qkvb.shape[1:]
-    gu_cols = gub.shape[2]
+    shard = wo_own.shape[0]
     q_cols = width // n_seq
+    qkv_cols = q_cols + 2 * HEAD_DIM
     ff_block = wd_own.shape[0]
+    gu_cols = 2 * n_dp * ff_block
     every = n_seq * rows
     any_spec = pl.BlockSpec(memory_space=pl.ANY)
     vmem = pl.BlockSpec(memory_space=pltpu.VMEM)
@@ -840,7 +1028,7 @@
         ((micro, length, q_cols), BF16, vmem),
         ((micro, length, 2 * HEAD_DIM), BF16, vmem),
         ((micro, length, q_cols), BF16, vmem),
-        ((n_seq, rows, width), BF16, any_spec),
+        ((micro, n_seq, rows // micro, width), BF16, any_spec),
         ((n_seq, rows, width), BF16, any_spec),
         ((n_dp, n_seq, shard, qkv_cols), BF16, any_spec),
         ((n_dp, shard, width), BF16, any_spec),
@@ -850,20 +1038,23 @@
     return pl.pallas_call(
         functools.partial(attention_kernel, n_seq, n_dp),
         out_shape=tuple(jax.ShapeDtypeStruct(s, t) for s, t, _ in outs),
-        in_specs=[pl.BlockSpec(memory_space=pltpu.SMEM)] + [vmem] * 4 + [any_spec] * 4,
+        in_specs=[pl.BlockSpec(memory_space=pltpu.SMEM)] + [vmem] * 10 + [any_spec] * 2,
         out_specs=tuple(spec for _, _, spec in outs),
         scratch_shapes=[
-            pltpu.VMEM((n_seq, rows, width), BF16),
+            pltpu.VMEM((micro, n_seq, rows // micro, width), BF16),
             pltpu.VMEM((n_seq, rows, width), BF16),
             pltpu.VMEM((n_dp, n_seq, shard, qkv_cols), BF16),
             pltpu.VMEM((n_dp, shard, width), BF16),
             pltpu.VMEM((length, q_cols), F32),
-            pltpu.VMEM((n_seq, rows, width), BF16),
-            *Scatter.buffers(n_seq, rows, width),
+            pltpu.VMEM((micro, n_seq, rows // micro, width), BF16),
+            *Scatter.buffers(n_seq, rows // micro, width, micro),
+            pltpu.VMEM((n_seq, shard, qkv_cols), BF16),
+            pltpu.VMEM((n_seq, shard, gu_cols), BF16),
+            pltpu.VMEM(bias_shape(length), F32),
             pltpu.SemaphoreType.DMA((4,)),
+            *Gather.sems(n_seq) * micro,
+            *Scatter.sems(n_seq) * micro,
             *Gather.sems(n_seq),
-            *Gather.sems(n_seq),
-            *Scatter.sems(n_seq),
             *Spread.sems(n_seq, n_dp),
             *Spread.sems(n_seq, n_dp),
             *OutRows.sems(n_dp),
@@ -874,13 +1065,13 @@
         ),
         cost_estimate=pl.CostEstimate(flops=10**10, bytes_accessed=40 << 20, transcendentals=0),
         name="attention",
-    )(prefix, tok, cot, cos, sin, qkvb, gub, wo_own, wd_own)
+    )(prefix, tok, cot, cos, sin, gains, w_query, w_key, w_value, w_gate, w_up, wo_own, wd_own)
 
 
 def mlp_kernel(
-    n_seq, n_dp, x_ref, cot_hbm, wgu_hbm, wd_hbm,
-    gnm_ref, pout_hbm, dgu_hbm, dwd_ref,
-    full, cot, wgu, wd, act, gg, gu, part, sib, rcv, dwd, land, stage_gu, stage_rows, load_sem, gu_sem, rows_sem, *sems,
+    n_seq, n_dp, x_ref, hidden_ref, cot_hbm, wgu_hbm, wd_hbm,
+    branch_ref, gh_ref, pout_hbm, dgu_hbm, dwd_ref,
+    full, cot, wgu, wd, act, gg, gu, part, sib, rcv, dwd, land, total, stage_gu, stage_rows, load_sem, gu_sem, rows_sem, *sems,
 ):
     n = Line(n_seq)
     rows, width = x_ref.shape
@@ -895,7 +1086,7 @@
     for load in loads:
         load.start()
     full[n.s] = x_ref[...]
-    n.greet(n_dp)
+    greet_all(n, n_dp, None)
     gather = Gather(n, full, *sems[:3])
     scatter = Scatter(n, part, sib, rcv, *sems[3:7])
     down = RowSum(n_dp, dwd, land, *sems[7:10])
@@ -930,7 +1121,6 @@
             part[two, :, cols] = value.astype(BF16).reshape(2, rows, TILE)
 
     scatter.begin()
-
     owners = TILE // dwd.shape[1]
 
     @pl.loop(0, ff // TILE)
@@ -988,18 +1178,21 @@
 
     for time in range(n.last):
         scatter.step(time)
+        if time == 0:
+            out_parts(0, n.n_line)
         gate_up_grads(*spread_work(width // TILE, n.last, time))
-        if time == n.last - 1:
-            out_parts(0, n.n_line)
-            drain_out()
+    scatter.finish(total)
+    grad_hidden = cot[n.s].astype(F32) + norm_back(hidden_ref[...], total[...])
+    gh_ref[...] = grad_hidden
+    branch_ref[...] = grad_hidden.astype(BF16)
+    drain_out()
     for slot in range(2):
         pltpu.make_async_copy(stage_gu.at[slot], dgu_hbm.at[pl.ds(0, TILE), :], gu_sem.at[slot]).wait()
-    scatter.finish(gnm_ref)
     down.finish(dwd_ref)
     gather.end()
 
 
-def mlp_call(x, cot, wgu, wd, n_seq, n_dp):
+def mlp_call(x, hidden, cot, wgu, wd, n_seq, n_dp):
     rows, width = x.shape
     ff = wd.shape[0]
     every = n_seq * rows
@@ -1008,13 +1201,14 @@
     return pl.pallas_call(
         functools.partial(mlp_kernel, n_seq, n_dp),
         out_shape=(
+            jax.ShapeDtypeStruct((rows, width), BF16),
             jax.ShapeDtypeStruct((rows, width), F32),
             jax.ShapeDtypeStruct((n_seq, rows, width), BF16),
             jax.ShapeDtypeStruct((width, 2 * ff), BF16),
             jax.ShapeDtypeStruct((ff // n_dp, width), F32),
         ),
-        in_specs=[vmem] + [any_spec] * 3,
-        out_specs=(vmem, any_spec, any_spec, vmem),
+        in_specs=[vmem] * 2 + [any_spec] * 3,
+        out_specs=(vmem, vmem, any_spec, any_spec, vmem),
         scratch_shapes=[
             pltpu.VMEM((n_seq, rows, width), BF16),
             pltpu.VMEM((n_seq, rows, width), BF16),
@@ -1027,6 +1221,7 @@
             *Scatter.buffers(n_seq, rows, width),
             pltpu.VMEM((n_dp, ff // n_dp, width), BF16),
             pltpu.VMEM((n_dp, ff // n_dp, width), BF16),
+            pltpu.VMEM((rows, width), F32),
             pltpu.VMEM((2, TILE, 2 * ff), BF16),
             pltpu.VMEM((2, TILE, width), BF16),
             pltpu.SemaphoreType.DMA((3,)),
@@ -1041,15 +1236,15 @@
         ),
         cost_estimate=pl.CostEstimate(flops=18 * every * width * ff, bytes_accessed=40 << 20, transcendentals=0),
         name="mlp",
-    )(x, cot, wgu, wd)
+    )(x, hidden, cot, wgu, wd)
 
 
 def backward_kernel(
-    n_seq, n_dp, prefix_ref, branch_ref, q_ref, kv_ref, mixed_ref, cos_ref, sin_ref, gains_ref,
-    pout_hbm, normed_hbm, wqkv_hbm, wo_hbm, dgu_hbm,
-    ge_ref, sum_ref, dqkv_out, dwo_out, dgate_ref, dup_ref,
-    full, tiles, wqkv, wo, gm, acc_q, acc_k, acc_v, gqkv, part, sib, rcv, sib_o, rcv_o,
-    land_gu, final_gu, dqkv, land_qkv, final_qkv, dwo, land_o, final_o, load_sem, tile_sem, *sems,
+    n_seq, n_dp, prefix_ref, branch_ref, tok_ref, q_ref, kv_ref, mixed_ref, cos_ref, sin_ref, gains_ref,
+    w_query_ref, w_key_ref, w_value_ref, gh_hbm, hidden_hbm, pout_hbm, normed_hbm, wqkv_hbm, wo_hbm, dgu_hbm,
+    out_ref, in_ref, dgain_ref, dq_ref, dk_ref, dv_ref, dwo_out, dgate_ref, dup_ref,
+    full, tiles, wqkv, wo, gm, acc_q, acc_k, acc_v, bias, gqkv, part, sib, rcv, sib_o, rcv_o,
+    land_gu, final_gu, dqkv, land_qkv, final_qkv, dwo, land_o, final_o, total, load_sem, tile_sem, *sems,
 ):
     n = Line(n_seq)
     rows, width = branch_ref.shape
@@ -1059,72 +1254,87 @@
     loads = [
         pltpu.make_async_copy(src, dst, load_sem.at[i])
         for i, (src, dst) in enumerate(
-            [(pout_hbm, part), (wo_hbm, wo), (wqkv_hbm, wqkv)]
+            [(pout_hbm, part), (wo_hbm, wo), (wqkv_hbm, wqkv), (hidden_hbm, total), (gh_hbm, in_ref)]
         )
     ]
     for load in loads:
         load.start()
-    full[n.s] = branch_ref[...]
-    gather = Gather(n, full, *sems[0:3])
-    scatter = Scatter(n, part, sib, rcv, *sems[3:7])
-    scatter_out = Scatter(n, part, sib_o, rcv_o, *sems[7:11])
-    gu_sum = Collect(n, n_dp, dgu_hbm, land_gu, final_gu, *sems[11:16])
-    qkv_sum = Collect(n, n_dp, dqkv, land_qkv, final_qkv, *sems[16:21])
-    out_sum = OutSum(n, n_dp, dwo, land_o, final_o, *sems[21:26])
+    for m in range(micro):
+        full[m, n.s] = branch_ref[m * span : (m + 1) * span, :]
+    sems = list(sems)
+    take = lambda count: [sems.pop(0) for _ in range(count)]
+    gathers = [Gather(n, full, *take(3), m=m) for m in range(micro)]
+    scatter = Scatter(n, part, sib, rcv, *take(4))
+    scatter_out = Scatter(n, part, sib_o, rcv_o, *take(4))
+    gu_sum = Collect(n, n_dp, dgu_hbm, land_gu, final_gu, *take(5))
+    qkv_sum = Collect(n, n_dp, dqkv, land_qkv, final_qkv, *take(5))
+    out_sum = OutSum(n, n_dp, dwo, land_o, final_o, *take(5))
     greet_all(n, n_dp, out_sum)
-    gather.begin()
+    gathers[0].begin()
+    gu_sum.begin(3)
     loads[0].wait()
+    loads[1].wait()
+    late = n_seq * 5 // 8
     scatter_out.begin()
-    gu_sum.begin()
-    loads[1].wait()
-    early = n_seq // 2
-
+    gathers[1].begin()
     for j in range(n.n_line):
-        chip = n.order(j)
-        gather.visit(chip)
-        two = pl.ds(pl.multiple_of(2 * chip, 2), 2)
-        value = nt(full[two].reshape(pair, width), wo[...].reshape(q_cols, width)).astype(BF16)
-        for core in range(2):
-            at = pl.ds(pl.multiple_of((2 * chip + core) * span, span), span)
-            for m in range(micro):
-                gm[m, at, :] = value[(core * micro + m) * span : (core * micro + m + 1) * span]
-        if j < n.last:
-            scatter_out.step(j)
-        if j > 0:
-            gu_sum.reduce(*spread_work(early, n.last, j - 1))
-
+        gathers[0].visit(n.order(j))
+    loads[2].wait()
+
+    heads = q_cols // HEAD_DIM
     scale = 1.0 / math.sqrt(HEAD_DIM)
     q_tile = min(length, QUERY_TILE)
     low = low_lanes((length, q_cols + 2 * HEAD_DIM))
-    loads[2].wait()
-
-    @pl.loop(0, micro)
-    def _(m):
-        prefix = prefix_ref[m]
+    here = lax.div(lax.broadcasted_iota(jnp.int32, (length, q_cols), 1), HEAD_DIM)
+
+    def attend_back(m, h):
+        key, val = head_lanes(kv_ref[m], h, q_cols)
+
+        @pl.loop(0, length // q_tile)
+        def _(i):
+            at = pl.ds(pl.multiple_of(i * q_tile, q_tile), q_tile)
+            query, grad = q_ref[m, at, :], gm[m, at, :]
+            scores = nt(key, query) + bias_tile(bias, prefix_ref[m], 1, length, q_tile, i)
+            weights = jnp.exp(scores - jnp.max(scores, axis=0, keepdims=True))
+            probs = weights * (1.0 / jnp.sum(weights, axis=0, keepdims=True))
+            grad_probs = nt(val, grad)
+            delta = jnp.sum(probs * grad_probs, axis=0, keepdims=True)
+            grad_scores = (probs * (grad_probs - delta)).astype(BF16)
+            acc_q[at, :] += tn(grad_scores, key)
+            acc_k[...] += jnp.where(here == h, nn(grad_scores, query), 0.0)
+            acc_v[...] += jnp.where(here == h, nn(probs.astype(BF16), grad), 0.0)
+
+    shard = dwo.shape[1]
+
+    def out_grads():
+
+        @pl.loop(0, width // TILE)
+        def _(w):
+            cols = pl.ds(pl.multiple_of(w * TILE, TILE), TILE)
+            d_out = jnp.zeros((q_cols, TILE), F32)
+            for m in range(micro):
+                d_out = d_out + tn(mixed_ref[m], full[m, :, :, cols].reshape(length, TILE))
+            dwo[:, :, cols] = d_out.astype(BF16).reshape(n_dp, shard, TILE)
+
+        out_sum.begin()
+
+    for m in range(micro):
+        gm[m] = nt(full[m].reshape(length, width), wo[...].reshape(q_cols, width)).astype(BF16)
+        fill_bias(bias, prefix_ref[m], 1, length)
         for ref in (acc_q, acc_k, acc_v):
             ref[...] = jnp.zeros_like(ref)
-
-        @pl.loop(0, q_cols // HEAD_DIM)
-        def _(h):
-            key, val = head_lanes(kv_ref[m], h, q_cols)
-            here = lax.div(lax.broadcasted_iota(jnp.int32, (length, q_cols), 1), HEAD_DIM) == h
-
-            @pl.loop(0, length // q_tile)
-            def _(i):
-                at = pl.ds(pl.multiple_of(i * q_tile, q_tile), q_tile)
-                query, grad = q_ref[m, at, :], gm[m, at, :]
-                scores = nt(key, query) * scale
-                key_pos = lax.broadcasted_iota(jnp.int32, scores.shape, 0)
-                query_pos = i * q_tile + lax.broadcasted_iota(jnp.int32, scores.shape, 1)
-                scores = jnp.where((key_pos <= query_pos) | (key_pos < prefix), scores, NEGATIVE)
-                weights = jnp.exp(scores - jnp.max(scores, axis=0, keepdims=True))
-                probs = weights / jnp.sum(weights, axis=0, keepdims=True)
-                grad_probs = nt(val, grad)
-                delta = jnp.sum(probs * grad_probs, axis=0, keepdims=True)
-                grad_scores = (probs * (grad_probs - delta)).astype(BF16)
-                acc_q[at, :] += tn(grad_scores, key)
-                acc_k[...] += jnp.where(here, nn(grad_scores, query), 0.0)
-                acc_v[...] += jnp.where(here, nn(probs.astype(BF16), grad), 0.0)
+        for h in range(heads):
+            if m + 1 < micro:
+                for j in range(*spread_work(n.n_line, heads, h)):
+                    gathers[m + 1].visit(n.order(j))
+            if m == 0:
+                for time in range(*spread_work(n.last, heads, h)):
+                    scatter_out.step(time)
+            if m == 1 and h == 0:
+                out_grads()
+            for j in range(*spread_work(late, micro * heads, m * heads + h)):
+                gu_sum.reduce(j, j + 1)
+            attend_back(m, h)
 
         def fold(ref):
             total = ref[:, : 2 * HEAD_DIM]
@@ -1133,10 +1343,12 @@
             return total + pltpu.roll(total, HEAD_DIM, 1)
 
         first = lax.broadcasted_iota(jnp.int32, (length, 2 * HEAD_DIM), 1) < HEAD_DIM
-        grads = jnp.concatenate([acc_q[...] * scale, jnp.where(first, fold(acc_k) * scale, fold(acc_v))], axis=1)
+        grads = jnp.concatenate([acc_q[...], jnp.where(first, fold(acc_k) * scale, fold(acc_v))], axis=1)
         gqkv[m] = (grads * cos_ref[...] - turn(grads, low) * sin_ref[...]).astype(BF16)
 
-    scatter_out.finish(sum_ref)
+    loads[3].wait()
+    scatter_out.finish(total, True)
+    out_ref[...] = total[...].astype(BF16)
     for m in range(micro):
 
         @pl.loop(0, width // TILE)
@@ -1147,25 +1359,13 @@
 
     scatter.begin()
 
-    shard = dwo.shape[1]
-
-    @pl.loop(0, width // TILE)
-    def _(w):
-        cols = pl.ds(pl.multiple_of(w * TILE, TILE), TILE)
-        d_out = jnp.zeros((q_cols, TILE), F32)
-        for m in range(micro):
-            d_out = d_out + tn(mixed_ref[m], full[:, m * span : (m + 1) * span, cols].reshape(length, TILE))
-        dwo[:, :, cols] = d_out.astype(BF16).reshape(n_dp, shard, TILE)
-
-    out_sum.begin()
-
     half = n_seq // 2
     depth = half * shard
 
     def fetch(w):
         cols = pl.ds(pl.multiple_of(w * depth, depth), depth)
         slot = lax.rem(w, 2)
-        return pltpu.make_async_copy(normed_hbm.at[:, :, cols], tiles.at[slot], tile_sem.at[slot])
+        return pltpu.make_async_copy(normed_hbm.at[:, :, :, cols], tiles.at[slot], tile_sem.at[slot])
 
     fetch(jnp.int32(0)).start()
 
@@ -1176,35 +1376,57 @@
         slot = lax.rem(w, 2)
         d_qkv = jnp.zeros((depth, q_cols + 2 * HEAD_DIM), F32)
         for m in range(micro):
-            d_qkv = d_qkv + tn(tiles[slot, :, m * span : (m + 1) * span, :].reshape(length, depth), gqkv[m])
+            d_qkv = d_qkv + tn(tiles[slot, m].reshape(length, depth), gqkv[m])
         at = pl.ds(pl.multiple_of(lax.rem(w, 2) * half, half), half)
         dqkv[lax.div(w, 2), at] = d_qkv.astype(BF16).reshape(half, shard, q_cols + 2 * HEAD_DIM)
 
-    qkv_sum.begin()
+    qkv_sum.begin(n_seq)
+    out_sum.reduce()
     for time in range(n.last):
         scatter.step(time)
-        first, end = spread_work(n_seq - early, n.last, time)
-        gu_sum.reduce(early + first, early + end)
-    out_sum.reduce()
+        first, end = spread_work(n_seq - late, n.last, time)
+        gu_sum.reduce(late + first, late + end)
     qkv_sum.reduce(0, n_seq)
-    scatter.finish(ge_ref)
+    scatter.finish(total)
+    loads[4].wait()
+    in_ref[...] += norm_back(tok_ref[...].astype(F32), total[...])
     gu_sum.end()
     ff_block = dgate_ref.shape[1] // (n_dp * n_seq)
-    gain = gains_ref[:, 2 * HEAD_DIM : 2 * HEAD_DIM + 1]
-    for t in range(n_seq):
-        for i, ref in enumerate((dgate_ref, dup_ref)):
-            for owner in range(n_dp):
+    gain_attn = gains_ref[:, :1]
+    for i, ref in enumerate((dgate_ref, dup_ref)):
+        for owner in range(n_dp):
+            for t in range(n_seq):
                 cols = slice((owner * n_seq + t) * ff_block, (owner * n_seq + t + 1) * ff_block)
                 first = (i * n_dp + owner) * ff_block
-                ref[:, cols] = final_gu[t, :, first : first + ff_block].astype(F32) * gain
+                ref[:, cols] = final_gu[t, :, first : first + ff_block]
     qkv_sum.end()
-    dqkv_out[...] = final_qkv[...].astype(F32) * gains_ref[:, :1][None]
+    repeat = n_seq // KV_HEADS
+    dots = jnp.zeros((shard, 1), F32)
+    for t in range(n_seq):
+        cols = slice(t * q_cols, (t + 1) * q_cols)
+        value = final_qkv[t, :, :q_cols].astype(F32)
+        dots = dots + jnp.sum(value * w_query_ref[:, cols].astype(F32), axis=1, keepdims=True)
+        dq_ref[:, cols] = value * gain_attn
+    for g in range(KV_HEADS):
+        cols = slice(g * HEAD_DIM, (g + 1) * HEAD_DIM)
+        for i, (ref, w_ref) in enumerate(((dk_ref, w_key_ref), (dv_ref, w_value_ref))):
+            lanes = slice(q_cols + i * HEAD_DIM, q_cols + (i + 1) * HEAD_DIM)
+            value = final_qkv[g * repeat, :, lanes].astype(F32)
+            for t in range(g * repeat + 1, (g + 1) * repeat):
+                value = value + final_qkv[t, :, lanes].astype(F32)
+            dots = dots + jnp.sum(value * w_ref[:, cols].astype(F32), axis=1, keepdims=True)
+            ref[:, cols] = value * gain_attn
+    dgain_ref[...] = dots * jnp.ones((shard, 2 * HEAD_DIM), F32)
     out_sum.end()
     dwo_out[...] = final_o[...].astype(F32)
-    gather.end()
-
-
-def backward_call(prefix, branch, q, kv, mixed, cos, sin, gains, pout, normed, wqkv, wo, dgu):
+    for gather in gathers:
+        gather.end()
+
+
+def backward_call(
+    prefix, branch, tok, q, kv, mixed, cos, sin, gains, w_query, w_key, w_value,
+    gh, hidden, pout, normed, wqkv, wo, dgu,
+):
     rows, width = branch.shape
     n_dp, n_seq, shard, gu_cols = dgu.shape
     ff = gu_cols // 2 * n_seq
@@ -1216,24 +1438,26 @@
     return pl.pallas_call(
         functools.partial(backward_kernel, n_seq, n_dp),
         out_shape=(
+            jax.ShapeDtypeStruct((rows, width), BF16),
             jax.ShapeDtypeStruct((rows, width), F32),
-            jax.ShapeDtypeStruct((rows, width), F32),
-            jax.ShapeDtypeStruct((n_seq, shard, qkv_cols), F32),
+            jax.ShapeDtypeStruct((shard, 2 * HEAD_DIM), F32),
+            *(jax.ShapeDtypeStruct(w.shape, F32) for w in (w_query, w_key, w_value)),
             jax.ShapeDtypeStruct((shard, width), F32),
-            jax.ShapeDtypeStruct((shard, ff), F32),
-            jax.ShapeDtypeStruct((shard, ff), F32),
+            jax.ShapeDtypeStruct((shard, ff), BF16),
+            jax.ShapeDtypeStruct((shard, ff), BF16),
         ),
-        in_specs=[pl.BlockSpec(memory_space=pltpu.SMEM)] + [vmem] * 7 + [any_spec] * 5,
-        out_specs=(vmem,) * 6,
+        in_specs=[pl.BlockSpec(memory_space=pltpu.SMEM)] + [vmem] * 11 + [any_spec] * 7,
+        out_specs=(vmem,) * 9,
         scratch_shapes=[
-            line_rows,
-            pltpu.VMEM((2, n_seq, rows, n_seq // 2 * shard), BF16),
+            pltpu.VMEM((micro, n_seq, rows // micro, width), BF16),
+            pltpu.VMEM((2, micro, n_seq, rows // micro, n_seq // 2 * shard), BF16),
             pltpu.VMEM((width, qkv_cols), BF16),
             pltpu.VMEM(wo.shape, BF16),
             pltpu.VMEM((micro, length, q_cols), BF16),
             pltpu.VMEM((length, q_cols), F32),
             pltpu.VMEM((length, q_cols), F32),
             pltpu.VMEM((length, q_cols), F32),
+            pltpu.VMEM(bias_shape(length), F32),
             pltpu.VMEM((micro, length, qkv_cols), BF16),
             line_rows,
             *Scatter.buffers(n_seq, rows, width),
@@ -1246,9 +1470,10 @@
             pltpu.VMEM((n_dp, shard, width), BF16),
             pltpu.VMEM((n_dp, shard, width), BF16),
             pltpu.VMEM((shard, width), BF16),
-            pltpu.SemaphoreType.DMA((3,)),
+            pltpu.VMEM((rows, width), F32),
+            pltpu.SemaphoreType.DMA((5,)),
             pltpu.SemaphoreType.DMA((2,)),
-            *Gather.sems(n_seq),
+            *Gather.sems(n_seq) * micro,
             *Scatter.sems(n_seq),
             *Scatter.sems(n_seq),
             *Collect.sems(n_seq, n_dp),
@@ -1260,7 +1485,10 @@
         ),
         cost_estimate=pl.CostEstimate(flops=10**10, bytes_accessed=40 << 20, transcendentals=0),
         name="backward",
-    )(prefix, branch, q, kv, mixed, cos, sin, gains, pout, normed, wqkv, wo, dgu)
+    )(
+        prefix, branch, tok, q, kv, mixed, cos, sin, gains, w_query, w_key, w_value,
+        gh, hidden, pout, normed, wqkv, wo, dgu,
+    )
 
 
 def body(
@@ -1268,89 +1496,37 @@
 ):
     n_dp = lax.axis_size("dp")
     n_seq = lax.axis_size("seq")
-    both = ("dp", "seq")
     micro, span, width = tokens.shape
     shard = w_query.shape[0]
-    ff_block = w_down.shape[0]
-    length = span * n_seq
     rows = micro * span
-    repeat = n_seq // KV_HEADS
-    q_cols = HEADS // n_seq * HEAD_DIM
-
-    gain_attn, gain_mlp = attn_gain.astype(F32), mlp_gain.astype(F32)
-
-    def kv_blocks(w):
-        w = w.reshape(shard, KV_HEADS, 1, HEAD_DIM)
-        return jnp.broadcast_to(w, (shard, KV_HEADS, repeat, HEAD_DIM)).reshape(shard, n_seq, HEAD_DIM)
-
-    def scaled(blocks, gain):
-        return (blocks.astype(F32) * gain[:, None, None]).astype(BF16).transpose(1, 0, 2)
-
-    qkv_blocks = scaled(
-        jnp.concatenate([w_query.reshape(shard, n_seq, q_cols), kv_blocks(w_key), kv_blocks(w_value)], axis=2),
-        gain_attn,
+    cos, sin = rope_tables(span * n_seq, HEADS // n_seq * HEAD_DIM)
+    gains = jnp.concatenate(
+        [jnp.broadcast_to(g.astype(F32)[:, None], (shard, 2 * HEAD_DIM)) for g in (attn_gain, mlp_gain)], axis=1
     )
-
-    def ff_blocks(w):
-        w = w.reshape(shard, n_dp, n_seq, ff_block).transpose(0, 2, 1, 3)
-        return w.reshape(shard, n_seq, n_dp * ff_block)
-
-    gu_blocks = scaled(jnp.concatenate([ff_blocks(w_gate), ff_blocks(w_up)], axis=2), gain_mlp)
-
-    cos_one, sin_one = rope_table(jnp.arange(length, dtype=jnp.int32), HEAD_DIM)
-    half = HEAD_DIM // 2
-    sin_one = jnp.concatenate([-sin_one[:, :half], sin_one[:, half:]], axis=1)
-    count = q_cols // HEAD_DIM + 1
-    cos = jnp.concatenate([jnp.tile(cos_one, (1, count)), jnp.ones((length, HEAD_DIM), F32)], axis=1)
-    sin = jnp.concatenate([jnp.tile(sin_one, (1, count)), jnp.zeros((length, HEAD_DIM), F32)], axis=1)
-
     tok = tokens.reshape(rows, width)
     cot = cotangent.reshape(rows, width)
-    hidden, normed_mlp, q, kv, mixed, normed_all, cot_all, wqkv, wo, wgu, wd = attention_call(
-        prefix_len, tok, cot, cos, sin, qkv_blocks, gu_blocks, w_out, w_down, n_seq, n_dp
+    hidden, normed_mlp, q, kv, mixed, normed, cot_all, wqkv, wo, wgu, wd = attention_call(
+        prefix_len, tok, cot, cos, sin, gains, w_query, w_key, w_value, w_gate, w_up, w_out, w_down, n_seq, n_dp
     )
-    ge_mlp, out_part, dgu, w_down_grad = mlp_call(
-        normed_mlp, cot_all, wgu.reshape(width, -1), wd.reshape(-1, width), n_seq, n_dp
+    branch, grad_hidden, out_part, dgu, w_down_grad = mlp_call(
+        normed_mlp, hidden, cot_all, wgu.reshape(width, -1), wd.reshape(-1, width), n_seq, n_dp
     )
-
-    def norm_back(u, ge):
-        r = lax.rsqrt(jnp.mean(u * u, axis=1, keepdims=True) + EPSILON)
-        return r * ge - u * (r * r * r * jnp.mean(u * ge, axis=1, keepdims=True)), jnp.sum(ge * u * r, axis=0)
-
-    back, gain_mlp_part = norm_back(hidden, ge_mlp)
-    grad_hidden = cot.astype(F32) + back
-    gains = jnp.concatenate(
-        [jnp.broadcast_to(g[:, None], (shard, 2 * HEAD_DIM)) for g in (gain_attn, gain_mlp)], axis=1
+    block_out, input_grad, attn_gain_grad, *w_grads, w_out_grad, d_gate, d_up = backward_call(
+        prefix_len, branch, tok, q, kv, mixed, cos, sin, gains, w_query, w_key, w_value,
+        grad_hidden, hidden, out_part, normed, wqkv.reshape(width, -1), wo.reshape(-1, width), dgu.reshape(n_dp, n_seq, shard, -1),
     )
-    ge_attn, out_sum, qkv_grad, w_out_grad, w_gate_grad, w_up_grad = backward_call(
-        prefix_len, grad_hidden.astype(BF16), q, kv, mixed, cos, sin, gains, out_part, normed_all,
-        wqkv.reshape(width, -1), wo.reshape(-1, width), dgu.reshape(n_dp, n_seq, shard, -1),
-    )
-    block_out = (hidden + out_sum).astype(BF16)
-    back, gain_attn_part = norm_back(tok.astype(F32), ge_attn)
-    input_grad = grad_hidden + back
-
-    qkv_grad = qkv_grad.transpose(1, 0, 2)
-    w_query_grad = qkv_grad[:, :, :q_cols].reshape(shard, -1)
-
-    def kv_grad(values):
-        return values.reshape(shard, KV_HEADS, repeat, HEAD_DIM).sum(axis=2).reshape(shard, -1)
-
-    w_key_grad = kv_grad(qkv_grad[:, :, q_cols : q_cols + HEAD_DIM])
-    w_value_grad = kv_grad(qkv_grad[:, :, q_cols + HEAD_DIM :])
-    gain_parts = jnp.stack([gain_attn_part, gain_mlp_part], axis=1).reshape(n_dp * n_seq, shard, 2)
-    gain_grads = lax.all_to_all(gain_parts, both, split_axis=0, concat_axis=0, tiled=True).sum(axis=0)
+    mlp_gain_grad = jnp.sum(d_gate.astype(F32) * w_gate.astype(F32), axis=1)
+    mlp_gain_grad = mlp_gain_grad + jnp.sum(d_up.astype(F32) * w_up.astype(F32), axis=1)
+    gain_column = mlp_gain.astype(F32)[:, None]
     return (
         block_out.reshape(micro, span, width),
         input_grad.reshape(micro, span, width),
-        gain_grads[:, 0] / gain_attn,
-        w_query_grad,
-        w_key_grad,
-        w_value_grad,
+        attn_gain_grad[:, 0],
+        *w_grads,
         w_out_grad,
-        gain_grads[:, 1] / gain_mlp,
-        w_gate_grad,
-        w_up_grad,
+        mlp_gain_grad,
+        d_gate.astype(F32) * gain_column,
+        d_up.astype(F32) * gain_column,
         w_down_grad,
     )
 

time: 577 us -> 492 us (0.85)
  Pallas kernels: 518 us -> 470 us
  local copies, waits for them, and re-layouts: 29 us -> 8.12 us
  starting transfers between devices: 12.8 us -> 0 us
  other arithmetic: 15 us -> 5.64 us
    pallas_call x1, Pallas kernels: 222 us -> 193 us  [attention_call(): pl.pallas_call(functools.partial(attention_kernel, n_seq, n_dp), out_shap...]
    pallas_call x1, Pallas kernels: 176 us -> 160 us  [backward_call(): pl.pallas_call(functools.partial(backward_kernel, n_seq, n_dp), out_shape...]
    all_to_all x1 -> x0, starting transfers between devices: 12.8 us -> none  [body(): lax.all_to_all(gain_parts, both, split_axis=0, concat_axis=0, tiled=True)]
    reshape x8 -> x0, local copies, waits for them, and re-layouts: 8.38 us -> none  [the longest x2 2.55 us: ff_blocks(): return w.reshape(shard, n_seq, n_dp * ff_block)]
    another operation x11 -> x0, local copies, waits for them, and re-layouts: 6.04 us -> none  [the longest x4 4.31 us: kv_blocks(): jnp.broadcast_to(w, (shard, KV_HEADS, repeat, HEAD_DIM))]
  transfers between devices with their start and end apart: 1 -> 0, of which waited for: 0 -> 0; matrix products, arithmetic and copies ran while one was open for 1% -> 0% of each run, Pallas kernels for 0% -> 0%
where the time goes in v4:
time: 492 us; the launch traced here: 485 us
  Pallas kernels  470 us (96%)
  local copies, waits for them, and re-layouts  8.12 us (2%)
  other arithmetic  5.64 us (1%)
    pallas_call x1, Pallas kernels, attention_call(): pl.pallas_call(functools.partial(attention_kernel, n_seq, n_dp), out_shap...  193 us
    pallas_call x1, Pallas kernels, backward_call(): pl.pallas_call(functools.partial(backward_kernel, n_seq, n_dp), out_shape...  160 us
    pallas_call x1, Pallas kernels, mlp_call(): pl.pallas_call(functools.partial(mlp_kernel, n_seq, n_dp), out_shape=(jax...  118 us

profile of v4, /device:TPU:0, one launch (start us, length us, event | category | flops | bytes accessed | tf_op | source)
XLA Modules:
  0.0 485.4 jit_solution(7603395216371559712)
XLA Ops:
  0.6 0.7 broadcast_in_dim.4
  1.4 0.7 broadcast_in_dim.5
  2.1 0.6 pad_maximum_fusion.gains_ref
  2.7 193.2 %attention.1 = (f32[128,2048]{1,0:T(8,128)}, bf16[128,2048]{1,0:T(8,128)(2,1)}, bf16[2,512,256]{2,1,0:T(8,128)(2,1)}, bf16[2,512,128]{2,1,0:T(8,128)(2,1)}, bf16...) custom-call(s32[2]{0:T(128)} %prefix_ref.3, ...), custom_call_target="tpu_custom_call" | custom-call | flops 10000000000 | bytes 41943040 | tf_op jit(solution)/shard_map/attention/pallas_call | solution.py:1038
  195.9 117.6 %mlp.1 = (bf16[128,2048]{1,0:T(8,128)(2,1)}, f32[128,2048]{1,0:T(8,128)}, bf16[8,128,2048]{2,1,0:T(8,128)(2,1)}, bf16[2048,2048]{1,0:T(8,128)(2,1)}, f32[256,2048]{1,0:T(8,128)}) custom-call(bf16[128,2048]{1,0:T(8,128)(2,1)} %get-tuple-element.36.x_ref, f32[128,2048]{1,0:T(8,128)} %get-tuple-element.37.hidden_ref.hidden_hbm, ...), custom_call_target="tpu_custom_call" | custom-call | flops 38654705664 | bytes 41943040 | tf_op jit(solution)/shard_map/mlp/pallas_call | solution.py:1201
  313.5 0.0 copy-start.10
  313.5 0.0 copy-start.1
  313.5 0.0 copy-start.2
  313.5 159.7 %backward.1 = (bf16[128,2048]{1,0:T(8,128)(2,1)}, f32[128,2048]{1,0:T(8,128)}, f32[64,128]{1,0:T(8,128)}, f32[64,2048]{1,0:T(8,128)}, f32[64,512]{1,0:T(8,128)},...) custom-call(s32[2]{0:T(128)} %prefix_ref.3, ...), custom_call_target="tpu_custom_call" | custom-call | flops 10000000000 | bytes 41943040 | tf_op jit(solution)/shard_map/backward/pallas_call | solution.py:1438
  473.3 0.0 copy-done.10
  473.3 0.0 copy-done.1
  473.3 0.0 copy-done.2
  473.3 0.0 copy-start.9
  473.3 0.0 copy-start.6
  473.3 0.0 copy-start.3
  473.4 4.5 convert_multiply_fusion
  477.8 0.0 copy-start.5
  477.8 0.5 add.3
  478.4 0.0 copy-done.9
  478.4 0.6 slice_reduce_fusion
  479.0 0.0 copy-done.6
  479.0 0.0 copy-start.8
  479.0 0.0 copy-start.7
  479.0 0.0 copy-start.4
  479.0 0.8 copy.32
  479.8 0.0 copy-done.3
  479.8 0.0 copy-start
  479.8 1.0 copy.33
  480.8 0.0 copy-done.5
  480.8 0.8 copy.34
  481.6 0.0 copy-done.8
  481.6 0.7 copy.35
  482.2 0.0 copy-done.7
  482.2 0.7 copy.36
  482.9 0.0 copy-done.4
  482.9 0.8 copy.37
  483.7 0.0 copy-done
  483.7 1.3 copy.38
  (1 shorter events, 0.0 us)
Async XLA Ops:
  313.5 159.8 %copy-start.10 = (bf16[64]{0:T(256)(128)(2,1)S(1)}, bf16[64]{0:T(256)(128)(2,1)}, u32[]{:S(2)}) copy-start(bf16[64]{0:T(256)(128)(2,1)} %param.22) | copy-start | bytes 388
  313.5 159.8 %copy-start.1 = (bf16[64,8192]{1,0:T(8,128)(2,1)S(1)}, bf16[64,8192]{1,0:T(8,128)(2,1)}, u32[]{:S(2)}) copy-start(bf16[64,8192]{1,0:T(8,128)(2,1)} %w_gate_ref.1) | copy-start | bytes 3145732
  313.5 159.8 %copy-start.2 = (bf16[64,8192]{1,0:T(8,128)(2,1)S(1)}, bf16[64,8192]{1,0:T(8,128)(2,1)}, u32[]{:S(2)}) copy-start(bf16[64,8192]{1,0:T(8,128)(2,1)} %w_up_ref.1) | copy-start | bytes 3145732
  473.3 5.0 %copy-start.9 = (f32[64,128]{1,0:T(8,128)S(1)}, f32[64,128]{1,0:T(8,128)}, u32[]{:S(2)}) copy-start(f32[64,128]{1,0:T(8,128)} %get-tuple-element.53) | copy-start | bytes 98308
  473.3 5.7 %copy-start.6 = (bf16[128,2048]{1,0:T(8,128)(2,1)S(1)}, bf16[128,2048]{1,0:T(8,128)(2,1)}, u32[]{:S(2)}) copy-start(bf16[128,2048]{1,0:T(8,128)(2,1)} %get-tuple-element.51) | copy-start | bytes 1572868
  473.3 6.5 %copy-start.3 = (f32[128,2048]{1,0:T(8,128)S(1)}, f32[128,2048]{1,0:T(8,128)}, u32[]{:S(2)}) copy-start(f32[128,2048]{1,0:T(8,128)} %get-tuple-element.52) | copy-start | bytes 3145732
  477.8 2.9 copy-start.5
  479.0 2.6 copy-start.8
  479.0 3.2 copy-start.7
  479.0 3.9 copy-start.4
  479.8 3.9 copy-start

commit v5 on v4

--- a/solution.py
+++ b/solution.py
@@ -288,14 +288,11 @@
 
 
 class Spread:
-    def __init__(self, line, n_dp, relay, blocks, dst, own_sem, send_z, send_xy, recv, recv_half):
+    def __init__(self, line, n_dp, blocks, dst, own_sem, send_z, send_xy, recv):
         self.line, self.n_dp, self.blocks, self.dst = line, n_dp, blocks, dst
-        self.relay = relay and n_dp == 4
-        self.own_sem, self.send_z, self.send_xy, self.recv, self.recv_half = own_sem, send_z, send_xy, recv, recv_half
+        self.own_sem, self.send_z, self.send_xy, self.recv = own_sem, send_z, send_xy, recv
         self.n_seq = 2 * line.n_line
         self.d = lax.axis_index("dp")
-        self.square = Square()
-        self.half = blocks.shape[1] // 2
 
     @staticmethod
     def sems(n_seq, n_dp):
@@ -304,7 +301,6 @@
             pltpu.SemaphoreType.DMA((n_seq,)),
             pltpu.SemaphoreType.DMA((n_seq, n_dp)),
             pltpu.SemaphoreType.DMA((n_dp, n_seq)),
-            pltpu.SemaphoreType.DMA((n_seq,)),
         ]
 
     def source(self, j):
@@ -333,38 +329,14 @@
     def over(self, source, own=False):
         src = self.blocks.at[self.line.s] if own else self.dst.at[self.d, source]
         peers = [lax.rem(self.d + k, self.n_dp) for k in range(1, self.n_dp)]
-        if self.relay:
-            peers = [self.square.first, self.square.second]
         return [
-            self.to_dp(src, self.dst.at[self.d, source], self.send_xy.at[source, k + 1], self.recv.at[self.d, source], peer)
+            self.to_dp(src, self.dst.at[self.d, source], self.send_xy.at[source, k], self.recv.at[self.d, source], peer)
             for k, peer in enumerate(peers)
         ]
 
     def landed(self, d, source):
         block = self.dst.at[d, source]
         return self.to_dp(block, block, self.send_z.at[0], self.recv.at[d, source], d)
-
-    def halves(self, source):
-        low, high = pl.ds(0, self.half), pl.ds(self.half, self.half)
-        one = self.dst.at[self.square.first, source, low]
-        two = self.dst.at[self.square.second, source, high]
-        return (
-            self.to_dp(one, one, self.send_xy.at[source, 3], self.recv.at[self.square.first, source], self.square.second),
-            self.to_dp(two, two, self.send_xy.at[source, 0], self.recv_half.at[source], self.square.first),
-        )
-
-    def pass_on(self, j):
-        if not self.relay:
-            return
-
-        @pl.when(j < self.n_seq)
-        def _():
-            source = self.source(j)
-            one, two = self.halves(source)
-            self.landed(self.square.first, source).wait_recv()
-            one.start()
-            self.landed(self.square.second, source).wait_recv()
-            two.start()
 
     def begin(self, end):
         n = self.line
@@ -393,15 +365,8 @@
     def arrive(self):
         @pl.loop(0, self.n_seq)
         def _(source):
-            if self.relay:
-                low, high = pl.ds(0, self.half), pl.ds(self.half, self.half)
-                one = self.dst.at[self.square.across, source, low]
-                two = self.dst.at[self.square.across, source, high]
-                self.to_dp(one, one, self.send_z.at[0], self.recv.at[self.square.across, source], self.d).wait_recv()
-                self.to_dp(two, two, self.send_z.at[0], self.recv_half.at[source], self.d).wait_recv()
-            else:
-                for k in range(1, self.n_dp):
-                    self.landed(lax.rem(self.d + k, self.n_dp), source).wait_recv()
+            for k in range(1, self.n_dp):
+                self.landed(lax.rem(self.d + k, self.n_dp), source).wait_recv()
 
         self.own().wait()
 
@@ -413,9 +378,6 @@
             pl.when(j != n.s)(lambda: self.hop(j).wait_send())
             for copy in self.over(j):
                 copy.wait_send()
-            if self.relay:
-                for copy in self.halves(j):
-                    copy.wait_send()
 
 
 class Copies:
@@ -874,8 +836,8 @@
     gathers = [Gather(n, full, *take(3), m=m) for m in range(micro)]
     scatters = [Scatter(n, part, sib, rcv, *take(4), m=m) for m in range(micro)]
     gather_cot = Gather(n, cot, *take(3))
-    qkv_w = Spread(n, n_dp, False, qkvb, wqkv, *take(5))
-    gu_w = Spread(n, n_dp, True, gub, wgu_hbm, *take(5))
+    qkv_w = Spread(n, n_dp, qkvb, wqkv, *take(4))
+    gu_w = Spread(n, n_dp, gub, wgu_hbm, *take(4))
     out_w = OutRows(n, n_dp, wo_own, wo, *take(4))
     down_w = Copies(n_dp, wd_own, wd_hbm, *take(3))
 
@@ -919,7 +881,6 @@
     half_line = length // span // 2
     heads = q_cols // HEAD_DIM
     q_tile = min(length, QUERY_TILE)
-    steps = n.last
 
     def project(m):
         @pl.loop(0, 2)
@@ -948,7 +909,7 @@
             else:
                 acc[at, :] += mixed
 
-    sent = passed = 0
+    sent = 0
     for m in range(micro):
         project(m)
         fill_bias(bias, prefix_ref[m], 0, length)
@@ -956,14 +917,13 @@
             if m + 1 < micro:
                 for j in range(*spread_work(n.n_line, heads, h)):
                     gathers[m + 1].visit(n.order(j))
-            if m > 0:
-                if h == 0:
-                    down_w.pass_on()
-                for time in range(*spread_work(steps, heads, h)):
-                    scatters[m - 1].step(time)
-                    sent += 1
-                    gu_w.forward_one(sent, AHEAD)
+            if m == 1 and h == 0:
+                down_w.pass_on()
             attend(m, h)
+            done = m * heads + h
+            for _ in range(*spread_work(n_seq - 1, micro * heads - 1, done - 1) if done else (0,)):
+                sent += 1
+                gu_w.forward_one(sent, AHEAD)
         mixed_ref[m] = acc[...].astype(BF16)
         if m == 0:
             out_w.arrive()
@@ -981,14 +941,10 @@
 
     pltpu.make_async_copy(full, normed_hbm, save_sem.at[0]).start()
     gather_cot.visit(n.l)
-    rest = n_seq - 1 - sent
     for time in range(n.last):
-        scatters[-1].step(time)
-        for j in range(*spread_work(rest, n.last, time)):
-            gu_w.forward_one(sent + 1 + j, AHEAD)
+        for scatter in scatters:
+            scatter.step(time)
         gather_cot.visit(n.order(time + 1))
-        for j in range(*spread_work(n_seq, n.last, time)):
-            gu_w.pass_on(j)
     pltpu.make_async_copy(cot, cot_hbm, save_sem.at[3]).start()
     for m in range(micro):
         at = slice(m * span, (m + 1) * span)
@@ -1121,10 +1077,10 @@
             part[two, :, cols] = value.astype(BF16).reshape(2, rows, TILE)
 
     scatter.begin()
+    scatter.step(0)
     owners = TILE // dwd.shape[1]
 
-    @pl.loop(0, ff // TILE)
-    def _(f):
+    def down_grad(f):
         cols = pl.ds(pl.multiple_of(f * TILE, TILE), TILE)
         at = pl.ds(f * owners, owners)
         for w in range(0, width, 2 * TILE):
@@ -1132,7 +1088,17 @@
             value = tn(act[:, cols], span).astype(BF16)
             dwd[at, :, w : w + 2 * TILE] = value.reshape(owners, dwd.shape[1], 2 * TILE)
 
-    down.begin()
+    if owners == 1:
+
+        @pl.loop(1, n_dp + 1)
+        def _(k):
+            down_grad(lax.rem(down.d + k, n_dp))
+            pl.when(k < n_dp)(lambda: down.copy(k, down.d).start())
+
+        down.own().start()
+    else:
+        pl.loop(0, ff // TILE)(down_grad)
+        down.begin()
 
     def gate_up_grads(first, end):
         @pl.loop(first, end)
@@ -1177,7 +1143,8 @@
                 ).wait()
 
     for time in range(n.last):
-        scatter.step(time)
+        if time > 0:
+            scatter.step(time)
         if time == 0:
             out_parts(0, n.n_line)
         gate_up_grads(*spread_work(width // TILE, n.last, time))

time: 492 us -> 476 us (0.967)
  Pallas kernels: 470 us -> 452 us
    pallas_call x1, Pallas kernels: 193 us -> 177 us  [attention_call(): pl.pallas_call(functools.partial(attention_kernel, n_seq, n_dp), out_shap...]
where the time goes in v5:
time: 476 us; the launch traced here: 467 us
  Pallas kernels  452 us (95%)
  local copies, waits for them, and re-layouts  8.12 us (2%)
  other arithmetic  5.64 us (1%)
    pallas_call x1, Pallas kernels, attention_call(): pl.pallas_call(functools.partial(attention_kernel, n_seq, n_dp), out_shap...  177 us
    pallas_call x1, Pallas kernels, backward_call(): pl.pallas_call(functools.partial(backward_kernel, n_seq, n_dp), out_shape...  159 us
    pallas_call x1, Pallas kernels, mlp_call(): pl.pallas_call(functools.partial(mlp_kernel, n_seq, n_dp), out_shape=(jax...  115 us

profile of v5, /device:TPU:0, one launch (start us, length us, event | category | flops | bytes accessed | tf_op | source)
XLA Modules:
  0.0 466.7 jit_solution(3310384812164980006)
XLA Ops:
  0.6 0.7 broadcast_in_dim.4
  1.4 0.7 broadcast_in_dim.5
  2.1 0.6 pad_maximum_fusion.gains_ref
  2.7 177.0 %attention.1 = (f32[128,2048]{1,0:T(8,128)}, bf16[128,2048]{1,0:T(8,128)(2,1)}, bf16[2,512,256]{2,1,0:T(8,128)(2,1)}, bf16[2,512,128]{2,1,0:T(8,128)(2,1)}, bf16...) custom-call(s32[2]{0:T(128)} %prefix_ref.3, ...), custom_call_target="tpu_custom_call" | custom-call | flops 10000000000 | bytes 41943040 | tf_op jit(solution)/shard_map/attention/pallas_call | solution.py:994
  179.7 115.4 %mlp.1 = (bf16[128,2048]{1,0:T(8,128)(2,1)}, f32[128,2048]{1,0:T(8,128)}, bf16[8,128,2048]{2,1,0:T(8,128)(2,1)}, bf16[2048,2048]{1,0:T(8,128)(2,1)}, f32[256,2048]{1,0:T(8,128)}) custom-call(bf16[128,2048]{1,0:T(8,128)(2,1)} %get-tuple-element.36.x_ref, f32[128,2048]{1,0:T(8,128)} %get-tuple-element.37.hidden_ref.hidden_hbm, ...), custom_call_target="tpu_custom_call" | custom-call | flops 38654705664 | bytes 41943040 | tf_op jit(solution)/shard_map/mlp/pallas_call | solution.py:1168
  295.1 0.0 copy-start.10
  295.2 0.0 copy-start.1
  295.2 0.0 copy-start.2
  295.2 159.4 %backward.1 = (bf16[128,2048]{1,0:T(8,128)(2,1)}, f32[128,2048]{1,0:T(8,128)}, f32[64,128]{1,0:T(8,128)}, f32[64,2048]{1,0:T(8,128)}, f32[64,512]{1,0:T(8,128)},...) custom-call(s32[2]{0:T(128)} %prefix_ref.3, ...), custom_call_target="tpu_custom_call" | custom-call | flops 10000000000 | bytes 41943040 | tf_op jit(solution)/shard_map/backward/pallas_call | solution.py:1405
  454.5 0.0 copy-done.10
  454.6 0.0 copy-done.1
  454.6 0.0 copy-done.2
  454.6 0.0 copy-start.9
  454.6 0.0 copy-start.6
  454.6 0.0 copy-start.3
  454.6 4.5 convert_multiply_fusion
  459.1 0.0 copy-start.5
  459.1 0.5 add.3
  459.6 0.0 copy-done.9
  459.6 0.6 slice_reduce_fusion
  460.3 0.0 copy-done.6
  460.3 0.0 copy-start.8
  460.3 0.0 copy-start.7
  460.3 0.0 copy-start.4
  460.3 0.8 copy.32
  461.1 0.0 copy-done.3
  461.1 0.0 copy-start
  461.1 1.0 copy.33
  462.0 0.0 copy-done.5
  462.0 0.8 copy.34
  462.8 0.0 copy-done.8
  462.8 0.7 copy.35
  463.5 0.0 copy-done.7
  463.5 0.7 copy.36
  464.1 0.0 copy-done.4
  464.2 0.8 copy.37
  464.9 0.0 copy-done
  464.9 1.3 copy.38
  (1 shorter events, 0.0 us)
Async XLA Ops:
  295.1 159.4 %copy-start.10 = (bf16[64]{0:T(256)(128)(2,1)S(1)}, bf16[64]{0:T(256)(128)(2,1)}, u32[]{:S(2)}) copy-start(bf16[64]{0:T(256)(128)(2,1)} %param.22) | copy-start | bytes 388
  295.2 159.4 %copy-start.1 = (bf16[64,8192]{1,0:T(8,128)(2,1)S(1)}, bf16[64,8192]{1,0:T(8,128)(2,1)}, u32[]{:S(2)}) copy-start(bf16[64,8192]{1,0:T(8,128)(2,1)} %w_gate_ref.1) | copy-start | bytes 3145732
  295.2 159.4 %copy-start.2 = (bf16[64,8192]{1,0:T(8,128)(2,1)S(1)}, bf16[64,8192]{1,0:T(8,128)(2,1)}, u32[]{:S(2)}) copy-start(bf16[64,8192]{1,0:T(8,128)(2,1)} %w_up_ref.1) | copy-start | bytes 3145732
  454.6 5.0 %copy-start.9 = (f32[64,128]{1,0:T(8,128)S(1)}, f32[64,128]{1,0:T(8,128)}, u32[]{:S(2)}) copy-start(f32[64,128]{1,0:T(8,128)} %get-tuple-element.53) | copy-start | bytes 98308
  454.6 5.7 %copy-start.6 = (bf16[128,2048]{1,0:T(8,128)(2,1)S(1)}, bf16[128,2048]{1,0:T(8,128)(2,1)}, u32[]{:S(2)}) copy-start(bf16[128,2048]{1,0:T(8,128)(2,1)} %get-tuple-element.51) | copy-start | bytes 1572868
  454.6 6.5 %copy-start.3 = (f32[128,2048]{1,0:T(8,128)S(1)}, f32[128,2048]{1,0:T(8,128)}, u32[]{:S(2)}) copy-start(f32[128,2048]{1,0:T(8,128)} %get-tuple-element.52) | copy-start | bytes 3145732
  459.1 2.9 copy-start.5
  460.3 2.6 copy-start.8
  460.3 3.2 copy-start.7
  460.3 3.9 copy-start.4
  461.1 3.9 copy-start

commit v6 on v5

--- a/solution.py
+++ b/solution.py
@@ -735,7 +735,7 @@
         out[...] = total
 
 
-def greet_all(line, n_dp, relay):
+def greet_all(line, n_dp, relay, between=None):
     barrier = pltpu.get_barrier_semaphore()
     n_seq = 2 * line.n_line
     d = lax.axis_index("dp")
@@ -745,6 +745,8 @@
         pl.semaphore_signal(barrier, 1, device_id={"dp": lax.rem(d + k, n_dp)}, device_id_type=MESH)
 
     if relay is None:
+        if between is not None:
+            between()
         pl.semaphore_wait(barrier, n_seq + n_dp - 2)
         return
 
@@ -753,6 +755,8 @@
         for device in ((relay.slot, relay.target), (relay.owner_d, relay.owner_s)):
             pl.semaphore_signal(barrier, 1, device_id=device, device_id_type=MESH)
 
+    if between is not None:
+        between()
     pl.semaphore_wait(barrier, n_seq + n_dp - 2 + jnp.where(relay.moves, 2, 0))
 
 
@@ -825,11 +829,18 @@
     span = rows // micro
     cols_all = wqkv.shape[3]
     pair = 2 * rows
-    tok = tok_ref[...].astype(F32)
-    normed = (tok * lax.rsqrt(jnp.mean(tok * tok, axis=1, keepdims=True) + EPSILON)).astype(BF16)
-    for m in range(micro):
-        full[m, n.s] = normed[m * span : (m + 1) * span]
-    cot[n.s] = cot_ref[...]
+
+    def prepare():
+        tok = tok_ref[...].astype(F32)
+        normed = (tok * lax.rsqrt(jnp.mean(tok * tok, axis=1, keepdims=True) + EPSILON)).astype(BF16)
+        for m in range(micro):
+            full[m, n.s] = normed[m * span : (m + 1) * span]
+        cot[n.s] = cot_ref[...]
+        for t in range(n_seq):
+            head = slice(t // repeat * HEAD_DIM, (t // repeat + 1) * HEAD_DIM)
+            qkvb[t, :, :q_cols] = (w_query_ref[:, t * q_cols : (t + 1) * q_cols].astype(F32) * gain_attn).astype(BF16)
+            key_value = jnp.concatenate([w_key_ref[:, head], w_value_ref[:, head]], axis=1)
+            qkvb[t, :, q_cols:] = (key_value.astype(F32) * gain_attn).astype(BF16)
 
     sems = list(sems)
     take = lambda count: [sems.pop(0) for _ in range(count)]
@@ -845,13 +856,8 @@
     ff_block = wd_own.shape[0]
     gain_attn = gains_ref[:, :1]
     gain_mlp = gains_ref[:, 2 * HEAD_DIM : 2 * HEAD_DIM + 1]
-    for t in range(n_seq):
-        head = slice(t // repeat * HEAD_DIM, (t // repeat + 1) * HEAD_DIM)
-        qkvb[t, :, :q_cols] = (w_query_ref[:, t * q_cols : (t + 1) * q_cols].astype(F32) * gain_attn).astype(BF16)
-        key_value = jnp.concatenate([w_key_ref[:, head], w_value_ref[:, head]], axis=1)
-        qkvb[t, :, q_cols:] = (key_value.astype(F32) * gain_attn).astype(BF16)
-
-    greet_all(n, n_dp, out_w)
+
+    greet_all(n, n_dp, out_w, prepare)
     qkv_w.begin(n_seq)
     gathers[0].begin()
     out_w.begin()
@@ -1039,10 +1045,13 @@
             [(wgu_hbm, wgu), (cot_hbm, cot), (wd_hbm, wd)]
         )
     ]
-    for load in loads:
-        load.start()
-    full[n.s] = x_ref[...]
-    greet_all(n, n_dp, None)
+
+    def prepare():
+        for load in loads:
+            load.start()
+        full[n.s] = x_ref[...]
+
+    greet_all(n, n_dp, None, prepare)
     gather = Gather(n, full, *sems[:3])
     scatter = Scatter(n, part, sib, rcv, *sems[3:7])
     down = RowSum(n_dp, dwd, land, *sems[7:10])
@@ -1053,7 +1062,10 @@
     @pl.loop(0, n.n_line)
     def _(j):
         chip = n.order(j)
-        gather.visit(chip)
+        near = 2 * jnp.minimum(n.l, n.last - n.l)
+        odd = lax.rem(j, 2) == 1
+        pl.when((j == 0) | odd | (j > near))(lambda: gather.visit(chip))
+        pl.when(odd & (j < near))(lambda: gather.visit(n.order(j + 1)))
         at = pl.ds(pl.multiple_of(chip * pair, pair), pair)
         two = pl.ds(pl.multiple_of(2 * chip, 2), 2)
 
@@ -1224,10 +1236,13 @@
             [(pout_hbm, part), (wo_hbm, wo), (wqkv_hbm, wqkv), (hidden_hbm, total), (gh_hbm, in_ref)]
         )
     ]
-    for load in loads:
-        load.start()
-    for m in range(micro):
-        full[m, n.s] = branch_ref[m * span : (m + 1) * span, :]
+
+    def prepare():
+        for load in loads:
+            load.start()
+        for m in range(micro):
+            full[m, n.s] = branch_ref[m * span : (m + 1) * span, :]
+
     sems = list(sems)
     take = lambda count: [sems.pop(0) for _ in range(count)]
     gathers = [Gather(n, full, *take(3), m=m) for m in range(micro)]
@@ -1236,7 +1251,7 @@
     gu_sum = Collect(n, n_dp, dgu_hbm, land_gu, final_gu, *take(5))
     qkv_sum = Collect(n, n_dp, dqkv, land_qkv, final_qkv, *take(5))
     out_sum = OutSum(n, n_dp, dwo, land_o, final_o, *take(5))
-    greet_all(n, n_dp, out_sum)
+    greet_all(n, n_dp, out_sum, prepare)
     gathers[0].begin()
     gu_sum.begin(3)
     loads[0].wait()
@@ -1325,6 +1340,7 @@
             part[:, m * span : (m + 1) * span, at] = value.astype(BF16).reshape(n_seq, span, TILE)
 
     scatter.begin()
+    scatter.step(0)
 
     half = n_seq // 2
     depth = half * shard
@@ -1350,7 +1366,8 @@
     qkv_sum.begin(n_seq)
     out_sum.reduce()
     for time in range(n.last):
-        scatter.step(time)
+        if time > 0:
+            scatter.step(time)
         first, end = spread_work(n_seq - late, n.last, time)
         gu_sum.reduce(late + first, late + end)
     qkv_sum.reduce(0, n_seq)

time: 476 us -> 471 us (0.989)
  Pallas kernels: 452 us -> 447 us
    pallas_call x1, Pallas kernels: 115 us -> 110 us  [mlp_call(): pl.pallas_call(functools.partial(mlp_kernel, n_seq, n_dp), out_shape=(jax...]
where the time goes in v6:
time: 471 us; the launch traced here: 462 us
  Pallas kernels  447 us (95%)
  local copies, waits for them, and re-layouts  8.12 us (2%)
  other arithmetic  5.64 us (1%)
    pallas_call x1, Pallas kernels, attention_call(): pl.pallas_call(functools.partial(attention_kernel, n_seq, n_dp), out_shap...  177 us
    pallas_call x1, Pallas kernels, backward_call(): pl.pallas_call(functools.partial(backward_kernel, n_seq, n_dp), out_shape...  160 us
    pallas_call x1, Pallas kernels, mlp_call(): pl.pallas_call(functools.partial(mlp_kernel, n_seq, n_dp), out_shape=(jax...  110 us

profile of v6, /device:TPU:0, one launch (start us, length us, event | category | flops | bytes accessed | tf_op | source)
XLA Modules:
  0.0 462.4 jit_solution(5418850525013607754)
XLA Ops:
  0.6 0.7 broadcast_in_dim.4
  1.4 0.7 broadcast_in_dim.5
  2.1 0.6 pad_maximum_fusion.gains_ref
  2.7 176.7 %attention.1 = (f32[128,2048]{1,0:T(8,128)}, bf16[128,2048]{1,0:T(8,128)(2,1)}, bf16[2,512,256]{2,1,0:T(8,128)(2,1)}, bf16[2,512,128]{2,1,0:T(8,128)(2,1)}, bf16...) custom-call(s32[2]{0:T(128)} %prefix_ref.3, ...), custom_call_target="tpu_custom_call" | custom-call | flops 10000000000 | bytes 41943040 | tf_op jit(solution)/shard_map/attention/pallas_call | solution.py:1000
  179.5 110.3 %mlp.1 = (bf16[128,2048]{1,0:T(8,128)(2,1)}, f32[128,2048]{1,0:T(8,128)}, bf16[8,128,2048]{2,1,0:T(8,128)(2,1)}, bf16[2048,2048]{1,0:T(8,128)(2,1)}, f32[256,2048]{1,0:T(8,128)}) custom-call(bf16[128,2048]{1,0:T(8,128)(2,1)} %get-tuple-element.36.x_ref, f32[128,2048]{1,0:T(8,128)} %get-tuple-element.37.hidden_ref.hidden_hbm, ...), custom_call_target="tpu_custom_call" | custom-call | flops 38654705664 | bytes 41943040 | tf_op jit(solution)/shard_map/mlp/pallas_call | solution.py:1180
  289.8 0.0 copy-start.10
  289.8 0.0 copy-start.1
  289.8 0.0 copy-start.2
  289.8 160.5 %backward.1 = (bf16[128,2048]{1,0:T(8,128)(2,1)}, f32[128,2048]{1,0:T(8,128)}, f32[64,128]{1,0:T(8,128)}, f32[64,2048]{1,0:T(8,128)}, f32[64,512]{1,0:T(8,128)},...) custom-call(s32[2]{0:T(128)} %prefix_ref.3, ...), custom_call_target="tpu_custom_call" | custom-call | flops 10000000000 | bytes 41943040 | tf_op jit(solution)/shard_map/backward/pallas_call | solution.py:1422
  450.3 0.0 copy-done.10
  450.3 0.0 copy-done.1
  450.3 0.0 copy-done.2
  450.3 0.0 copy-start.9
  450.3 0.0 copy-start.6
  450.3 0.0 copy-start.3
  450.3 4.5 convert_multiply_fusion
  454.8 0.0 copy-start.5
  454.8 0.5 add.3
  455.3 0.0 copy-done.9
  455.3 0.6 slice_reduce_fusion
  456.0 0.0 copy-done.6
  456.0 0.0 copy-start.8
  456.0 0.0 copy-start.7
  456.0 0.0 copy-start.4
  456.0 0.8 copy.32
  456.8 0.0 copy-done.3
  456.8 0.0 copy-start
  456.8 1.0 copy.33
  457.8 0.0 copy-done.5
  457.8 0.8 copy.34
  458.6 0.0 copy-done.8
  458.6 0.7 copy.35
  459.2 0.0 copy-done.7
  459.2 0.7 copy.36
  459.9 0.0 copy-done.4
  459.9 0.8 copy.37
  460.7 0.0 copy-done
  460.7 1.3 copy.38
  (1 shorter events, 0.0 us)
Async XLA Ops:
  289.8 160.5 %copy-start.10 = (bf16[64]{0:T(256)(128)(2,1)S(1)}, bf16[64]{0:T(256)(128)(2,1)}, u32[]{:S(2)}) copy-start(bf16[64]{0:T(256)(128)(2,1)} %param.22) | copy-start | bytes 388
  289.8 160.5 %copy-start.1 = (bf16[64,8192]{1,0:T(8,128)(2,1)S(1)}, bf16[64,8192]{1,0:T(8,128)(2,1)}, u32[]{:S(2)}) copy-start(bf16[64,8192]{1,0:T(8,128)(2,1)} %w_gate_ref.1) | copy-start | bytes 3145732
  289.8 160.5 %copy-start.2 = (bf16[64,8192]{1,0:T(8,128)(2,1)S(1)}, bf16[64,8192]{1,0:T(8,128)(2,1)}, u32[]{:S(2)}) copy-start(bf16[64,8192]{1,0:T(8,128)(2,1)} %w_up_ref.1) | copy-start | bytes 3145732
  450.3 5.0 %copy-start.9 = (f32[64,128]{1,0:T(8,128)S(1)}, f32[64,128]{1,0:T(8,128)}, u32[]{:S(2)}) copy-start(f32[64,128]{1,0:T(8,128)} %get-tuple-element.53) | copy-start | bytes 98308
  450.3 5.7 %copy-start.6 = (bf16[128,2048]{1,0:T(8,128)(2,1)S(1)}, bf16[128,2048]{1,0:T(8,128)(2,1)}, u32[]{:S(2)}) copy-start(bf16[128,2048]{1,0:T(8,128)(2,1)} %get-tuple-element.51) | copy-start | bytes 1572868
  450.3 6.5 %copy-start.3 = (f32[128,2048]{1,0:T(8,128)S(1)}, f32[128,2048]{1,0:T(8,128)}, u32[]{:S(2)}) copy-start(f32[128,2048]{1,0:T(8,128)} %get-tuple-element.52) | copy-start | bytes 3145732
  454.8 2.9 copy-start.5
  456.0 2.6 copy-start.8
  456.0 3.2 copy-start.7
  456.0 3.9 copy-start.4
  456.8 3.9 copy-start

commit v7 on v6

--- a/solution.py
+++ b/solution.py
@@ -1475,6 +1475,81 @@
     )
 
 
+def finish_kernel(count, gains_ref, *refs):
+    moved, (d_gate, d_up, w_gate, w_up) = refs[:count], refs[count : count + 4]
+    targets = refs[count + 4 : 2 * count + 4]
+    gate_hbm, up_hbm, dots_ref = refs[2 * count + 4 : 2 * count + 7]
+    held = refs[2 * count + 7 : 3 * count + 7]
+    grads, weights, scaled, acc, move_sem, out_sem, load_sem, save_sem = refs[3 * count + 7 :]
+    loads = [
+        pltpu.make_async_copy(src, dst.at[i], load_sem.at[i, k])
+        for i, pair in enumerate(((d_gate, w_gate), (d_up, w_up)))
+        for k, (src, dst) in enumerate(zip(pair, (grads, weights)))
+    ]
+    moves = [
+        pltpu.make_async_copy(src, mid, move_sem.at[i]) for i, (src, mid) in enumerate(zip(moved, held))
+    ]
+    outs = [
+        pltpu.make_async_copy(mid, dst, out_sem.at[i]) for i, (mid, dst) in enumerate(zip(held, targets))
+    ]
+    for copy in loads + moves:
+        copy.start()
+    gain = gains_ref[:, 2 * HEAD_DIM : 2 * HEAD_DIM + 1]
+    shard, ff = grads.shape[1:]
+    acc[...] = jnp.zeros_like(acc)
+    for move, out in zip(moves, outs):
+        move.wait()
+        out.start()
+    saves = []
+    for i, dst in enumerate((gate_hbm, up_hbm)):
+        loads[2 * i].wait()
+        loads[2 * i + 1].wait()
+
+        @pl.loop(0, ff // (2 * TILE))
+        def _(f):
+            cols = pl.ds(pl.multiple_of(f * 2 * TILE, 2 * TILE), 2 * TILE)
+            value = grads[i, :, cols].astype(F32)
+            scaled[i, :, cols] = value * gain
+            acc[...] += value * weights[i, :, cols].astype(F32)
+
+        saves.append(pltpu.make_async_copy(scaled.at[i], dst, save_sem.at[i]))
+        saves[-1].start()
+    dots_ref[...] = jnp.sum(acc[...], axis=1, keepdims=True) * jnp.ones_like(dots_ref)
+    for copy in outs + saves:
+        copy.wait()
+
+
+def finish_call(gains, moved, d_gate, d_up, w_gate, w_up):
+    count = len(moved)
+    any_spec = pl.BlockSpec(memory_space=pl.ANY)
+    vmem = pl.BlockSpec(memory_space=pltpu.VMEM)
+    shape = d_gate.shape
+    return pl.pallas_call(
+        functools.partial(finish_kernel, count),
+        out_shape=(
+            *(jax.ShapeDtypeStruct(v.shape, v.dtype) for v in moved),
+            jax.ShapeDtypeStruct(shape, F32),
+            jax.ShapeDtypeStruct(shape, F32),
+            jax.ShapeDtypeStruct((shape[0], 2 * HEAD_DIM), F32),
+        ),
+        in_specs=[vmem] + [any_spec] * (count + 4),
+        out_specs=(any_spec,) * (count + 2) + (vmem,),
+        scratch_shapes=[
+            *(pltpu.VMEM(v.shape, v.dtype) for v in moved),
+            pltpu.VMEM((2, *shape), BF16),
+            pltpu.VMEM((2, *shape), BF16),
+            pltpu.VMEM((2, *shape), F32),
+            pltpu.VMEM((shape[0], 2 * TILE), F32),
+            pltpu.SemaphoreType.DMA((count,)),
+            pltpu.SemaphoreType.DMA((count,)),
+            pltpu.SemaphoreType.DMA((2, 2)),
+            pltpu.SemaphoreType.DMA((2,)),
+        ],
+        compiler_params=pltpu.CompilerParams(vmem_limit_bytes=VMEM_LIMIT),
+        name="results",
+    )(gains, *moved, d_gate, d_up, w_gate, w_up)
+
+
 def body(
     tokens, cotangent, prefix_len, attn_gain, w_query, w_key, w_value, w_out, mlp_gain, w_gate, w_up, w_down
 ):
@@ -1499,18 +1574,18 @@
         prefix_len, branch, tok, q, kv, mixed, cos, sin, gains, w_query, w_key, w_value,
         grad_hidden, hidden, out_part, normed, wqkv.reshape(width, -1), wo.reshape(-1, width), dgu.reshape(n_dp, n_seq, shard, -1),
     )
-    mlp_gain_grad = jnp.sum(d_gate.astype(F32) * w_gate.astype(F32), axis=1)
-    mlp_gain_grad = mlp_gain_grad + jnp.sum(d_up.astype(F32) * w_up.astype(F32), axis=1)
-    gain_column = mlp_gain.astype(F32)[:, None]
+    moved = (block_out, input_grad, *w_grads, w_out_grad, w_down_grad)
+    *moved, w_gate_grad, w_up_grad, mlp_gain_grad = finish_call(gains, moved, d_gate, d_up, w_gate, w_up)
+    block_out, input_grad, *w_grads, w_out_grad, w_down_grad = moved
     return (
         block_out.reshape(micro, span, width),
         input_grad.reshape(micro, span, width),
         attn_gain_grad[:, 0],
         *w_grads,
         w_out_grad,
-        mlp_gain_grad,
-        d_gate.astype(F32) * gain_column,
-        d_up.astype(F32) * gain_column,
+        mlp_gain_grad[:, 0],
+        w_gate_grad,
+        w_up_grad,
         w_down_grad,
     )
 

time: 471 us -> 471 us (level)
  Pallas kernels: 447 us -> 457 us
  local copies, waits for them, and re-layouts: 8.12 us -> 2.85 us
  other arithmetic: 5.64 us -> 0.65 us
    pallas_call x0 -> x1, Pallas kernels: none -> 9.99 us  [finish_call(): pl.pallas_call(functools.partial(finish_kernel, count), out_shape=(*(jax....]
    unnamed x29 -> x2, local copies, waits for them, and re-layouts: 6.03 us -> 0.01 us
where the time goes in v7:
time: 471 us; the launch traced here: 462 us
  Pallas kernels  457 us (97%)
    pallas_call x1, Pallas kernels, attention_call(): pl.pallas_call(functools.partial(attention_kernel, n_seq, n_dp), out_shap...  177 us
    pallas_call x1, Pallas kernels, backward_call(): pl.pallas_call(functools.partial(backward_kernel, n_seq, n_dp), out_shape...  161 us
    pallas_call x1, Pallas kernels, mlp_call(): pl.pallas_call(functools.partial(mlp_kernel, n_seq, n_dp), out_shape=(jax...  110 us
    pallas_call x1, Pallas kernels, finish_call(): pl.pallas_call(functools.partial(finish_kernel, count), out_shape=(*(jax....  9.99 us

profile of v7, /device:TPU:0, one launch (start us, length us, event | category | flops | bytes accessed | tf_op | source)
XLA Modules:
  0.0 462.1 jit_solution(16724869348830511040)
XLA Ops:
  0.6 0.7 broadcast_in_dim.4
  1.4 0.7 broadcast_in_dim.5
  2.1 0.7 pad_maximum_fusion.gains_ref
  2.8 176.7 %attention.1 = (f32[128,2048]{1,0:T(8,128)}, bf16[128,2048]{1,0:T(8,128)(2,1)}, bf16[2,512,256]{2,1,0:T(8,128)(2,1)}, bf16[2,512,128]{2,1,0:T(8,128)(2,1)}, bf16...) custom-call(s32[2]{0:T(128)} %prefix_ref.3, ...), custom_call_target="tpu_custom_call" | custom-call | flops 10000000000 | bytes 41943040 | tf_op jit(solution)/shard_map/attention/pallas_call | solution.py:1000
  179.5 110.2 %mlp.1 = (bf16[128,2048]{1,0:T(8,128)(2,1)}, f32[128,2048]{1,0:T(8,128)}, bf16[8,128,2048]{2,1,0:T(8,128)(2,1)}, bf16[2048,2048]{1,0:T(8,128)(2,1)}, f32[256,2048]{1,0:T(8,128)}) custom-call(bf16[128,2048]{1,0:T(8,128)(2,1)} %get-tuple-element.46.x_ref, f32[128,2048]{1,0:T(8,128)} %get-tuple-element.47.hidden_ref.hidden_hbm, ...), custom_call_target="tpu_custom_call" | custom-call | flops 38654705664 | bytes 41943040 | tf_op jit(solution)/shard_map/mlp/pallas_call | solution.py:1180
  289.7 160.5 %backward.1 = (bf16[128,2048]{1,0:T(8,128)(2,1)}, f32[128,2048]{1,0:T(8,128)}, f32[64,128]{1,0:T(8,128)}, f32[64,2048]{1,0:T(8,128)}, f32[64,512]{1,0:T(8,128)},...) custom-call(s32[2]{0:T(128)} %prefix_ref.3, ...), custom_call_target="tpu_custom_call" | custom-call | flops 10000000000 | bytes 41943040 | tf_op jit(solution)/shard_map/backward/pallas_call | solution.py:1422
  450.2 0.0 copy-start
  450.3 10.0 %results.1 = (bf16[128,2048]{1,0:T(8,128)(2,1)}, f32[128,2048]{1,0:T(8,128)}, f32[64,2048]{1,0:T(8,128)}, f32[64,512]{1,0:T(8,128)}, f32[64,512]{1,0:T(8,128)}, ...) custom-call(f32[64,256]{1,0:T(8,128)} %pad_maximum_fusion.gains_ref,, ...), custom_call_target="tpu_custom_call" | custom-call | tf_op jit(solution)/shard_map/results/pallas_call | solution.py:1527
  460.3 0.0 copy-done
  460.3 1.4 slice_reduce_fusion
Async XLA Ops:
  450.2 10.0 %copy-start = (f32[64,128]{1,0:T(8,128)S(1)}, f32[64,128]{1,0:T(8,128)}, u32[]{:S(2)}) copy-start(f32[64,128]{1,0:T(8,128)} %get-tuple-element.72) | copy-start | bytes 98308
